TPU v7x, 32 devices: a whole 2x2x4 slice. The times are simulated.
32 devices in a mesh: scene: 2 (over x), mrow: 8 (over z, y), mcol: 2 (over core).
Axes of the slice: x: 2, y: 2, z: 4, core: 2. Of those that a mesh axis runs over, the one named last changes fastest.
Arguments:
- pan_blocks: bfloat16 [2048, 128, 128], P(('scene', 'mrow', 'mcol')), parts along dimension 0, may hold values from -6 to 6
- ms_blocks: bfloat16 [2048, 32, 256], P(('scene', 'mrow', 'mcol')), parts along dimension 0, may hold values from -6 to 6
- send_list: int32 [3, 2048], P(None, ('scene', 'mrow', 'mcol')), parts along dimension 1, may hold values from 0 to 127, as said below
- tile_list: int32 [3, 4096], P(None, ('scene', 'mrow', 'mcol')), parts along dimension 1, may hold values from 0 to 9, as said below
- row_grid: float32 [48], P(('scene', 'mrow')), parts along dimension 0, may hold values from -32 to 288
- col_grid: float32 [16, 16], P(('scene', 'mrow'), 'mcol'), parts along dimension 0, may hold values from -32 to 1312
- band_mix: float32 [8, 8], replicated, may hold values from -1.5 to 1.5
- band_gain: float32 [8], replicated, may hold values from 0.4 to 1.2
- synth_weight: float32 [8], replicated, may hold values from 0.05 to 0.3
Outputs:
- sharpened: bfloat16 [8, 2048, 1024], P(None, ('scene', 'mrow'), 'mcol'), parts along dimension 1
There are 2 independent parts, one for each index of `scene`. A program takes and returns all parts, laid end to end along the dimension named above; an argument that names none is the same for every part. Nothing has to cross between parts.
Inputs may be any that keep to these rules, and one draw needn't show every extreme that they name: `send_list`: row 0 gives each source block of a device a distinct send slot; slot p goes to map-row owner p // 16 in the device's own map column, so one device sends at most 16 blocks to one tile; in every draw one tile of each map column receives 16 blocks from every device of that column, and every device fills 16 slots of it. Row 1 is a cell row below 2; row 2 a cell column between mcol * 5 and mcol * 5 + 4. `tile_list`: row 0 is 1 exactly in the receive slots that send_list fills and 0 elsewhere; rows 1 and 2 repeat the cell row and column of the block sent there, and are 0 in empty slots.
All inputs are finite; a program needn't handle non-finite values.
Results may differ from a plain program's by a relative error of at most 0.0073.
Values may be sent and summed in bfloat16 or wider, within the bound.
No kernel may reach another device: no remote copies, remote signals or barrier semaphores. Data moves between devices by JAX's collectives and lax.ppermute only.
A program may use at most 128 MiB of HBM per device.

v0:
```python
import jax
import jax.numpy as jnp
from jax import lax
from jax.sharding import PartitionSpec as P

GRID = 64
TR = 128
TC = 512


highest = lax.Precision.HIGHEST


def padded(cells, sides, width):
    for axis, dim in sides:
        count = lax.axis_size(axis)
        ends = count - 1
        head = lax.slice_in_dim(cells, 0, width, axis=dim)
        tail = lax.slice_in_dim(cells, cells.shape[dim] - width, cells.shape[dim], axis=dim)
        cells = jnp.concatenate(
            [
                lax.ppermute(tail, axis, [(i, (i + 1) % count) for i in range(ends)]),
                cells,
                lax.ppermute(head, axis, [((i + 1) % count, i) for i in range(ends)]),
            ],
            axis=dim,
        )
    return cells


def cubic_weight(offset):
    distance = jnp.abs(offset)
    near_part = (1.5 * distance - 2.5) * distance * distance + 1.0
    far_part = ((-0.5 * distance + 2.5) * distance - 4.0) * distance + 2.0
    return jnp.where(
        distance <= 1.0, near_part, jnp.where(distance < 2.0, far_part, jnp.zeros_like(distance))
    )


def along_nodes(node_values, position, offset, spacing):
    segment = jnp.minimum(position // spacing, node_values.shape[-1] - 2)
    left_node = jnp.take(node_values, segment, axis=-1)
    right_node = jnp.take(node_values, segment + 1, axis=-1)
    within = ((position - segment * spacing).astype(jnp.float32) + offset) / spacing
    return left_node + (right_node - left_node) * within


def source_weights(coords, cell_ids, block_size):
    pixels = (
        cell_ids[:, None, None] * block_size
        + jnp.arange(block_size, dtype=jnp.int32)[None, None, :]
    ).astype(jnp.float32)
    return cubic_weight(coords[:, :, None] - pixels).astype(jnp.bfloat16)


def row_weights(coords, cell_ids, is_valid, block_size):
    pixels = (
        cell_ids[None, :, None] * block_size
        + jnp.arange(block_size, dtype=jnp.int32)[None, None, :]
    ).astype(jnp.float32)
    return (cubic_weight(coords[:, None, None] - pixels) * is_valid[None, :, None]).astype(
        jnp.bfloat16
    )


def upsample_table(length, coarse):
    position = (jnp.arange(length, dtype=jnp.int32).astype(jnp.float32) - 1.5) * 0.25 + 2.0
    taps = jnp.arange(coarse + 4, dtype=jnp.int32).astype(jnp.float32)
    return cubic_weight(position[:, None] - taps[None, :]).astype(jnp.bfloat16)


def combine(upsampled, pan_map, band_mix, band_gain, synth_weight):
    mixture = jnp.transpose(upsampled, (1, 0, 2)) + jnp.einsum(
        "bk,rkc->brc", band_mix, upsampled, precision=highest
    )
    synthetic = jnp.einsum("k,rkc->rc", synth_weight, upsampled, precision=highest)
    return (mixture + band_gain[:, None, None] * (pan_map - synthetic)[None, :, :]).astype(
        jnp.bfloat16
    )


def column_pass(members):
    pan_data, ms_data, x_pan, x_ms, cell_ids = members
    block_size = pan_data.shape[1]
    coarse_size = ms_data.shape[1]
    band_count = ms_data.shape[2] // coarse_size
    col_weight = source_weights(x_pan, cell_ids, block_size)
    pan_cols = jnp.einsum(
        "sij,scj->sic", pan_data, col_weight, preferred_element_type=jnp.float32
    ).astype(jnp.bfloat16)
    spread = ms_data.reshape(ms_data.shape[0], coarse_size, band_count, coarse_size)
    ms_col_weight = source_weights(x_ms, cell_ids, coarse_size)
    ms_cols = jnp.einsum(
        "sibj,scj->sibc", spread, ms_col_weight, preferred_element_type=jnp.float32
    ).astype(jnp.bfloat16)
    return (pan_cols, ms_cols)


def grouped_pass(pan_data, ms_data, x_pan, x_ms, cell_ids):
    partition_total = pan_data.shape[0]
    groups = partition_total // 8
    stacked = (
        pan_data.reshape((groups, 8) + pan_data.shape[1:]),
        ms_data.reshape((groups, 8) + ms_data.shape[1:]),
        x_pan.reshape(groups, 8, x_pan.shape[1]),
        x_ms.reshape(groups, 8, x_ms.shape[1]),
        cell_ids.reshape(groups, 8),
    )
    pan_cols, ms_cols = lax.map(column_pass, stacked)
    return (
        pan_cols.reshape((partition_total,) + pan_cols.shape[2:]),
        ms_cols.reshape((partition_total,) + ms_cols.shape[2:]),
    )


def local(
    pan_blocks,
    ms_blocks,
    send_list,
    tile_list,
    row_grid,
    col_grid,
    band_mix,
    band_gain,
    synth_weight,
):
    row_owners = lax.axis_size("mrow")
    horizontal_location = lax.axis_index("mcol")
    own_blocks = pan_blocks.shape[0]
    partition_total = tile_list.shape[1]
    capacity = partition_total // row_owners
    block_size = pan_blocks.shape[1]
    coarse_size = ms_blocks.shape[1]
    band_count = band_gain.shape[0]
    coarse_rows = TR // 4
    coarse_cols = TC // 4
    band_nodes = lax.all_gather(col_grid, "mcol", axis=1, tiled=True)
    map_rows = jnp.arange(TR, dtype=jnp.int32)
    map_cols = horizontal_location * TC + jnp.arange(TC, dtype=jnp.int32)
    coarse_pos = horizontal_location * TC + 4 * jnp.arange(coarse_cols, dtype=jnp.int32) + 1
    y_pan = along_nodes(row_grid, map_rows, 0.0, GRID)
    y_ms = (
        along_nodes(row_grid, 4 * jnp.arange(coarse_rows, dtype=jnp.int32) + 1, 0.5, GRID) - 1.5
    ) * 0.25
    partition_number = send_list[0]
    owner_ids = (
        jnp.zeros((partition_total,), jnp.int32)
        .at[partition_number]
        .set(jnp.arange(own_blocks, dtype=jnp.int32))
    )
    filled = jnp.zeros((partition_total,), jnp.int32).at[partition_number].set(1) > 0
    zero_bf = jnp.zeros((), jnp.bfloat16)
    pan_send = jnp.where(filled[:, None, None], jnp.take(pan_blocks, owner_ids, axis=0), zero_bf)
    ms_send = jnp.where(filled[:, None, None], jnp.take(ms_blocks, owner_ids, axis=0), zero_bf)
    pan_recv, ms_recv = (
        lax.all_to_all(
            pan_send.reshape(row_owners, capacity, block_size, block_size),
            "mrow",
            split_axis=0,
            concat_axis=0,
            tiled=True,
        ),
        lax.all_to_all(
            ms_send.reshape(row_owners, capacity, coarse_size, ms_blocks.shape[2]),
            "mrow",
            split_axis=0,
            concat_axis=0,
            tiled=True,
        ),
    )
    x_pan = along_nodes(band_nodes[0], map_cols, 0.0, GRID)
    x_ms = (along_nodes(band_nodes[0], coarse_pos, 0.5, GRID) - 1.5) * 0.25
    pan_cols, ms_cols = grouped_pass(
        pan_recv.reshape(partition_total, block_size, block_size),
        ms_recv.reshape(partition_total, coarse_size, ms_blocks.shape[2]),
        jnp.broadcast_to(x_pan[None, :], (partition_total, TC)),
        jnp.broadcast_to(x_ms[None, :], (partition_total, coarse_cols)),
        tile_list[2],
    )
    is_valid = tile_list[0].astype(jnp.float32)
    cell_rows = tile_list[1]
    row_weight = row_weights(y_pan, cell_rows, is_valid, block_size)
    pan_map = jnp.dot(
        row_weight.reshape(TR, partition_total * block_size),
        pan_cols.reshape(partition_total * block_size, TC),
        preferred_element_type=jnp.float32,
    )
    ms_row_weight = row_weights(y_ms, cell_rows, is_valid, coarse_size)
    ms_map = jnp.dot(
        ms_row_weight.reshape(coarse_rows, partition_total * coarse_size),
        ms_cols.reshape(partition_total * coarse_size, band_count * coarse_cols),
        preferred_element_type=jnp.float32,
    ).astype(jnp.bfloat16)
    ms_map = ms_map.reshape(coarse_rows, band_count, coarse_cols)
    window = padded(ms_map, (("mrow", 0), ("mcol", 2)), 2)
    up_rows = upsample_table(TR, coarse_rows)
    up_cols = upsample_table(TC, coarse_cols)
    across = jnp.einsum("mbn,cn->mbc", window, up_cols, preferred_element_type=jnp.float32).astype(
        jnp.bfloat16
    )
    upsampled = jnp.dot(
        up_rows,
        across.reshape(coarse_rows + 4, band_count * TC),
        preferred_element_type=jnp.float32,
    ).reshape(TR, band_count, TC)
    return combine(upsampled, pan_map, band_mix, band_gain, synth_weight)


def solution(mesh):
    return jax.shard_map(
        local,
        mesh=mesh,
        in_specs=(
            P(("scene", "mrow", "mcol"), None, None),
            P(("scene", "mrow", "mcol"), None, None),
            P(None, ("scene", "mrow", "mcol")),
            P(None, ("scene", "mrow", "mcol")),
            P(("scene", "mrow")),
            P(("scene", "mrow"), "mcol"),
            P(),
            P(),
            P(),
        ),
        out_specs=P(None, ("scene", "mrow"), "mcol"),
        check_vma=False,
    )
```

profile of v0, /device:TPU:11, one launch (start us, length us, event | category | flops | bytes accessed | tf_op | source)
XLA Modules:
  0.0 288.9 jit_solution(7386547417058513332)
XLA Ops:
  2.6 3.2 %gather_fusion.1 = bf16[128,32,256]{2,1,0:T(8,128)(2,1)} fusion(bf16[64,32,256]{2,1,0:T(8,128)(2,1)} %param.20, s32[1024]{0:T(1024)S(1)} %pad_clamp_fusion), kind=kCustom, calls=%fused_computation.1 | custom fusion | bytes 4194816 | tf_op jit(solution)/shard_map/jit(_take)/gather | solution.py:154
  5.9 2.8 select_select_fusion.1
  8.7 5.7 %all-to-all-start.1 = ((bf16[8,16,32,256]{3,2,1,0:T(8,128)(2,1)}), bf16[8,16,32,256]{3,2,1,0:T(8,128)(2,1)}, u32[]{:S(2)}, u32[]{:S(2)}) async-start(bf16[8,16,32,256]{3,2,1,0:T(8,128)(2,1)} %select_select_fusion.1), calls=%async_computation.1 | async-start | bytes 4194304 | tf_op jit(solution)/shard_map/all_to_all | solution.py:163
  14.4 3.0 %gather_fusion = bf16[128,128,128]{2,1,0:T(8,128)(2,1)} fusion(bf16[64,128,128]{2,1,0:T(8,128)(2,1)S(1)} %copy-done, s32[1024]{0:T(1024)S(1)} %pad_clamp_fusion), kind=kCustom, calls=%fused_computation | custom fusion | bytes 8389120 | tf_op jit(solution)/shard_map/jit(_take)/gather | solution.py:153
  17.4 3.9 %select_select_fusion = bf16[8,16,128,128]{3,2,1,0:T(8,128)(2,1)} fusion(bf16[8,16,128,128]{3,2,1,0:T(8,128)(2,1)} %bitcast.200, pred[8,16]{1,0:T(8,128)(4,1)S(1)} %broadcast_in_dim.148, pred[8,16]{1,0:T(8,128)(4,1)S(1)} %broadcast_in_dim.146), kind=kLoop, calls=%fused_computation.95 | loop fusion | flops 4194304 | bytes 8388864 | tf_op jit(solution)/shard_map/jit(_where)/select_n | solution.py:153
  21.3 39.6 %all-to-all-done.1 = bf16[8,16,32,256]{3,2,1,0:T(8,128)(2,1)} async-done(((bf16[8,16,32,256]{3,2,1,0:T(8,128)(2,1)}), bf16[8,16,32,256]{3,2,1,0:T(8,128)(2,1)}, u32[]{:S(2)}, u32[]{:S(2)}) %all-to-all-start.1) | async-done | bytes 2097184 | tf_op jit(solution)/shard_map/all_to_all | solution.py:163
  60.9 5.6 %all-to-all-start = ((bf16[8,16,128,128]{3,2,1,0:T(8,128)(2,1)}), bf16[8,16,128,128]{3,2,1,0:T(8,128)(2,1)}, u32[]{:S(2)}, u32[]{:S(2)}) async-start(bf16[8,16,128,128]{3,2,1,0:T(8,128)(2,1)} %select_select_fusion), calls=%async_computation | async-start | bytes 8388608 | tf_op jit(solution)/shard_map/all_to_all | solution.py:156
  68.5 4.0 %all-reduce = f32[16]{0:T(128)S(1)} all-reduce(f32[16]{0:T(128)S(1)} %bitcast_dynamic-update-slice_fusion), channel_id=1, replica_groups=mesh['scene'=2,'mrow'=8,'mcol'=2] {'mcol'}, use_global_device_ids=true, to_apply=%add | all-reduce | flops 16 | bytes 128 | tf_op jit(solution)/shard_map/squeeze | solution.py:171
  73.1 1.8 add_multiply_fusion.1
  75.7 10.1 %add_multiply_fusion = f32[128]{0:T(128)S(1)} fusion(f32[]{:T(128)} %bitcast.39, f32[]{:T(128)} %bitcast.38, f32[]{:T(128)} %bitcast.37, f32[]{:T(128)} %bitcast.36, f32[]{:T(128)} %bitcast.35, f32[]{:T(128)} %bitcast.34, f32[]{:T(128)} %bitcast.33, f32[]{:T(128)} %bitcast.32, f32[]{:T(128)} %bitcast.31, f32[]{:T(128)} %bitcast.30, f32[]{:T(128)} %bitcast.29, ...), kind=kLoop, calls=%fused_computation.281 | loop fusion | flops 13312 | bytes 580 | tf_op jit(solution)/shard_map/mul | solution.py:172
  85.8 10.1 %fusion.154 = f32[512]{0:T(512)S(1)} fusion(f32[]{:T(128)} %bitcast.39, f32[]{:T(128)} %bitcast.38, f32[]{:T(128)} %bitcast.37, f32[]{:T(128)} %bitcast.36, f32[]{:T(128)} %bitcast.35, f32[]{:T(128)} %bitcast.34, f32[]{:T(128)} %bitcast.33, f32[]{:T(128)} %bitcast.32, f32[]{:T(128)} %bitcast.31, f32[]{:T(128)} %bitcast.30, f32[]{:T(128)} %bitcast.29, ...), kind=kLoop, calls=%fused_computation.201 | loop fusion | flops 50688 | bytes 2116 | tf_op jit(solution)/shard_map/add | solution.py:45
  96.3 61.7 %all-to-all-done = bf16[8,16,128,128]{3,2,1,0:T(8,128)(2,1)} async-done(((bf16[8,16,128,128]{3,2,1,0:T(8,128)(2,1)}), bf16[8,16,128,128]{3,2,1,0:T(8,128)(2,1)}, u32[]{:S(2)}, u32[]{:S(2)}) %all-to-all-start) | async-done | bytes 4194336 | tf_op jit(solution)/shard_map/all_to_all | solution.py:156
  158.0 95.9 %while.15 = (s32[]{:T(128)}, bf16[16,8,128,512]{3,2,1,0:T(8,128)(2,1)}, bf16[16,8,32,8,128]{4,3,2,1,0:T(8,128)(2,1)}, bf16[16,8,128,128]{3,2,1,0:T(8,128)(2,1)},...) while((s32[]{:T(128)}, ...), condition=%wide.region_3.7_spmd, body=%wide.region_2.6_spmd.sunk | while | flops 161810960 | bytes 2563853 | solution.py:109
  158.1 0.9 constant_dynamic-slice_fusion.3
  159.3 1.2 fusion.224
  160.6 3.5 %fusion.223 = bf16[16,8,128,512]{3,2,1,0:T(8,128)(2,1)} fusion(bf16[16,8,128,512]{3,2,1,0:T(8,128)(2,1)} %get-tuple-element.249, s32[]{:T(128)} %get-tuple-element.248, f32[8,128]{1,0:T(8,128)S(1)} %add_convert_fusion.5, f32[8,512]{1,0:T(8,128)S(1)} %dynamic-slice_bitcast_fusion.4, bf16[16,8,128,128]{3,2,1,0:T(8,128)(2,1)} %get-tuple-element.260), kind=kOutput, calls=%fused_computation.13.clone.1 | convolution fusion | flops 144179200 | bytes 1332224 | tf_op jit(solution)/shard_map/while/body/eval_jaxpr/sij,scj->sic/dot_general | solution.py:88
  164.1 0.9 constant_dynamic-slice_fusion.3
  165.3 1.2 fusion.224
  166.6 3.5 %fusion.223 = bf16[16,8,128,512]{3,2,1,0:T(8,128)(2,1)} fusion(bf16[16,8,128,512]{3,2,1,0:T(8,128)(2,1)} %get-tuple-element.249, s32[]{:T(128)} %get-tuple-element.248, f32[8,128]{1,0:T(8,128)S(1)} %add_convert_fusion.5, f32[8,512]{1,0:T(8,128)S(1)} %dynamic-slice_bitcast_fusion.4, bf16[16,8,128,128]{3,2,1,0:T(8,128)(2,1)} %get-tuple-element.260), kind=kOutput, calls=%fused_computation.13.clone.1 | convolution fusion | flops 144179200 | bytes 1332224 | tf_op jit(solution)/shard_map/while/body/eval_jaxpr/sij,scj->sic/dot_general | solution.py:88
  170.1 0.9 constant_dynamic-slice_fusion.3
  171.3 1.2 fusion.224
  172.6 3.5 %fusion.223 = bf16[16,8,128,512]{3,2,1,0:T(8,128)(2,1)} fusion(bf16[16,8,128,512]{3,2,1,0:T(8,128)(2,1)} %get-tuple-element.249, s32[]{:T(128)} %get-tuple-element.248, f32[8,128]{1,0:T(8,128)S(1)} %add_convert_fusion.5, f32[8,512]{1,0:T(8,128)S(1)} %dynamic-slice_bitcast_fusion.4, bf16[16,8,128,128]{3,2,1,0:T(8,128)(2,1)} %get-tuple-element.260), kind=kOutput, calls=%fused_computation.13.clone.1 | convolution fusion | flops 144179200 | bytes 1332224 | tf_op jit(solution)/shard_map/while/body/eval_jaxpr/sij,scj->sic/dot_general | solution.py:88
  176.2 0.9 constant_dynamic-slice_fusion.3
  177.3 1.2 fusion.224
  178.6 3.5 %fusion.223 = bf16[16,8,128,512]{3,2,1,0:T(8,128)(2,1)} fusion(bf16[16,8,128,512]{3,2,1,0:T(8,128)(2,1)} %get-tuple-element.249, s32[]{:T(128)} %get-tuple-element.248, f32[8,128]{1,0:T(8,128)S(1)} %add_convert_fusion.5, f32[8,512]{1,0:T(8,128)S(1)} %dynamic-slice_bitcast_fusion.4, bf16[16,8,128,128]{3,2,1,0:T(8,128)(2,1)} %get-tuple-element.260), kind=kOutput, calls=%fused_computation.13.clone.1 | convolution fusion | flops 144179200 | bytes 1332224 | tf_op jit(solution)/shard_map/while/body/eval_jaxpr/sij,scj->sic/dot_general | solution.py:88
  182.1 0.9 constant_dynamic-slice_fusion.3
  183.3 1.2 fusion.224
  184.5 3.5 %fusion.223 = bf16[16,8,128,512]{3,2,1,0:T(8,128)(2,1)} fusion(bf16[16,8,128,512]{3,2,1,0:T(8,128)(2,1)} %get-tuple-element.249, s32[]{:T(128)} %get-tuple-element.248, f32[8,128]{1,0:T(8,128)S(1)} %add_convert_fusion.5, f32[8,512]{1,0:T(8,128)S(1)} %dynamic-slice_bitcast_fusion.4, bf16[16,8,128,128]{3,2,1,0:T(8,128)(2,1)} %get-tuple-element.260), kind=kOutput, calls=%fused_computation.13.clone.1 | convolution fusion | flops 144179200 | bytes 1332224 | tf_op jit(solution)/shard_map/while/body/eval_jaxpr/sij,scj->sic/dot_general | solution.py:88
  188.1 0.9 constant_dynamic-slice_fusion.3
  189.2 1.2 fusion.224
  190.5 3.5 %fusion.223 = bf16[16,8,128,512]{3,2,1,0:T(8,128)(2,1)} fusion(bf16[16,8,128,512]{3,2,1,0:T(8,128)(2,1)} %get-tuple-element.249, s32[]{:T(128)} %get-tuple-element.248, f32[8,128]{1,0:T(8,128)S(1)} %add_convert_fusion.5, f32[8,512]{1,0:T(8,128)S(1)} %dynamic-slice_bitcast_fusion.4, bf16[16,8,128,128]{3,2,1,0:T(8,128)(2,1)} %get-tuple-element.260), kind=kOutput, calls=%fused_computation.13.clone.1 | convolution fusion | flops 144179200 | bytes 1332224 | tf_op jit(solution)/shard_map/while/body/eval_jaxpr/sij,scj->sic/dot_general | solution.py:88
  194.1 0.9 constant_dynamic-slice_fusion.3
  195.3 1.2 fusion.224
  196.5 3.5 %fusion.223 = bf16[16,8,128,512]{3,2,1,0:T(8,128)(2,1)} fusion(bf16[16,8,128,512]{3,2,1,0:T(8,128)(2,1)} %get-tuple-element.249, s32[]{:T(128)} %get-tuple-element.248, f32[8,128]{1,0:T(8,128)S(1)} %add_convert_fusion.5, f32[8,512]{1,0:T(8,128)S(1)} %dynamic-slice_bitcast_fusion.4, bf16[16,8,128,128]{3,2,1,0:T(8,128)(2,1)} %get-tuple-element.260), kind=kOutput, calls=%fused_computation.13.clone.1 | convolution fusion | flops 144179200 | bytes 1332224 | tf_op jit(solution)/shard_map/while/body/eval_jaxpr/sij,scj->sic/dot_general | solution.py:88
  200.1 0.9 constant_dynamic-slice_fusion.3
  201.2 1.2 fusion.224
  202.5 3.5 %fusion.223 = bf16[16,8,128,512]{3,2,1,0:T(8,128)(2,1)} fusion(bf16[16,8,128,512]{3,2,1,0:T(8,128)(2,1)} %get-tuple-element.249, s32[]{:T(128)} %get-tuple-element.248, f32[8,128]{1,0:T(8,128)S(1)} %add_convert_fusion.5, f32[8,512]{1,0:T(8,128)S(1)} %dynamic-slice_bitcast_fusion.4, bf16[16,8,128,128]{3,2,1,0:T(8,128)(2,1)} %get-tuple-element.260), kind=kOutput, calls=%fused_computation.13.clone.1 | convolution fusion | flops 144179200 | bytes 1332224 | tf_op jit(solution)/shard_map/while/body/eval_jaxpr/sij,scj->sic/dot_general | solution.py:88
  207.2 1.2 fusion.224
  208.5 3.5 %fusion.223 = bf16[16,8,128,512]{3,2,1,0:T(8,128)(2,1)} fusion(bf16[16,8,128,512]{3,2,1,0:T(8,128)(2,1)} %get-tuple-element.249, s32[]{:T(128)} %get-tuple-element.248, f32[8,128]{1,0:T(8,128)S(1)} %add_convert_fusion.5, f32[8,512]{1,0:T(8,128)S(1)} %dynamic-slice_bitcast_fusion.4, bf16[16,8,128,128]{3,2,1,0:T(8,128)(2,1)} %get-tuple-element.260), kind=kOutput, calls=%fused_computation.13.clone.1 | convolution fusion | flops 144179200 | bytes 1332224 | tf_op jit(solution)/shard_map/while/body/eval_jaxpr/sij,scj->sic/dot_general | solution.py:88
  213.2 1.2 fusion.224
  214.4 3.5 %fusion.223 = bf16[16,8,128,512]{3,2,1,0:T(8,128)(2,1)} fusion(bf16[16,8,128,512]{3,2,1,0:T(8,128)(2,1)} %get-tuple-element.249, s32[]{:T(128)} %get-tuple-element.248, f32[8,128]{1,0:T(8,128)S(1)} %add_convert_fusion.5, f32[8,512]{1,0:T(8,128)S(1)} %dynamic-slice_bitcast_fusion.4, bf16[16,8,128,128]{3,2,1,0:T(8,128)(2,1)} %get-tuple-element.260), kind=kOutput, calls=%fused_computation.13.clone.1 | convolution fusion | flops 144179200 | bytes 1332224 | tf_op jit(solution)/shard_map/while/body/eval_jaxpr/sij,scj->sic/dot_general | solution.py:88
  218.0 0.9 constant_dynamic-slice_fusion.3
  219.2 1.2 fusion.224
  220.5 3.5 %fusion.223 = bf16[16,8,128,512]{3,2,1,0:T(8,128)(2,1)} fusion(bf16[16,8,128,512]{3,2,1,0:T(8,128)(2,1)} %get-tuple-element.249, s32[]{:T(128)} %get-tuple-element.248, f32[8,128]{1,0:T(8,128)S(1)} %add_convert_fusion.5, f32[8,512]{1,0:T(8,128)S(1)} %dynamic-slice_bitcast_fusion.4, bf16[16,8,128,128]{3,2,1,0:T(8,128)(2,1)} %get-tuple-element.260), kind=kOutput, calls=%fused_computation.13.clone.1 | convolution fusion | flops 144179200 | bytes 1332224 | tf_op jit(solution)/shard_map/while/body/eval_jaxpr/sij,scj->sic/dot_general | solution.py:88
  225.2 1.2 fusion.224
  226.5 3.5 %fusion.223 = bf16[16,8,128,512]{3,2,1,0:T(8,128)(2,1)} fusion(bf16[16,8,128,512]{3,2,1,0:T(8,128)(2,1)} %get-tuple-element.249, s32[]{:T(128)} %get-tuple-element.248, f32[8,128]{1,0:T(8,128)S(1)} %add_convert_fusion.5, f32[8,512]{1,0:T(8,128)S(1)} %dynamic-slice_bitcast_fusion.4, bf16[16,8,128,128]{3,2,1,0:T(8,128)(2,1)} %get-tuple-element.260), kind=kOutput, calls=%fused_computation.13.clone.1 | convolution fusion | flops 144179200 | bytes 1332224 | tf_op jit(solution)/shard_map/while/body/eval_jaxpr/sij,scj->sic/dot_general | solution.py:88
  231.2 1.2 fusion.224
  232.4 3.5 %fusion.223 = bf16[16,8,128,512]{3,2,1,0:T(8,128)(2,1)} fusion(bf16[16,8,128,512]{3,2,1,0:T(8,128)(2,1)} %get-tuple-element.249, s32[]{:T(128)} %get-tuple-element.248, f32[8,128]{1,0:T(8,128)S(1)} %add_convert_fusion.5, f32[8,512]{1,0:T(8,128)S(1)} %dynamic-slice_bitcast_fusion.4, bf16[16,8,128,128]{3,2,1,0:T(8,128)(2,1)} %get-tuple-element.260), kind=kOutput, calls=%fused_computation.13.clone.1 | convolution fusion | flops 144179200 | bytes 1332224 | tf_op jit(solution)/shard_map/while/body/eval_jaxpr/sij,scj->sic/dot_general | solution.py:88
  237.2 1.2 fusion.224
  238.5 3.5 %fusion.223 = bf16[16,8,128,512]{3,2,1,0:T(8,128)(2,1)} fusion(bf16[16,8,128,512]{3,2,1,0:T(8,128)(2,1)} %get-tuple-element.249, s32[]{:T(128)} %get-tuple-element.248, f32[8,128]{1,0:T(8,128)S(1)} %add_convert_fusion.5, f32[8,512]{1,0:T(8,128)S(1)} %dynamic-slice_bitcast_fusion.4, bf16[16,8,128,128]{3,2,1,0:T(8,128)(2,1)} %get-tuple-element.260), kind=kOutput, calls=%fused_computation.13.clone.1 | convolution fusion | flops 144179200 | bytes 1332224 | tf_op jit(solution)/shard_map/while/body/eval_jaxpr/sij,scj->sic/dot_general | solution.py:88
  243.2 1.2 fusion.224
  244.4 3.5 %fusion.223 = bf16[16,8,128,512]{3,2,1,0:T(8,128)(2,1)} fusion(bf16[16,8,128,512]{3,2,1,0:T(8,128)(2,1)} %get-tuple-element.249, s32[]{:T(128)} %get-tuple-element.248, f32[8,128]{1,0:T(8,128)S(1)} %add_convert_fusion.5, f32[8,512]{1,0:T(8,128)S(1)} %dynamic-slice_bitcast_fusion.4, bf16[16,8,128,128]{3,2,1,0:T(8,128)(2,1)} %get-tuple-element.260), kind=kOutput, calls=%fused_computation.13.clone.1 | convolution fusion | flops 144179200 | bytes 1332224 | tf_op jit(solution)/shard_map/while/body/eval_jaxpr/sij,scj->sic/dot_general | solution.py:88
  249.2 1.2 fusion.224
  250.5 3.5 %fusion.223 = bf16[16,8,128,512]{3,2,1,0:T(8,128)(2,1)} fusion(bf16[16,8,128,512]{3,2,1,0:T(8,128)(2,1)} %get-tuple-element.249, s32[]{:T(128)} %get-tuple-element.248, f32[8,128]{1,0:T(8,128)S(1)} %add_convert_fusion.5, f32[8,512]{1,0:T(8,128)S(1)} %dynamic-slice_bitcast_fusion.4, bf16[16,8,128,128]{3,2,1,0:T(8,128)(2,1)} %get-tuple-element.260), kind=kOutput, calls=%fused_computation.13.clone.1 | convolution fusion | flops 144179200 | bytes 1332224 | tf_op jit(solution)/shard_map/while/body/eval_jaxpr/sij,scj->sic/dot_general | solution.py:88
  253.9 5.2 %fusion.87 = bf16[32,1024]{1,0:T(8,128)(2,1)S(1)} fusion(bf16[512,8,8,128]{3,2,1,0:T(8,128)(2,1)} %bitcast.208, f32[4096]{0:T(1024)S(1)} %mul.388, f32[4096]{0:T(1024)S(1)} %add_convert_fusion.2, f32[32]{0:T(128)S(1)} %add_multiply_fusion.1), kind=kOutput, calls=%fused_computation.106 | convolution fusion | flops 270958592 | bytes 8487040 | tf_op jit(solution)/shard_map/dot_general | solution.py:189
  259.1 2.7 collective-permute-start
  261.9 3.9 %collective-permute-start.1 = (bf16[2,8,128]{2,1,0:T(8,128)(2,1)S(1)}, bf16[2,8,128]{2,1,0:T(8,128)(2,1)S(1)}, u32[]{:S(2)}, u32[]{:S(2)}) collective-permute-start(bf16[2,8,128]{2,1,0:T(8,128)(2,1)S(1)} %bitcast.206), channel_id=1, source_target_pairs={{2,0},{4,2},{6,4},{8,6},{10,8},{12,10},{14,12},{3,1},{5,3},{7,5},{... | collective-permute-start | bytes 12296 | tf_op jit(solution)/shard_map/ppermute | solution.py:24
  266.6 1.3 collective-permute-start.2
  267.9 4.3 %collective-permute-start.3 = (bf16[36,8,2]{2,1,0:T(8,128)(2,1)S(1)}, bf16[36,8,2]{2,1,0:T(8,128)(2,1)S(1)}, u32[]{:S(2)}, u32[]{:S(2)}) collective-permute-start(bf16[36,8,2]{2,1,0:T(8,128)(2,1)S(1)} %get-tuple-element.160), channel_id=1, source_target_pairs={{1,0},{3,2},{5,4},{7,6},{9,8},{11,10},{13,12},{15,14},{17,16},{19,... | collective-permute-start | bytes 3464 | tf_op jit(solution)/shard_map/ppermute | solution.py:24
  272.2 1.8 fusion.168
  275.1 3.0 %fusion.80 = f32[1,128,512]{2,0,1:T(1,128)S(1)} fusion(f32[128,8,512]{2,0,1:T(8,128)S(1)} %fusion.96, f32[8]{0:T(128)S(1)} %copy-done.4), kind=kOutput, calls=%fused_computation.100 | convolution fusion | flops 6291456 | bytes 2359328 | tf_op jit(solution)/shard_map/k,rkc->rc/dot_general | solution.py:76
  278.2 3.3 %fusion.82 = f32[128,512,8]{1,2,0:T(8,128)S(1)} fusion(f32[128,8,512]{2,0,1:T(8,128)S(1)} %fusion.96, f32[8,8]{1,0:T(8,128)S(1)} %copy-done.2), kind=kOutput, calls=%fused_computation.102 | convolution fusion | flops 50331648 | bytes 4194560 | tf_op jit(solution)/shard_map/bk,rkc->brc/dot_general | solution.py:73
  281.5 5.2 %fusion.84 = f32[128,512]{1,0:T(8,128)S(1)} fusion(bf16[16384,512]{1,0:T(8,128)(2,1)S(1)} %bitcast.207, f32[16384]{0:T(1024)S(1)} %broadcast_bitcast_fusion, f32[16384]{0:T(1024)S(1)} %fusion.132, f32[128]{0:T(128)S(1)} %fusion.168, f32[1,128,512]{2,0,1:T(1,128)S(1)} %fusion.80), kind=kOutput, calls=%fused_computation.105 | convolution fusion | flops 2187395072 | bytes 17433088 | tf_op jit(solution)/shard_map/dot_general | solution.py:183
  286.7 2.3 fusion.79
  (172 shorter events, 20.3 us)
Async XLA Ops:
  0.0 14.4 %copy-start = (bf16[64,128,128]{2,1,0:T(8,128)(2,1)S(1)}, bf16[64,128,128]{2,1,0:T(8,128)(2,1)}, u32[]{:S(2)}) copy-start(bf16[64,128,128]{2,1,0:T(8,128)(2,1)} %param.19) | copy-start | bytes 6291460
  8.7 52.2 %all-to-all-start.1 = ((bf16[8,16,32,256]{3,2,1,0:T(8,128)(2,1)}), bf16[8,16,32,256]{3,2,1,0:T(8,128)(2,1)}, u32[]{:S(2)}, u32[]{:S(2)}) async-start(bf16[8,16,32,256]{3,2,1,0:T(8,128)(2,1)} %select_select_fusion.1), calls=%async_computation.1 | async-start | bytes 4194304 | tf_op jit(solution)/shard_map/all_to_all | solution.py:163
  21.3 45.3 %copy-start.3 = (s32[3,128]{1,0:T(4,128)S(1)}, s32[3,128]{1,0:T(4,128)}, u32[]{:S(2)}) copy-start(s32[3,128]{1,0:T(4,128)} %param.22) | copy-start | bytes 4612
  21.3 45.8 %copy-start.8 = (u32[32]{0:T(128)S(1)}, u32[32]{0:T(128)}, u32[]{:S(2)}) copy-start(u32[32]{0:T(128)} %constant.385) | copy-start | bytes 388
  21.3 47.1 %copy-start.6 = (f32[1,8]{1,0:T(1,128)S(1)}, f32[1,8]{1,0:T(1,128)}, u32[]{:S(2)}) copy-start(f32[1,8]{1,0:T(1,128)} %param.24) | copy-start | bytes 100
  21.3 51.2 %copy-start.1 = (f32[3]{0:T(128)S(1)}, f32[3]{0:T(128)}, u32[]{:S(2)}) copy-start(f32[3]{0:T(128)} %param.23) | copy-start | bytes 40
  60.9 97.1 %all-to-all-start = ((bf16[8,16,128,128]{3,2,1,0:T(8,128)(2,1)}), bf16[8,16,128,128]{3,2,1,0:T(8,128)(2,1)}, u32[]{:S(2)}, u32[]{:S(2)}) async-start(bf16[8,16,128,128]{3,2,1,0:T(8,128)(2,1)} %select_select_fusion), calls=%async_computation | async-start | bytes 8388608 | tf_op jit(solution)/shard_map/all_to_all | solution.py:156
  253.9 27.5 %copy-start.7 = (bf16[16,8,128,512]{3,2,1,0:T(8,128)(2,1)S(1)}, bf16[16,8,128,512]{3,2,1,0:T(8,128)(2,1)}, u32[]{:S(2)}) copy-start(bf16[16,8,128,512]{3,2,1,0:T(8,128)(2,1)} %get-tuple-element.140) | copy-start | bytes 50331652
  259.1 6.6 %collective-permute-start = (bf16[2,8,128]{2,1,0:T(8,128)(2,1)S(1)}, bf16[2,8,128]{2,1,0:T(8,128)(2,1)S(1)}, u32[]{:S(2)}, u32[]{:S(2)}) collective-permute-start(bf16[2,8,128]{2,1,0:T(8,128)(2,1)S(1)} %bitcast.205), channel_id=1, source_target_pairs={{0,2},{2,4},{4,6},{6,8},{8,10},{10,12},{12,14},{1,3},{3,5},{5,7},{... | collective-permute-start | bytes 12296 | tf_op jit(solution)/shard_map/ppermute | solution.py:22
  261.9 4.6 %collective-permute-start.1 = (bf16[2,8,128]{2,1,0:T(8,128)(2,1)S(1)}, bf16[2,8,128]{2,1,0:T(8,128)(2,1)S(1)}, u32[]{:S(2)}, u32[]{:S(2)}) collective-permute-start(bf16[2,8,128]{2,1,0:T(8,128)(2,1)S(1)} %bitcast.206), channel_id=1, source_target_pairs={{2,0},{4,2},{6,4},{8,6},{10,8},{12,10},{14,12},{3,1},{5,3},{7,5},{... | collective-permute-start | bytes 12296 | tf_op jit(solution)/shard_map/ppermute | solution.py:24
  266.6 7.4 %collective-permute-start.2 = (bf16[36,8,2]{2,1,0:T(8,128)(2,1)S(1)}, bf16[36,8,2]{2,1,0:T(8,128)(2,1)S(1)}, u32[]{:S(2)}, u32[]{:S(2)}) collective-permute-start(bf16[36,8,2]{2,1,0:T(8,128)(2,1)S(1)} %get-tuple-element.159), channel_id=1, source_target_pairs={{0,1},{2,3},{4,5},{6,7},{8,9},{10,11},{12,13},{14,15},{16,17},{18,... | collective-permute-start | bytes 3464 | tf_op jit(solution)/shard_map/ppermute | solution.py:22
  267.9 6.1 %collective-permute-start.3 = (bf16[36,8,2]{2,1,0:T(8,128)(2,1)S(1)}, bf16[36,8,2]{2,1,0:T(8,128)(2,1)S(1)}, u32[]{:S(2)}, u32[]{:S(2)}) collective-permute-start(bf16[36,8,2]{2,1,0:T(8,128)(2,1)S(1)} %get-tuple-element.160), channel_id=1, source_target_pairs={{1,0},{3,2},{5,4},{7,6},{9,8},{11,10},{13,12},{15,14},{17,16},{19,... | collective-permute-start | bytes 3464 | tf_op jit(solution)/shard_map/ppermute | solution.py:24
  274.0 1.1 copy-start.4
  274.5 3.6 %copy-start.2 = (f32[8,8]{1,0:T(8,128)S(1)}, f32[8,8]{1,0:T(8,128)}, u32[]{:S(2)}) copy-start(f32[8,8]{1,0:T(8,128)} %param.25) | copy-start | bytes 772
  281.5 5.2 %copy-start.5 = (f32[8]{0:T(128)S(1)}, f32[8]{0:T(128)}, u32[]{:S(2)}) copy-start(f32[8]{0:T(128)} %param.26) | copy-start | bytes 100
where the time goes:
time: 294 us; the launch traced here: 289 us
  waiting for transfers between devices  102 us (35%)
  matrix products  92.2 us (31%)
  other arithmetic  36.2 us (12%)
  local copies, waits for them, and re-layouts  29.7 us (10%)
  starting transfers between devices  23.5 us (8%)
  blocking collectives  3.98 us (1%)
    all_to_all x1, waiting for transfers between devices, local(): lax.all_to_all(pan_send.reshape(row_owners, capacity, block_size, block_s...  61.7 us
    dot_general x16, matrix products, column_pass(): jnp.einsum('sij,scj->sic', pan_data, col_weight, preferred_element_type=j...  55.7 us
    all_to_all x1, waiting for transfers between devices, local(): lax.all_to_all(ms_send.reshape(row_owners, capacity, coarse_size, ms_bloc...  39.6 us
    dot_general x16, matrix products, column_pass(): jnp.einsum('sibj,scj->sibc', spread, ms_col_weight, preferred_element_typ...  18.8 us
    dynamic_slice x16, local copies, waits for them, and re-layouts, grouped_pass(): pan_cols, ms_cols = lax.map(column_pass, stacked)  14.6 us
    add x2, other arithmetic, along_nodes(): return left_node + (right_node - left_node) * within  12 us
    mul x1, other arithmetic, local(): x_ms = (along_nodes(band_nodes[0], coarse_pos, 0.5, GRID) - 1.5) * 0.25  10.1 us
    ppermute x2, starting transfers between devices, padded(): lax.ppermute(head, axis, [((i + 1) % count, i) for i in range(ends)])  8.17 us
  transfers between devices with their start and end apart: 6, of which 3 were waited for; matrix products, arithmetic and copies ran while one was open for 12% of the time, Pallas kernels for 0%

commit v1 on v0

v1 whole, which is shorter than its diff:
```python
import functools

import jax
import jax.numpy as jnp
from jax import lax
from jax.experimental import pallas as pl
from jax.experimental.pallas import tpu as pltpu
from jax.sharding import PartitionSpec as P

GRID = 64
TR = 128
TC = 512
KR = 2
KC = 5

F32 = jnp.float32
BF16 = jnp.bfloat16
VMEM_LIMIT = 56 * 1024 * 1024


def params():
    return pltpu.CompilerParams(vmem_limit_bytes=VMEM_LIMIT)


def whole(memory_space=pltpu.VMEM):
    return pl.BlockSpec(memory_space=memory_space)


def cubic_weight(offset):
    distance = jnp.abs(offset)
    near_part = (1.5 * distance - 2.5) * distance * distance + 1.0
    far_part = ((-0.5 * distance + 2.5) * distance - 4.0) * distance + 2.0
    return jnp.where(
        distance <= 1.0, near_part, jnp.where(distance < 2.0, far_part, jnp.zeros_like(distance))
    )


def iota(shape, dim):
    return lax.broadcasted_iota(jnp.int32, shape, dim)


def along(node, local, position, offset, first, count, last):
    left = jnp.zeros(position.shape, F32)
    right = left
    start = jnp.zeros(position.shape, jnp.int32)
    for k in range(count):
        segment = jnp.minimum(first + k, last)
        here = local == k
        left = jnp.where(here, node(segment), left)
        right = jnp.where(here, node(segment + 1), right)
        start = jnp.where(here, segment * GRID, start)
    within = ((position - start).astype(F32) + offset) / GRID
    return left + (right - left) * within


def cell_sums(n_dest, group, capacity, list_ref, pan_ref, ms_ref, pan_out, ms_out, pan_acc, ms_acc):
    first = pl.program_id(0) * group
    block, coarse = pan_ref.shape[1], ms_ref.shape[1]
    pan_acc[...] = jnp.zeros_like(pan_acc)
    ms_acc[...] = jnp.zeros_like(ms_acc)

    def add(j, carry):
        place = list_ref[0, j] // capacity - first
        row, col = list_ref[1, j], list_ref[2, j]
        cell = place * KC + lax.rem(col, KC)

        @pl.when((place >= 0) & (place < group))
        def _():
            rows = pl.ds(pl.multiple_of(row * block, block), block)
            pan_acc[cell, rows, :] += pan_ref[j].astype(F32)
            rows = pl.ds(pl.multiple_of(row * coarse, coarse), coarse)
            ms_acc[cell, rows, :] += ms_ref[j].astype(F32)

        return carry

    lax.fori_loop(0, pan_ref.shape[0], add, 0)
    pan_out[...] = pan_acc[...].astype(BF16)
    ms_out[...] = ms_acc[...].astype(BF16)


def tap_fill(table, row0, rows, x, first_pixel, cols=None):
    floor = jnp.floor(x)
    taps = [cubic_weight(x - (floor - 1.0 + a)).astype(BF16) for a in range(4)]
    offset = jnp.clip(floor - 1.0 - first_pixel, -8.0, rows + 8.0)
    base = (iota(x.shape, 0).astype(F32) - offset).astype(BF16)
    zero = jnp.zeros(x.shape, BF16)
    for slab in range(rows // 16):
        value = zero
        for a in range(4):
            value = jnp.where(base == jnp.asarray(a - 16 * slab, BF16), taps[a], value)
        yield slab, value


def maps(n, bands, who, rows_ref, cols_ref, pan_ref, ms_ref, *rest):
    outs, (table, spread, edge) = rest[:n], rest[n:]
    g = pl.program_id(0)
    me, c = who[0], who[1]
    dest = me ^ g
    block = pan_ref.shape[2] // KR
    coarse = ms_ref.shape[2] // KR
    half = 128 // coarse
    halves = bands // half
    crows, ccols = TR // 4, TC // 4
    row_nodes = TR // GRID + 1
    col_nodes = cols_ref.shape[1]

    @pl.when(g == 0)
    def _():
        spread[...] = jnp.zeros_like(spread)

    def row_node(s):
        return rows_ref[g, s]

    position = iota((TR, 128), 0)
    y = along(row_node, position // GRID, position, 0.0, 0, row_nodes - 1, row_nodes - 2)
    lane = iota((TR, 128), 1)
    weight = [
        cubic_weight(y - (lane + k * 128).astype(F32)).astype(BF16)
        for k in range(KR * block // 128)
    ]
    weight = jnp.concatenate(weight, axis=1)
    source = jnp.concatenate([pan_ref[0, k] for k in range(KC)], axis=1)
    held = jnp.dot(weight, source, preferred_element_type=F32).astype(BF16)

    def col_node(s):
        return cols_ref[g, s]

    segments = TC // GRID
    local = iota((16, TC), 1)
    x = along(
        col_node, local // GRID, c * TC + local, 0.0, c * segments, segments, col_nodes - 2
    )
    for k in range(KC):
        pixel = ((c * KC + k) * block).astype(F32)
        for slab, value in tap_fill(table, k * block, block, x, pixel):
            table[pl.ds(k * block + 16 * slab, 16), :] = value
    pan_map = jnp.dot(held, table[...], preferred_element_type=F32).astype(BF16)

    i = iota((crows + 8, KR * coarse), 0)
    extra = (i - crows) % 4
    i = jnp.where(i < crows, i, jnp.where(extra < 2, crows - 2 + extra, extra - 2))
    position = 4 * i + 1
    y = along(row_node, position // GRID, position, 0.5, 0, row_nodes - 1, row_nodes - 2)
    y = (y - 1.5) * 0.25
    weight = cubic_weight(y - iota(y.shape, 1).astype(F32)).astype(BF16)
    source = jnp.concatenate([ms_ref[0, k] for k in range(KC)], axis=1)
    held = jnp.dot(weight, source, preferred_element_type=F32)
    lanes = bands * coarse
    left = jnp.concatenate(
        [
            jnp.concatenate(
                [held[:, k * lanes + h * 128 : k * lanes + h * 128 + 128] for k in range(KC)],
                axis=1,
            )
            for h in range(halves)
        ],
        axis=0,
    ).astype(BF16)
    v = iota((16, ccols), 1)
    position = 4 * v + 1
    x = along(
        col_node, position // GRID, c * TC + position, 0.5, c * segments, segments, col_nodes - 2
    )
    x = (x - 1.5) * 0.25
    for k in range(KC):
        pixel = ((c * KC + k) * coarse).astype(F32)
        for slab, value in tap_fill(spread, k * 128, coarse, x, pixel):
            for s in range(half):
                at = k * 128 + s * coarse + 16 * slab
                spread[pl.ds(at, 16), s * ccols : (s + 1) * ccols] = value
    ms_map = jnp.dot(left, spread[...], preferred_element_type=F32)
    tall = crows + 8
    main = jnp.concatenate([ms_map[h * tall : h * tall + crows] for h in range(halves)], axis=0)
    main = main.astype(BF16)
    group = ms_map[crows:tall]
    upper = iota(group.shape, 0) < 4
    edge[dest + 1] = jnp.where(upper, group, ms_map[tall + crows : 2 * tall])
    base = TR + halves * crows
    for k in range(n):

        @pl.when(g == k)
        def _(k=k):
            outs[k][0:TR, :] = pan_map
            outs[k][TR:base, :] = main

    @pl.when(g == n - 1)
    def _():
        edge[0] = jnp.zeros(edge.shape[1:], F32)
        edge[n + 1] = jnp.zeros(edge.shape[1:], F32)
        mine = (iota(group.shape, 0) & 2) == 0
        for k in range(n):
            at = me ^ k
            halo = jnp.where(mine, edge[at], edge[at + 2])
            halo = jnp.concatenate([halo, jnp.zeros_like(halo)], axis=0)
            outs[k][base : base + 16, :] = halo.astype(BF16)


def ms_total(start, *refs):
    out = refs[-1]
    total = refs[0][start:, :].astype(F32)
    for ref in refs[1:-1]:
        total = total + ref[start:, :].astype(F32)
    out[...] = total.astype(BF16)


def pan_total(stop, *refs):
    out = refs[-1]
    total = refs[0][:stop, :].astype(F32)
    for ref in refs[1:-1]:
        total = total + ref[:stop, :].astype(F32)
    out[...] = total


def tables(bands, who, mix, gain, synth, up_out, cols_out):
    c = who[1]
    crows, ccols = TR // 4, TC // 4
    half = bands // 2
    v = iota((2 * ccols, TC), 1).astype(F32)
    q = iota((2 * ccols, TC), 0)
    q = jnp.where(q < ccols, q, jnp.where(c == 0, q, q - 2 * ccols)).astype(F32)
    cols_out[...] = cubic_weight((v - 1.5) * 0.25 - q).astype(BF16)
    lanes = up_out.shape[2]
    lane = iota((1, lanes), 1)
    s = lane // 80
    q = lane - s * 80
    e = q - 2 * crows
    low = q < 2 * crows
    h = jnp.where(low, q // crows, e // 4)
    band = jnp.where((s < half) & (q < 2 * crows + 8), h * half + s, -1)
    tail = e % 4
    w = jnp.where(low, 2 + q % crows, jnp.where(tail < 2, tail, crows + tail))
    r = iota((TR, lanes), 0).astype(F32)
    up = cubic_weight((r - 1.5) * 0.25 + 2.0 - w.astype(F32)).astype(BF16).astype(F32)
    for b in range(bands):
        factor = jnp.zeros((1, lanes), F32)
        for k in range(bands):
            value = mix[b, k] - gain[b] * synth[k]
            if k == b:
                value = value + 1.0
            factor = jnp.where(band == k, value, factor)
        up_out[b] = (up * factor).astype(BF16)


def finish(bands, gain, up_ref, cols_ref, pan_ref, ms_ref, other_ref, out):
    half = bands // 2
    ccols = TC // 4
    pieces = []
    for s in range(half):
        at = slice(s * ccols, (s + 1) * ccols)
        pieces.append(jnp.concatenate([ms_ref[:, at], other_ref[:, at]], axis=1))
    left = jnp.concatenate(pieces, axis=0)
    across = jnp.dot(left, cols_ref[...], preferred_element_type=F32).astype(BF16)
    pad = up_ref.shape[2] - across.shape[0]
    if pad:
        across = jnp.concatenate([across, jnp.zeros((pad, TC), BF16)], axis=0)
    for b in range(bands):
        value = jnp.dot(up_ref[b], across, preferred_element_type=F32)
        out[b] = (value + gain[b] * pan_ref[...]).astype(BF16)


def exchange(x, step, count):
    return lax.ppermute(x, "mrow", [(i, i ^ step) for i in range(count)])


def local(
    pan_blocks,
    ms_blocks,
    send_list,
    tile_list,
    row_grid,
    col_grid,
    band_mix,
    band_gain,
    synth_weight,
):
    n = lax.axis_size("mrow")
    me, c = lax.axis_index("mrow"), lax.axis_index("mcol")
    capacity = tile_list.shape[1] // n
    own, block = pan_blocks.shape[0], pan_blocks.shape[1]
    coarse = ms_blocks.shape[1]
    bands = band_gain.shape[0]
    who = jnp.stack([me, c]).astype(jnp.int32)

    across_cols = lax.all_gather(col_grid[0], "mcol", axis=0, tiled=True)
    mine = jnp.concatenate([row_grid, across_cols])[None]
    pair = jnp.concatenate([mine, exchange(mine, 1, n)], axis=0)
    grids = jnp.concatenate([pair] + [exchange(pair, k, n) for k in range(2, n, 2)], axis=0)
    rows_all, cols_all = grids[:, : row_grid.shape[0]], grids[:, row_grid.shape[0] :]

    group = min(n, 8)
    pan_cells, ms_cells = pl.pallas_call(
        functools.partial(cell_sums, n, group, capacity),
        grid=(n // group,),
        in_specs=[whole(pltpu.SMEM), whole(), whole()],
        out_specs=[
            pl.BlockSpec((group * KC, KR * block, block), lambda i: (i, 0, 0)),
            pl.BlockSpec((group * KC, KR * coarse, bands * coarse), lambda i: (i, 0, 0)),
        ],
        out_shape=[
            jax.ShapeDtypeStruct((n * KC, KR * block, block), BF16),
            jax.ShapeDtypeStruct((n * KC, KR * coarse, bands * coarse), BF16),
        ],
        scratch_shapes=[
            pltpu.VMEM((group * KC, KR * block, block), F32),
            pltpu.VMEM((group * KC, KR * coarse, bands * coarse), F32),
        ],
        compiler_params=params(),
        name="cell_sums",
    )(send_list, pan_blocks, ms_blocks)

    start = TR
    height = TR + 2 * (TR // 4) + 16
    pieces = pl.pallas_call(
        functools.partial(maps, n, bands),
        grid_spec=pltpu.PrefetchScalarGridSpec(
            num_scalar_prefetch=3,
            grid=(n,),
            in_specs=[
                pl.BlockSpec((1, KC, KR * block, block), lambda g, w, a, b: (w[0] ^ g, 0, 0, 0)),
                pl.BlockSpec(
                    (1, KC, KR * coarse, bands * coarse), lambda g, w, a, b: (w[0] ^ g, 0, 0, 0)
                ),
            ],
            out_specs=[pl.BlockSpec((height, TC), lambda g, w, a, b: (0, 0)) for _ in range(n)],
            scratch_shapes=[
                pltpu.VMEM((KC * block, TC), BF16),
                pltpu.VMEM((KC * 128, TC), BF16),
                pltpu.VMEM((n + 2, 8, TC), F32),
            ],
        ),
        out_shape=[jax.ShapeDtypeStruct((height, TC), BF16) for _ in range(n)],
        compiler_params=params(),
        name="maps",
    )(
        who,
        rows_all,
        cols_all,
        pan_cells.reshape(n, KC, KR * block, block),
        ms_cells.reshape(n, KC, KR * coarse, bands * coarse),
    )
    got = [pieces[0]] + [exchange(pieces[k], k, n) for k in range(1, n)]

    lanes = 3 * 128
    up, cols = pl.pallas_call(
        functools.partial(tables, bands),
        in_specs=[whole(pltpu.SMEM)] * 4,
        out_specs=[whole(), whole()],
        out_shape=[
            jax.ShapeDtypeStruct((bands, TR, lanes), BF16),
            jax.ShapeDtypeStruct((TC // 2, TC), BF16),
        ],
        compiler_params=params(),
        name="tables",
    )(who, band_mix, band_gain, synth_weight)

    ms_map = pl.pallas_call(
        functools.partial(ms_total, start),
        in_specs=[whole()] * n,
        out_specs=whole(),
        out_shape=jax.ShapeDtypeStruct((height - start, TC), BF16),
        compiler_params=params(),
        name="ms_total",
    )(*got)
    other = lax.ppermute(ms_map, "mcol", [(0, 1), (1, 0)])
    pan_map = pl.pallas_call(
        functools.partial(pan_total, start),
        in_specs=[whole()] * n,
        out_specs=whole(),
        out_shape=jax.ShapeDtypeStruct((TR, TC), F32),
        compiler_params=params(),
        name="pan_total",
    )(*got)
    return pl.pallas_call(
        functools.partial(finish, bands),
        in_specs=[whole(pltpu.SMEM)] + [whole()] * 5,
        out_specs=whole(),
        out_shape=jax.ShapeDtypeStruct((bands, TR, TC), BF16),
        compiler_params=params(),
        name="finish",
    )(band_gain, up, cols, pan_map, ms_map, other)


def solution(mesh):
    return jax.shard_map(
        local,
        mesh=mesh,
        in_specs=(
            P(("scene", "mrow", "mcol"), None, None),
            P(("scene", "mrow", "mcol"), None, None),
            P(None, ("scene", "mrow", "mcol")),
            P(None, ("scene", "mrow", "mcol")),
            P(("scene", "mrow")),
            P(("scene", "mrow"), "mcol"),
            P(),
            P(),
            P(),
        ),
        out_specs=P(None, ("scene", "mrow"), "mcol"),
        check_vma=False,
    )
```

time: 294 us -> 81.8 us (0.28); the launches traced: 289 us -> 80.9 us
  matrix products: 92.2 us -> 0 us
  waiting for transfers between devices: 102 us -> 29.6 us
  other arithmetic: 36.2 us -> 1.31 us
  Pallas kernels: 0 us -> 26.8 us
  local copies, waits for them, and re-layouts: 29.7 us -> 4 us
  starting transfers between devices: 23.5 us -> 15.7 us
    all_to_all x2 -> x0, waiting for transfers between devices: 101 us -> none  [the longest x1 61.7 us: local(): lax.all_to_all(pan_send.reshape(row_owners, capacity, block_size, block_s...]
    dot_general x38 -> x0, matrix products: 92.2 us -> none  [the longest x16 55.7 us: column_pass(): jnp.einsum('sij,scj->sic', pan_data, col_weight, preferred_element_type=j...]
    ppermute x4 -> x12, waiting for transfers between devices: 0.7 us -> 29.6 us  [the longest x11 29.6 us: exchange(): return lax.ppermute(x, 'mrow', [(i, i ^ step) for i in range(count)])]
    pallas_call x0 -> x6, Pallas kernels: none -> 26.8 us  [the longest x1 10.3 us: local(): pl.pallas_call(functools.partial(maps, n, bands), grid_spec=pltpu.Prefetc...]
    dynamic_slice x16 -> x0, local copies, waits for them, and re-layouts: 14.6 us -> none  [grouped_pass(): pan_cols, ms_cols = lax.map(column_pass, stacked)]
    mul x19 -> x0, other arithmetic: 12.1 us -> none  [the longest x1 10.1 us: local(): x_ms = (along_nodes(band_nodes[0], coarse_pos, 0.5, GRID) - 1.5) * 0.25]
    add x4 -> x0, other arithmetic: 12 us -> none  [the longest x2 12 us: along_nodes(): return left_node + (right_node - left_node) * within]
    all_to_all x2 -> x0, starting transfers between devices: 11.4 us -> none  [the longest x1 5.72 us: local(): lax.all_to_all(ms_send.reshape(row_owners, capacity, coarse_size, ms_bloc...]
  transfers between devices with their start and end apart: 6 -> 12, of which waited for: 3 -> 6; matrix products, arithmetic and copies ran while one was open for 12% -> 1% of each run, Pallas kernels for 0% -> 14%
where the time goes in v1:
time: 81.8 us; the launch traced here: 80.9 us
  waiting for transfers between devices  29.6 us (36%)
  Pallas kernels  26.8 us (33%)
  starting transfers between devices  15.7 us (19%)
  local copies, waits for them, and re-layouts  4 us (5%)
  blocking collectives  2.78 us (3%)
  other arithmetic  1.31 us (2%)
    ppermute x11, waiting for transfers between devices, exchange(): return lax.ppermute(x, 'mrow', [(i, i ^ step) for i in range(count)])  29.6 us
    ppermute x11, starting transfers between devices, exchange(): return lax.ppermute(x, 'mrow', [(i, i ^ step) for i in range(count)])  13.7 us
    pallas_call x1, Pallas kernels, local(): pl.pallas_call(functools.partial(maps, n, bands), grid_spec=pltpu.Prefetc...  10.3 us
    pallas_call x1, Pallas kernels, local(): pl.pallas_call(functools.partial(cell_sums, n, group, capacity), grid=(n...  6.43 us
    unnamed x21, local copies, waits for them, and re-layouts  3.31 us
    pallas_call x1, Pallas kernels, local(): pl.pallas_call(functools.partial(finish, bands), in_specs=[whole(pltpu.SM...  3.2 us
    all_gather x1, blocking collectives, local(): across_cols = lax.all_gather(col_grid[0], 'mcol', axis=0, tiled=True)  2.78 us
    pallas_call x1, Pallas kernels, local(): pl.pallas_call(functools.partial(pan_total, start), in_specs=[whole()] *...  2.34 us
  transfers between devices with their start and end apart: 12, of which 6 were waited for; matrix products, arithmetic and copies ran while one was open for 1% of the time, Pallas kernels for 14%

profile of v1, /device:TPU:11, one launch (start us, length us, event | category | flops | bytes accessed | tf_op | source)
XLA Modules:
  0.0 80.9 jit_solution(6417099900165991446)
XLA Ops:
  0.0 1.2 %dynamic-slice = u32[1]{0:T(128)} dynamic-slice(u32[32]{0:T(128)} %constant.12, u32[]{:T(128)S(6)} %add), dynamic_slice_sizes={1} | dynamic-slice | bytes 12
  1.9 0.8 bitcast_dynamic-update-slice_fusion
  2.7 2.8 %all-reduce = f32[16]{0:T(128)S(1)} all-reduce(f32[16]{0:T(128)S(1)} %bitcast_dynamic-update-slice_fusion), channel_id=2, replica_groups=mesh['scene'=2,'mrow'=8,'mcol'=2] {'mcol'}, use_global_device_ids=true, to_apply=%add | all-reduce | flops 16 | bytes 128 | tf_op jit(solution)/shard_map/all_gather | solution.py:284
  5.4 0.7 maximum_bitcast_fusion
  6.2 1.2 %collective-permute-start = (f32[1,19]{1,0:T(1,128)S(1)}, f32[1,19]{1,0:T(1,128)S(1)}, u32[]{:S(2)}, u32[]{:S(2)}) collective-permute-start(f32[1,19]{1,0:T(1,128)S(1)} %maximum_bitcast_fusion), channel_id=1, source_target_pairs={{0,2},{2,0},{4,6},{6,4},{8,10},{10,8},{12,14},{14,12},{1,3},{3,1},... | collective-permute-start | bytes 236 | tf_op jit(solution)/shard_map/ppermute | solution.py:262
  7.4 0.6 pad_add_fusion.who
  8.0 0.6 collective-permute-done
  8.6 0.2 collective-permute-start.1
  8.8 2.3 %collective-permute-start.2 = (f32[2,19]{1,0:T(2,128)S(1)}, f32[2,19]{1,0:T(2,128)S(1)}, u32[]{:S(2)}, u32[]{:S(2)}) collective-permute-start(f32[2,19]{1,0:T(2,128)S(1)} %pad_maximum_fusion), channel_id=1, source_target_pairs={{0,8},{2,10},{4,12},{6,14},{8,0},{10,2},{12,4},{14,6},{1,9},{3,11}... | collective-permute-start | bytes 464 | tf_op jit(solution)/shard_map/ppermute | solution.py:262
  11.1 0.2 collective-permute-start.3
  11.3 6.4 %cell_sums.1 = (bf16[40,256,128]{2,1,0:T(8,128)(2,1)}, bf16[40,64,256]{2,1,0:T(8,128)(2,1)}) custom-call(s32[3,64]{1,0:T(4,128)} %list_ref.1, bf16[64,128,128]{2,1,0:T(8,128)(2,1)} %pan_ref.1, bf16[64,32,256]{2,1,0:T(8,128)(2,1)} %ms_ref.1), custom_call_target="tpu_custom_call" | custom-call | tf_op jit(solution)/shard_map/cell_sums/pallas_call | solution.py:291
  17.7 0.0 collective-permute-done.1
  17.7 0.0 collective-permute-done.2
  17.7 0.0 collective-permute-done.3
  17.7 0.0 copy-start.8
  17.7 0.7 slice.7.cols_ref
  18.4 0.0 copy-done.8
  18.4 10.3 %maps.1 = (bf16[208,512]{1,0:T(8,128)(2,1)}, bf16[208,512]{1,0:T(8,128)(2,1)}, bf16[208,512]{1,0:T(8,128)(2,1)}, bf16[208,512]{1,0:T(8,128)(2,1)}, bf16[208,512]...) custom-call(s32[2]{0:T(128)} %pad_add_fusion.who, ...), custom_call_target="tpu_custom_call" | custom-call | tf_op jit(solution)/shard_map/maps/pallas_call | solution.py:313
  28.7 2.3 %collective-permute-start.10 = (bf16[208,512]{1,0:T(8,128)(2,1)}, bf16[208,512]{1,0:T(8,128)(2,1)S(1)}, u32[]{:S(2)}, u32[]{:S(2)}) collective-permute-start(bf16[208,512]{1,0:T(8,128)(2,1)} %get-tuple-element.28), channel_id=1, source_target_pairs={{0,14},{2,12},{4,10},{6,8},{8,6},{10,4},{12,2},{14,0},{1,15},{3,13... | collective-permute-start | bytes 638984 | tf_op jit(solution)/shard_map/ppermute | solution.py:262
  31.0 0.2 collective-permute-start.4
  31.2 3.1 %collective-permute-start.5 = (bf16[208,512]{1,0:T(8,128)(2,1)}, bf16[208,512]{1,0:T(8,128)(2,1)S(1)}, u32[]{:S(2)}, u32[]{:S(2)}) collective-permute-start(bf16[208,512]{1,0:T(8,128)(2,1)} %get-tuple-element.23), channel_id=1, source_target_pairs={{0,4},{2,6},{4,0},{6,2},{8,12},{10,14},{12,8},{14,10},{1,5},{3,7},... | collective-permute-start | bytes 638984 | tf_op jit(solution)/shard_map/ppermute | solution.py:262
  34.3 1.0 %collective-permute-start.6 = (bf16[208,512]{1,0:T(8,128)(2,1)}, bf16[208,512]{1,0:T(8,128)(2,1)S(1)}, u32[]{:S(2)}, u32[]{:S(2)}) collective-permute-start(bf16[208,512]{1,0:T(8,128)(2,1)} %get-tuple-element.24), channel_id=1, source_target_pairs={{0,6},{2,4},{4,2},{6,0},{8,14},{10,12},{12,10},{14,8},{1,7},{3,5},... | collective-permute-start | bytes 638984 | tf_op jit(solution)/shard_map/ppermute | solution.py:262
  35.3 0.3 collective-permute-start.7
  35.6 2.2 %collective-permute-done.10.refs_7_ = bf16[208,512]{1,0:T(8,128)(2,1)S(1)} collective-permute-done((bf16[208,512]{1,0:T(8,128)(2,1)}, bf16[208,512]{1,0:T(8,128)(2,1)S(1)}, u32[]{:S(2)}, u32[]{:S(2)}) %collective-permute-start.10) | collective-permute-done | bytes 213024 | tf_op jit(solution)/shard_map/ppermute | solution.py:262
  37.8 0.0 copy-start
  37.8 3.0 %collective-permute-start.8 = (bf16[208,512]{1,0:T(8,128)(2,1)}, bf16[208,512]{1,0:T(8,128)(2,1)S(1)}, u32[]{:S(2)}, u32[]{:S(2)}) collective-permute-start(bf16[208,512]{1,0:T(8,128)(2,1)} %get-tuple-element.26), channel_id=1, source_target_pairs={{0,10},{2,8},{4,14},{6,12},{8,2},{10,0},{12,6},{14,4},{1,11},{3,9}... | collective-permute-start | bytes 638984 | tf_op jit(solution)/shard_map/ppermute | solution.py:262
  40.7 0.0 collective-permute-done.4.refs_1_
  40.7 0.0 copy-start.1
  40.7 0.0 collective-permute-start.9
  40.7 1.2 %collective-permute-done.5.refs_2_ = bf16[208,512]{1,0:T(8,128)(2,1)S(1)} collective-permute-done((bf16[208,512]{1,0:T(8,128)(2,1)}, bf16[208,512]{1,0:T(8,128)(2,1)S(1)}, u32[]{:S(2)}, u32[]{:S(2)}) %collective-permute-start.5) | collective-permute-done | bytes 213024 | tf_op jit(solution)/shard_map/ppermute | solution.py:262
  42.0 0.0 copy-start.2
  42.0 10.1 %collective-permute-done.6.refs_3_ = bf16[208,512]{1,0:T(8,128)(2,1)S(1)} collective-permute-done((bf16[208,512]{1,0:T(8,128)(2,1)}, bf16[208,512]{1,0:T(8,128)(2,1)S(1)}, u32[]{:S(2)}, u32[]{:S(2)}) %collective-permute-start.6) | collective-permute-done | bytes 213024 | tf_op jit(solution)/shard_map/ppermute | solution.py:262
  52.1 0.0 copy-start.3
  52.1 0.0 collective-permute-done.7.refs_4_
  52.1 0.0 copy-start.4
  52.1 2.2 %collective-permute-done.8.refs_5_ = bf16[208,512]{1,0:T(8,128)(2,1)S(1)} collective-permute-done((bf16[208,512]{1,0:T(8,128)(2,1)}, bf16[208,512]{1,0:T(8,128)(2,1)S(1)}, u32[]{:S(2)}, u32[]{:S(2)}) %collective-permute-start.8) | collective-permute-done | bytes 213024 | tf_op jit(solution)/shard_map/ppermute | solution.py:262
  54.3 0.0 copy-start.5
  54.3 13.2 %collective-permute-done.9.refs_6_ = bf16[208,512]{1,0:T(8,128)(2,1)S(1)} collective-permute-done((bf16[208,512]{1,0:T(8,128)(2,1)}, bf16[208,512]{1,0:T(8,128)(2,1)S(1)}, u32[]{:S(2)}, u32[]{:S(2)}) %collective-permute-start.9) | collective-permute-done | bytes 213024 | tf_op jit(solution)/shard_map/ppermute | solution.py:262
  67.5 0.0 copy-start.6
  67.5 0.0 copy-done
  67.5 0.0 copy-done.1
  67.5 0.0 copy-done.2
  67.5 0.0 copy-done.3
  67.5 0.0 copy-done.4
  67.6 0.0 copy-done.5
  67.6 0.7 copy-done.6
  68.2 2.2 %ms_total.1.ms_ref = bf16[80,512]{1,0:T(8,128)(2,1)} custom-call(bf16[208,512]{1,0:T(8,128)(2,1)} %get-tuple-element.21.refs_0_, bf16[208,512]{1,0:T(8,128)(2,1)} %copy-done.1, bf16[208,512]{1,0:T(8,128)(2,1)} %copy-done.2, bf16[208,512]{1,0:T(8,128)(2,1)} %copy-done.3, bf16[208,512]{1,0:T(8,128)(2,1)} %copy-done.4, bf16[208,512]{1,0:T(8,128)(2,1)} %copy-done.5, ...), custom_call_target="tpu_custom_call" | custom-call | tf_op jit(solution)/shard_map/ms_total/pallas_call | solution.py:356
  70.4 2.0 %collective-permute-start.11 = (bf16[80,512]{1,0:T(8,128)(2,1)}, bf16[80,512]{1,0:T(8,128)(2,1)S(1)}, u32[]{:S(2)}, u32[]{:S(2)}) collective-permute-start(bf16[80,512]{1,0:T(8,128)(2,1)} %ms_total.1.ms_ref), channel_id=1, source_target_pairs={{0,1},{1,0},{2,3},{3,2},{4,5},{5,4},{6,7},{7,6},{8,9},{9,8},{10,11... | collective-permute-start | bytes 245768 | tf_op jit(solution)/shard_map/ppermute | solution.py:364
  72.4 2.3 %tables.1 = (bf16[8,128,384]{2,1,0:T(8,128)(2,1)}, bf16[256,512]{1,0:T(8,128)(2,1)}) custom-call(s32[2]{0:T(128)} %pad_add_fusion.who, f32[8,8]{1,0:T(8,128)} %mix.1, f32[8]{0:T(128)} %gain.3, f32[8]{0:T(128)} %synth.1), custom_call_target="tpu_custom_call" | custom-call | tf_op jit(solution)/shard_map/tables/pallas_call | solution.py:344
  74.7 2.3 %pan_total.1.pan_ref = f32[128,512]{1,0:T(8,128)} custom-call(bf16[208,512]{1,0:T(8,128)(2,1)} %get-tuple-element.21.refs_0_, bf16[208,512]{1,0:T(8,128)(2,1)} %copy-done.1, bf16[208,512]{1,0:T(8,128)(2,1)} %copy-done.2, bf16[208,512]{1,0:T(8,128)(2,1)} %copy-done.3, bf16[208,512]{1,0:T(8,128)(2,1)} %copy-done.4, bf16[208,512]{1,0:T(8,128)(2,1)} %copy-done.5, ...), custom_call_target="tpu_custom_call" | custom-call | tf_op jit(solution)/shard_map/pan_total/pallas_call | solution.py:365
  77.0 0.0 collective-permute-done.11.other_ref
  77.0 0.0 copy-start.7
  77.0 0.6 copy-done.7
  77.7 3.2 %finish.1 = bf16[8,128,512]{2,1,0:T(8,128)(2,1)} custom-call(f32[8]{0:T(128)} %gain.3, bf16[8,128,384]{2,1,0:T(8,128)(2,1)} %get-tuple-element.17.up_ref, bf16[256,512]{1,0:T(8,128)(2,1)} %get-tuple-element.18.cols_ref, f32[128,512]{1,0:T(8,128)} %pan_total.1.pan_ref, bf16[80,512]{1,0:T(8,128)(2,1)} %ms_total.1.ms_ref, bf16[80,512]{1,0:T(8,128)(2,1)} %copy-done.7), custom_call_target="tpu_custom_call" | custom-call | tf_op jit(solution)/shard_map/finish/pallas_call | solution.py:373
  (3 shorter events, 0.0 us)
Async XLA Ops:
  6.2 2.4 %collective-permute-start = (f32[1,19]{1,0:T(1,128)S(1)}, f32[1,19]{1,0:T(1,128)S(1)}, u32[]{:S(2)}, u32[]{:S(2)}) collective-permute-start(f32[1,19]{1,0:T(1,128)S(1)} %maximum_bitcast_fusion), channel_id=1, source_target_pairs={{0,2},{2,0},{4,6},{6,4},{8,10},{10,8},{12,14},{14,12},{1,3},{3,1},... | collective-permute-start | bytes 236 | tf_op jit(solution)/shard_map/ppermute | solution.py:262
  8.6 9.1 %collective-permute-start.1 = (f32[2,19]{1,0:T(2,128)S(1)}, f32[2,19]{1,0:T(2,128)S(1)}, u32[]{:S(2)}, u32[]{:S(2)}) collective-permute-start(f32[2,19]{1,0:T(2,128)S(1)} %pad_maximum_fusion), channel_id=1, source_target_pairs={{0,4},{2,6},{4,0},{6,2},{8,12},{10,14},{12,8},{14,10},{1,5},{3,7},... | collective-permute-start | bytes 464 | tf_op jit(solution)/shard_map/ppermute | solution.py:262
  8.8 8.9 %collective-permute-start.2 = (f32[2,19]{1,0:T(2,128)S(1)}, f32[2,19]{1,0:T(2,128)S(1)}, u32[]{:S(2)}, u32[]{:S(2)}) collective-permute-start(f32[2,19]{1,0:T(2,128)S(1)} %pad_maximum_fusion), channel_id=1, source_target_pairs={{0,8},{2,10},{4,12},{6,14},{8,0},{10,2},{12,4},{14,6},{1,9},{3,11}... | collective-permute-start | bytes 464 | tf_op jit(solution)/shard_map/ppermute | solution.py:262
  11.1 6.6 %collective-permute-start.3 = (f32[2,19]{1,0:T(2,128)S(1)}, f32[2,19]{1,0:T(2,128)S(1)}, u32[]{:S(2)}, u32[]{:S(2)}) collective-permute-start(f32[2,19]{1,0:T(2,128)S(1)} %pad_maximum_fusion), channel_id=1, source_target_pairs={{0,12},{2,14},{4,8},{6,10},{8,4},{10,6},{12,0},{14,2},{1,13},{3,15... | collective-permute-start | bytes 464 | tf_op jit(solution)/shard_map/ppermute | solution.py:262
  17.7 0.7 copy-start.8
  28.7 9.0 %collective-permute-start.10 = (bf16[208,512]{1,0:T(8,128)(2,1)}, bf16[208,512]{1,0:T(8,128)(2,1)S(1)}, u32[]{:S(2)}, u32[]{:S(2)}) collective-permute-start(bf16[208,512]{1,0:T(8,128)(2,1)} %get-tuple-element.28), channel_id=1, source_target_pairs={{0,14},{2,12},{4,10},{6,8},{8,6},{10,4},{12,2},{14,0},{1,15},{3,13... | collective-permute-start | bytes 638984 | tf_op jit(solution)/shard_map/ppermute | solution.py:262
  31.0 9.7 %collective-permute-start.4 = (bf16[208,512]{1,0:T(8,128)(2,1)}, bf16[208,512]{1,0:T(8,128)(2,1)S(1)}, u32[]{:S(2)}, u32[]{:S(2)}) collective-permute-start(bf16[208,512]{1,0:T(8,128)(2,1)} %get-tuple-element.22), channel_id=1, source_target_pairs={{0,2},{2,0},{4,6},{6,4},{8,10},{10,8},{12,14},{14,12},{1,3},{3,1},... | collective-permute-start | bytes 638984 | tf_op jit(solution)/shard_map/ppermute | solution.py:262
  31.2 10.7 %collective-permute-start.5 = (bf16[208,512]{1,0:T(8,128)(2,1)}, bf16[208,512]{1,0:T(8,128)(2,1)S(1)}, u32[]{:S(2)}, u32[]{:S(2)}) collective-permute-start(bf16[208,512]{1,0:T(8,128)(2,1)} %get-tuple-element.23), channel_id=1, source_target_pairs={{0,4},{2,6},{4,0},{6,2},{8,12},{10,14},{12,8},{14,10},{1,5},{3,7},... | collective-permute-start | bytes 638984 | tf_op jit(solution)/shard_map/ppermute | solution.py:262
  34.3 17.8 %collective-permute-start.6 = (bf16[208,512]{1,0:T(8,128)(2,1)}, bf16[208,512]{1,0:T(8,128)(2,1)S(1)}, u32[]{:S(2)}, u32[]{:S(2)}) collective-permute-start(bf16[208,512]{1,0:T(8,128)(2,1)} %get-tuple-element.24), channel_id=1, source_target_pairs={{0,6},{2,4},{4,2},{6,0},{8,14},{10,12},{12,10},{14,8},{1,7},{3,5},... | collective-permute-start | bytes 638984 | tf_op jit(solution)/shard_map/ppermute | solution.py:262
  35.3 16.8 %collective-permute-start.7 = (bf16[208,512]{1,0:T(8,128)(2,1)}, bf16[208,512]{1,0:T(8,128)(2,1)S(1)}, u32[]{:S(2)}, u32[]{:S(2)}) collective-permute-start(bf16[208,512]{1,0:T(8,128)(2,1)} %get-tuple-element.25), channel_id=1, source_target_pairs={{0,8},{2,10},{4,12},{6,14},{8,0},{10,2},{12,4},{14,6},{1,9},{3,11}... | collective-permute-start | bytes 638984 | tf_op jit(solution)/shard_map/ppermute | solution.py:262
  37.8 29.8 %copy-start = (bf16[208,512]{1,0:T(8,128)(2,1)}, bf16[208,512]{1,0:T(8,128)(2,1)S(1)}, u32[]{:S(2)}) copy-start(bf16[208,512]{1,0:T(8,128)(2,1)S(1)} %collective-permute-done.10.refs_7_) | copy-start | bytes 638980
  37.8 16.6 %collective-permute-start.8 = (bf16[208,512]{1,0:T(8,128)(2,1)}, bf16[208,512]{1,0:T(8,128)(2,1)S(1)}, u32[]{:S(2)}, u32[]{:S(2)}) collective-permute-start(bf16[208,512]{1,0:T(8,128)(2,1)} %get-tuple-element.26), channel_id=1, source_target_pairs={{0,10},{2,8},{4,14},{6,12},{8,2},{10,0},{12,6},{14,4},{1,11},{3,9}... | collective-permute-start | bytes 638984 | tf_op jit(solution)/shard_map/ppermute | solution.py:262
  40.7 26.8 %copy-start.1 = (bf16[208,512]{1,0:T(8,128)(2,1)}, bf16[208,512]{1,0:T(8,128)(2,1)S(1)}, u32[]{:S(2)}) copy-start(bf16[208,512]{1,0:T(8,128)(2,1)S(1)} %collective-permute-done.4.refs_1_) | copy-start | bytes 638980
  40.7 26.8 %collective-permute-start.9 = (bf16[208,512]{1,0:T(8,128)(2,1)}, bf16[208,512]{1,0:T(8,128)(2,1)S(1)}, u32[]{:S(2)}, u32[]{:S(2)}) collective-permute-start(bf16[208,512]{1,0:T(8,128)(2,1)} %get-tuple-element.27), channel_id=1, source_target_pairs={{0,12},{2,14},{4,8},{6,10},{8,4},{10,6},{12,0},{14,2},{1,13},{3,15... | collective-permute-start | bytes 638984 | tf_op jit(solution)/shard_map/ppermute | solution.py:262
  42.0 25.6 %copy-start.2 = (bf16[208,512]{1,0:T(8,128)(2,1)}, bf16[208,512]{1,0:T(8,128)(2,1)S(1)}, u32[]{:S(2)}) copy-start(bf16[208,512]{1,0:T(8,128)(2,1)S(1)} %collective-permute-done.5.refs_2_) | copy-start | bytes 638980
  52.1 15.4 %copy-start.3 = (bf16[208,512]{1,0:T(8,128)(2,1)}, bf16[208,512]{1,0:T(8,128)(2,1)S(1)}, u32[]{:S(2)}) copy-start(bf16[208,512]{1,0:T(8,128)(2,1)S(1)} %collective-permute-done.6.refs_3_) | copy-start | bytes 638980
  52.1 15.5 %copy-start.4 = (bf16[208,512]{1,0:T(8,128)(2,1)}, bf16[208,512]{1,0:T(8,128)(2,1)S(1)}, u32[]{:S(2)}) copy-start(bf16[208,512]{1,0:T(8,128)(2,1)S(1)} %collective-permute-done.7.refs_4_) | copy-start | bytes 638980
  54.3 13.2 %copy-start.5 = (bf16[208,512]{1,0:T(8,128)(2,1)}, bf16[208,512]{1,0:T(8,128)(2,1)S(1)}, u32[]{:S(2)}) copy-start(bf16[208,512]{1,0:T(8,128)(2,1)S(1)} %collective-permute-done.8.refs_5_) | copy-start | bytes 638980
  67.5 0.7 copy-start.6
  70.4 6.6 %collective-permute-start.11 = (bf16[80,512]{1,0:T(8,128)(2,1)}, bf16[80,512]{1,0:T(8,128)(2,1)S(1)}, u32[]{:S(2)}, u32[]{:S(2)}) collective-permute-start(bf16[80,512]{1,0:T(8,128)(2,1)} %ms_total.1.ms_ref), channel_id=1, source_target_pairs={{0,1},{1,0},{2,3},{3,2},{4,5},{5,4},{6,7},{7,6},{8,9},{9,8},{10,11... | collective-permute-start | bytes 245768 | tf_op jit(solution)/shard_map/ppermute | solution.py:364
  77.0 0.6 copy-start.7

commit v2 on v1

v2 whole, which is shorter than its diff:
```python
import functools

import jax
import jax.numpy as jnp
from jax import lax
from jax.experimental import pallas as pl
from jax.experimental.pallas import tpu as pltpu
from jax.sharding import PartitionSpec as P

GRID = 64
TR = 128
TC = 512
KR = 2
KC = 5

F32 = jnp.float32
BF16 = jnp.bfloat16
VMEM_LIMIT = 56 * 1024 * 1024


def params():
    return pltpu.CompilerParams(vmem_limit_bytes=VMEM_LIMIT)


def whole(memory_space=pltpu.VMEM):
    return pl.BlockSpec(memory_space=memory_space)


def cubic_weight(offset):
    distance = jnp.abs(offset)
    near_part = (1.5 * distance - 2.5) * distance * distance + 1.0
    far_part = ((-0.5 * distance + 2.5) * distance - 4.0) * distance + 2.0
    return jnp.where(
        distance <= 1.0, near_part, jnp.where(distance < 2.0, far_part, jnp.zeros_like(distance))
    )


def iota(shape, dim):
    return lax.broadcasted_iota(jnp.int32, shape, dim)


def along(node, local, position, offset, first, count, last):
    left = jnp.zeros(position.shape, F32)
    right = left
    start = jnp.zeros(position.shape, jnp.int32)
    for k in range(count):
        segment = jnp.minimum(first + k, last)
        here = local == k
        left = jnp.where(here, node(segment), left)
        right = jnp.where(here, node(segment + 1), right)
        start = jnp.where(here, segment * GRID, start)
    within = ((position - start).astype(F32) + offset) / GRID
    return left + (right - left) * within


def cell_sums(group, capacity, who, list_ref, pan_ref, ms_ref, pan_out, ms_out, pan_acc, ms_acc):
    first = pl.program_id(0) * group
    block, coarse = pan_ref.shape[1], ms_ref.shape[1]
    pan_acc[...] = jnp.zeros_like(pan_acc)
    ms_acc[...] = jnp.zeros_like(ms_acc)

    def add(j, carry):
        place = ((list_ref[0, j] // capacity) ^ who[0]) - first
        row, col = list_ref[1, j], list_ref[2, j]
        cell = place * KC + lax.rem(col, KC)

        @pl.when((place >= 0) & (place < group))
        def _():
            rows = pl.ds(pl.multiple_of(row * block, block), block)
            pan_acc[cell, rows, :] += pan_ref[j].astype(F32)
            rows = pl.ds(pl.multiple_of(row * coarse, coarse), coarse)
            ms_acc[cell, rows, :] += ms_ref[j].astype(F32)

        return carry

    lax.fori_loop(0, pan_ref.shape[0], add, 0)
    pan_out[...] = pan_acc[...].astype(BF16)
    ms_out[...] = ms_acc[...].astype(BF16)


def repeat_rows(x):
    return jnp.concatenate([x, x], axis=0)


def tap_fill(rows, x, first_pixel):
    floor = jnp.floor(x)
    taps = [repeat_rows(cubic_weight(x - (floor - 1.0 + a))).astype(BF16) for a in range(4)]
    row = iota((16, x.shape[1]), 0).astype(F32)
    zero = jnp.zeros(row.shape, BF16)
    corner = floor - 1.0

    def at(first):
        offset = jnp.clip(corner - first, -8.0, rows + 8.0)
        base = (row - repeat_rows(offset)).astype(BF16)
        for slab in range(rows // 16):
            value = zero
            for a in range(4):
                value = jnp.where(base == jnp.asarray(a - 16 * slab, BF16), taps[a], value)
            yield slab, value

    for k, first in enumerate(first_pixel):
        for slab, value in at(first):
            yield k, slab, value


def row_nodes(grids, g):
    return lambda s: grids[g, s]


def col_nodes(grids, g, c):
    first = TR // GRID + 1
    each = (grids.shape[1] - first) // 2

    def node(s):
        half = s // each
        return grids[g, first + (half ^ c) * each + (s - half * each)]

    return node


def last_col(grids):
    return grids.shape[1] - (TR // GRID + 1) - 2


def ms_piece(bands, c, g, grids, cells, spread):
    coarse = cells.shape[1] // KR
    half = 128 // coarse
    halves = bands // half
    crows, ccols = TR // 4, TC // 4
    tall = crows + 8
    lanes = bands * coarse
    i = iota((tall, KR * coarse), 0)
    extra = (i - crows) % 4
    i = jnp.where(i < crows, i, jnp.where(extra < 2, crows - 2 + extra, extra - 2))
    position = 4 * i + 1
    y = along(row_nodes(grids, g), position // GRID, position, 0.5, 0, TR // GRID, TR // GRID - 1)
    y = (y - 1.5) * 0.25
    weight = cubic_weight(y - iota(y.shape, 1).astype(F32)).astype(BF16)
    source = jnp.concatenate([cells[k] for k in range(KC)], axis=1)
    held = jnp.dot(weight, source, preferred_element_type=F32)
    left = jnp.concatenate(
        [
            jnp.concatenate(
                [held[:, k * lanes + h * 128 : k * lanes + h * 128 + 128] for k in range(KC)],
                axis=1,
            )
            for h in range(halves)
        ],
        axis=0,
    ).astype(BF16)
    segments = TC // GRID
    position = 4 * iota((8, ccols), 1) + 1
    x = along(
        col_nodes(grids, g, c),
        position // GRID,
        c * TC + position,
        0.5,
        c * segments,
        segments,
        last_col(grids),
    )
    x = (x - 1.5) * 0.25
    pixels = [((c * KC + k) * coarse).astype(F32) for k in range(KC)]
    for k, slab, value in tap_fill(coarse, x, pixels):
        for s in range(half):
            at = k * 128 + s * coarse + 16 * slab
            spread[at : at + 16, s * ccols : (s + 1) * ccols] = value
    return jnp.dot(left, spread[...], preferred_element_type=F32)


def pan_piece(c, g, grids, cells, table):
    block = cells.shape[1] // KR
    position = iota((TR, 128), 0)
    y = along(row_nodes(grids, g), position // GRID, position, 0.0, 0, TR // GRID, TR // GRID - 1)
    lane = iota((TR, 128), 1)
    weight = jnp.concatenate(
        [
            cubic_weight(y - (lane + k * 128).astype(F32)).astype(BF16)
            for k in range(KR * block // 128)
        ],
        axis=1,
    )
    source = jnp.concatenate([cells[k] for k in range(KC)], axis=1)
    held = jnp.dot(weight, source, preferred_element_type=F32).astype(BF16)
    segments = TC // GRID
    v = iota((8, TC), 1)
    x = along(
        col_nodes(grids, g, c), v // GRID, c * TC + v, 0.0, c * segments, segments, last_col(grids)
    )
    pixels = [((c * KC + k) * block).astype(F32) for k in range(KC)]
    for k, slab, value in tap_fill(block, x, pixels):
        at = k * block + 16 * slab
        table[at : at + 16, :] = value
    return jnp.dot(held, table[...], preferred_element_type=F32)


def far_maps(n, bands, who, grids, ms_cells, pan_cells, *refs):
    pairs = n // 2
    outs, near = refs[:pairs], refs[pairs]
    spread, (table, edge) = refs[pairs + 1 : pairs + 3], refs[pairs + 3 :]
    step = pl.program_id(0)
    me, c = who[0], who[1]
    crows = TR // 4
    tall = crows + 8
    group = (8, TC)
    upper = iota(group, 0) < 4
    base = TR + 2 * crows

    @pl.when(step == 0)
    def _():
        for ref in spread:
            ref[...] = jnp.zeros_like(ref)

    mains = []
    for u in range(2):
        g = 2 * step + u
        ms_map = ms_piece(bands, c, g, grids, ms_cells[u], spread[u])
        main = jnp.concatenate([ms_map[0:crows], ms_map[tall : tall + crows]], axis=0)
        mains.append(main.astype(BF16))
        edge[(me ^ g) + 1] = jnp.where(upper, ms_map[crows:tall], ms_map[tall + crows : 2 * tall])
    pan_map = pan_piece(c, n - 1 - 2 * step, grids, pan_cells[0], table).astype(BF16)
    near[pairs - 1 - step, 0 : 2 * crows, :] = mains[0]
    for k in range(pairs):

        @pl.when(step == k)
        def _(k=k):
            outs[k][0:TR, :] = pan_map
            outs[pairs - 1 - k][TR:base, :] = mains[1]

    @pl.when(step == pairs - 1)
    def _():
        edge[0] = jnp.zeros(group, F32)
        edge[n + 1] = jnp.zeros(group, F32)
        mine = (iota(group, 0) & 2) == 0

        def halo(g):
            dest = me ^ g
            value = jnp.where(mine, edge[dest], edge[dest + 2])
            return jnp.concatenate([value, jnp.zeros_like(value)], axis=0).astype(BF16)

        for k in range(pairs):
            outs[k][base:, :] = halo(n - 1 - 2 * k)
            near[k, 2 * crows :, :] = halo(n - 2 - 2 * k)


def near_maps(n, fold, who, grids, ms, *refs):
    pairs = n // 2
    cells, outs, table = refs[:fold], refs[fold : fold + pairs], refs[fold + pairs :]
    step = pl.program_id(0)
    for u in range(fold):
        g = n - 2 - 2 * (fold * step + u)
        pan_map = pan_piece(who[1], g, grids, cells[u][0], table[u])
        ms_map = ms[u].astype(F32)
        for k in range(u, pairs, fold):

            @pl.when(fold * step + u == k)
            def _(k=k):
                outs[k][0:TR, :] = pan_map
                outs[k][TR:, :] = ms_map


def tables(bands, who, mix, gain, synth, up_out, cols_out):
    c = who[1]
    crows, ccols = TR // 4, TC // 4
    half = bands // 2
    v = iota((2 * ccols, TC), 1).astype(F32)
    q = iota((2 * ccols, TC), 0)
    q = jnp.where(q < ccols, q, jnp.where(c == 0, q, q - 2 * ccols)).astype(F32)
    cols_out[...] = cubic_weight((v - 1.5) * 0.25 - q).astype(BF16)
    lanes = up_out.shape[2]
    lane = iota((1, lanes), 1)
    s = lane // 80
    q = lane - s * 80
    e = q - 2 * crows
    low = q < 2 * crows
    h = jnp.where(low, q // crows, e // 4)
    band = jnp.where((s < half) & (q < 2 * crows + 8), h * half + s, -1)
    tail = e % 4
    w = jnp.where(low, 2 + q % crows, jnp.where(tail < 2, tail, crows + tail))
    r = iota((TR, lanes), 0).astype(F32)
    up = cubic_weight((r - 1.5) * 0.25 + 2.0 - w.astype(F32)).astype(BF16).astype(F32)
    for b in range(bands):
        factor = jnp.zeros((1, lanes), F32)
        for k in range(bands):
            value = mix[b, k] - gain[b] * synth[k]
            if k == b:
                value = value + 1.0
            factor = jnp.where(band == k, value, factor)
        up_out[b] = (up * factor).astype(BF16)


def finish(bands, gain, up_ref, cols_ref, ms_ref, other_ref, *refs):
    parts, (out, across, pan) = refs[:-3], refs[-3:]
    half = bands // 2
    ccols = TC // 4
    step = pl.program_id(0)

    @pl.when(step == 0)
    def _():
        pieces = []
        for s in range(half):
            at = slice(s * ccols, (s + 1) * ccols)
            pieces.append(jnp.concatenate([ms_ref[:, at], other_ref[:, at]], axis=1))
        left = jnp.concatenate(pieces, axis=0)
        rows = left.shape[0]
        across[0:rows, :] = jnp.dot(left, cols_ref[...], preferred_element_type=F32).astype(BF16)
        across[rows:, :] = jnp.zeros((across.shape[0] - rows, TC), BF16)
        total = parts[0][0:TR, :].astype(F32)
        for ref in parts[1:]:
            total = total + ref[0:TR, :].astype(F32)
        pan[...] = total

    count = up_ref.shape[0]
    for u in range(count):
        value = jnp.dot(up_ref[u], across[...], preferred_element_type=F32)
        out[u] = (value + gain[count * step + u] * pan[...]).astype(BF16)


def exchange(x, step, count):
    return lax.ppermute(x, "mrow", [(i, i ^ step) for i in range(count)])


def local(
    pan_blocks,
    ms_blocks,
    send_list,
    tile_list,
    row_grid,
    col_grid,
    band_mix,
    band_gain,
    synth_weight,
):
    n = lax.axis_size("mrow")
    me, c = lax.axis_index("mrow"), lax.axis_index("mcol")
    capacity = tile_list.shape[1] // n
    own, block = pan_blocks.shape[0], pan_blocks.shape[1]
    coarse = ms_blocks.shape[1]
    bands = band_gain.shape[0]
    who = jnp.stack([me, c]).astype(jnp.int32)

    other_cols = lax.ppermute(col_grid, "mcol", [(0, 1), (1, 0)])
    mine = jnp.concatenate([row_grid[None], col_grid, other_cols], axis=1)
    pair = jnp.concatenate([mine, exchange(mine, 1, n)], axis=0)
    grids = jnp.concatenate([pair] + [exchange(pair, k, n) for k in range(2, n, 2)], axis=0)

    group = min(n, 8)
    pan_cells, ms_cells = pl.pallas_call(
        functools.partial(cell_sums, group, capacity),
        grid=(n // group,),
        in_specs=[whole(pltpu.SMEM), whole(pltpu.SMEM), whole(), whole()],
        out_specs=[
            pl.BlockSpec((group * KC, KR * block, block), lambda i: (i, 0, 0)),
            pl.BlockSpec((group * KC, KR * coarse, bands * coarse), lambda i: (i, 0, 0)),
        ],
        out_shape=[
            jax.ShapeDtypeStruct((n * KC, KR * block, block), BF16),
            jax.ShapeDtypeStruct((n * KC, KR * coarse, bands * coarse), BF16),
        ],
        scratch_shapes=[
            pltpu.VMEM((group * KC, KR * block, block), F32),
            pltpu.VMEM((group * KC, KR * coarse, bands * coarse), F32),
        ],
        compiler_params=params(),
        name="cell_sums",
    )(who, send_list, pan_blocks, ms_blocks)

    start = TR
    tall = 2 * (TR // 4) + 16
    height = TR + tall
    pan_cells = pan_cells.reshape(n, KC, KR * block, block)
    ms_cells = ms_cells.reshape(n, KC, KR * coarse, bands * coarse)

    pairs = n // 2
    result = pl.BlockSpec((height, TC), lambda i: (0, 0))
    *far, near_ms = pl.pallas_call(
        functools.partial(far_maps, n, bands),
        grid=(pairs,),
        in_specs=[
            whole(pltpu.SMEM),
            whole(pltpu.SMEM),
            pl.BlockSpec((2,) + ms_cells.shape[1:], lambda i: (i, 0, 0, 0)),
            pl.BlockSpec((1,) + pan_cells.shape[1:], lambda i: (n - 1 - 2 * i, 0, 0, 0)),
        ],
        out_specs=[result] * pairs + [pl.BlockSpec((pairs, tall, TC), lambda i: (0, 0, 0))],
        scratch_shapes=[pltpu.VMEM((KC * 128, TC), BF16)] * 2
        + [pltpu.VMEM((KC * block, TC), BF16), pltpu.VMEM((n + 2, 8, TC), F32)],
        out_shape=[jax.ShapeDtypeStruct((height, TC), BF16)] * pairs
        + [jax.ShapeDtypeStruct((pairs, tall, TC), BF16)],
        compiler_params=params(),
        name="far_maps",
    )(who, grids, ms_cells, pan_cells)
    steps = [n - 2 - 2 * i for i in range(pairs)]
    theirs = [exchange(piece, 1, n) for piece in far]
    fold = 2
    near = pl.pallas_call(
        functools.partial(near_maps, n, fold),
        grid=(pairs // fold,),
        in_specs=[
            whole(pltpu.SMEM),
            whole(pltpu.SMEM),
            pl.BlockSpec((fold, tall, TC), lambda i: (i, 0, 0)),
        ]
        + [
            pl.BlockSpec(
                (1,) + pan_cells.shape[1:], lambda i, u=u: (n - 2 - 2 * (fold * i + u), 0, 0, 0)
            )
            for u in range(fold)
        ],
        out_specs=[result] * pairs,
        scratch_shapes=[pltpu.VMEM((KC * block, TC), BF16)] * fold,
        out_shape=[jax.ShapeDtypeStruct((height, TC), F32)] * pairs,
        compiler_params=params(),
        name="near_maps",
    )(who, grids, near_ms, *([pan_cells] * fold))

    lanes = 3 * 128
    up, cols = pl.pallas_call(
        functools.partial(tables, bands),
        in_specs=[whole(pltpu.SMEM)] * 4,
        out_specs=[whole(), whole()],
        out_shape=[
            jax.ShapeDtypeStruct((bands, TR, lanes), BF16),
            jax.ShapeDtypeStruct((TC // 2, TC), BF16),
        ],
        compiler_params=params(),
        name="tables",
    )(who, band_mix, band_gain, synth_weight)

    got = [near[-1], theirs[-1]]
    for k, a, b in zip(steps[:-1], near, theirs):
        got.append(exchange((a + b.astype(F32)).astype(BF16), k, n))
    ms_map = sum(part[start:].astype(F32) for part in got).astype(BF16)
    other = lax.ppermute(ms_map, "mcol", [(0, 1), (1, 0)])
    each = 2
    once = lambda x: pl.BlockSpec(x.shape, lambda i: (0, 0))
    return pl.pallas_call(
        functools.partial(finish, bands),
        grid=(bands // each,),
        in_specs=[
            whole(pltpu.SMEM),
            pl.BlockSpec((each, TR, lanes), lambda i: (i, 0, 0)),
            once(cols),
            once(ms_map),
            once(other),
        ]
        + [once(part) for part in got],
        out_specs=pl.BlockSpec((each, TR, TC), lambda i: (i, 0, 0)),
        out_shape=jax.ShapeDtypeStruct((bands, TR, TC), BF16),
        scratch_shapes=[pltpu.VMEM((lanes, TC), BF16), pltpu.VMEM((TR, TC), F32)],
        compiler_params=params(),
        name="finish",
    )(band_gain, up, cols, ms_map, other, *got)


def solution(mesh):
    return jax.shard_map(
        local,
        mesh=mesh,
        in_specs=(
            P(("scene", "mrow", "mcol"), None, None),
            P(("scene", "mrow", "mcol"), None, None),
            P(None, ("scene", "mrow", "mcol")),
            P(None, ("scene", "mrow", "mcol")),
            P(("scene", "mrow")),
            P(("scene", "mrow"), "mcol"),
            P(),
            P(),
            P(),
        ),
        out_specs=P(None, ("scene", "mrow"), "mcol"),
        check_vma=False,
    )
```

time: 81.8 us -> 63.7 us (0.78)
  the two profiles are of different devices: /device:TPU:11 before, /device:TPU:1 now
where the time goes in v2:
time: 63.7 us; the launch traced here: 63.2 us
  Pallas kernels  24.7 us (39%)
  starting transfers between devices  16.3 us (26%)
  waiting for transfers between devices  14.5 us (23%)
  other arithmetic  6.43 us (10%)
  local copies, waits for them, and re-layouts  1.21 us (2%)
    ppermute x11, waiting for transfers between devices, exchange(): return lax.ppermute(x, 'mrow', [(i, i ^ step) for i in range(count)])  13.3 us
    ppermute x11, starting transfers between devices, exchange(): return lax.ppermute(x, 'mrow', [(i, i ^ step) for i in range(count)])  13.2 us
    pallas_call x1, Pallas kernels, local(): pl.pallas_call(functools.partial(far_maps, n, bands), grid=(pairs,), in_s...  6.58 us
    pallas_call x1, Pallas kernels, local(): pl.pallas_call(functools.partial(cell_sums, group, capacity), grid=(n //...  6.48 us
    pallas_call x1, Pallas kernels, local(): pl.pallas_call(functools.partial(finish, bands), grid=(bands // each,), i...  4.75 us
    pallas_call x1, Pallas kernels, local(): pl.pallas_call(functools.partial(near_maps, n, fold), grid=(pairs // fold...  4.63 us
    convert_element_type x3, other arithmetic, local(): got.append(exchange((a + b.astype(F32)).astype(BF16), k, n))  3.18 us
    ppermute x1, starting transfers between devices, local(): other = lax.ppermute(ms_map, 'mcol', [(0, 1), (1, 0)])  3 us
  transfers between devices with their start and end apart: 13, of which 5 were waited for; matrix products, arithmetic and copies ran while one was open for 6% of the time, Pallas kernels for 21%

profile of v2, /device:TPU:1, one launch (start us, length us, event | category | flops | bytes accessed | tf_op | source)
XLA Modules:
  0.0 63.2 jit_solution(15486531610120974104)
XLA Ops:
  0.0 0.1 collective-permute-start
  0.1 1.2 %collective-permute-done = f32[1,8]{1,0:T(1,128)S(1)} collective-permute-done((f32[1,8]{1,0:T(1,128)}, f32[1,8]{1,0:T(1,128)S(1)}, u32[]{:S(2)}, u32[]{:S(2)}) %collective-permute-start) | collective-permute-done | bytes 64 | tf_op jit(solution)/shard_map/ppermute | solution.py:342
  1.3 0.7 %pad_maximum_fusion.1 = f32[1,19]{1,0:T(1,128)S(1)} fusion(f32[1,8]{1,0:T(1,128)S(1)} %collective-permute-done, f32[1,8]{1,0:T(1,128)} %param.13, f32[1,3]{1,0:T(1,128)} %bitcast.9), kind=kLoop, calls=%fused_computation.6 | loop fusion | flops 38 | bytes 152 | tf_op jit(solution)/shard_map/concatenate | solution.py:343
  2.0 2.4 %collective-permute-start.1 = (f32[1,19]{1,0:T(1,128)S(1)}, f32[1,19]{1,0:T(1,128)S(1)}, u32[]{:S(2)}, u32[]{:S(2)}) collective-permute-start(f32[1,19]{1,0:T(1,128)S(1)} %pad_maximum_fusion.1), channel_id=1, source_target_pairs={{0,2},{2,0},{4,6},{6,4},{8,10},{10,8},{12,14},{14,12},{1,3},{3,1},... | collective-permute-start | bytes 236 | tf_op jit(solution)/shard_map/ppermute | solution.py:320
  4.4 0.6 %pad_add_fusion.who = s32[2]{0:T(128)} fusion(s32[1]{0:T(128)} %bitcast.1, s32[1]{0:T(128)} %bitcast), kind=kLoop, calls=%fused_computation.5 | loop fusion | flops 2 | bytes 16 | tf_op jit(solution)/shard_map/stack | solution.py:340
  5.1 0.3 collective-permute-done.1
  5.4 0.7 %pad_maximum_fusion = f32[2,19]{1,0:T(2,128)S(1)} fusion(f32[1,19]{1,0:T(1,128)S(1)} %collective-permute-done.1, f32[1,8]{1,0:T(1,128)S(1)} %collective-permute-done, f32[1,8]{1,0:T(1,128)} %param.13, f32[1,3]{1,0:T(1,128)} %bitcast.10), kind=kLoop, calls=%fused_computation.4 | loop fusion | flops 114 | bytes 304 | tf_op jit(solution)/shard_map/concatenate | solution.py:344
  6.1 1.5 %collective-permute-start.2 = (f32[2,19]{1,0:T(2,128)S(1)}, f32[2,19]{1,0:T(2,128)S(1)}, u32[]{:S(2)}, u32[]{:S(2)}) collective-permute-start(f32[2,19]{1,0:T(2,128)S(1)} %pad_maximum_fusion), channel_id=1, source_target_pairs={{0,4},{2,6},{4,0},{6,2},{8,12},{10,14},{12,8},{14,10},{1,5},{3,7},... | collective-permute-start | bytes 464 | tf_op jit(solution)/shard_map/ppermute | solution.py:320
  7.6 2.3 %collective-permute-start.3 = (f32[2,19]{1,0:T(2,128)S(1)}, f32[2,19]{1,0:T(2,128)S(1)}, u32[]{:S(2)}, u32[]{:S(2)}) collective-permute-start(f32[2,19]{1,0:T(2,128)S(1)} %pad_maximum_fusion), channel_id=1, source_target_pairs={{0,8},{2,10},{4,12},{6,14},{8,0},{10,2},{12,4},{14,6},{1,9},{3,11}... | collective-permute-start | bytes 464 | tf_op jit(solution)/shard_map/ppermute | solution.py:320
  10.0 0.0 collective-permute-start.4
  10.0 6.5 %cell_sums.1 = (bf16[40,256,128]{2,1,0:T(8,128)(2,1)}, bf16[40,64,256]{2,1,0:T(8,128)(2,1)}) custom-call(s32[2]{0:T(128)} %pad_add_fusion.who, s32[3,64]{1,0:T(4,128)} %list_ref.1, bf16[64,128,128]{2,1,0:T(8,128)(2,1)} %pan_ref.1, bf16[64,32,256]{2,1,0:T(8,128)(2,1)} %ms_ref.1), custom_call_target="tpu_custom_call" | custom-call | tf_op jit(solution)/shard_map/cell_sums/pallas_call | solution.py:348
  16.4 0.0 collective-permute-done.2
  16.4 0.0 collective-permute-done.3
  16.4 0.0 collective-permute-done.4
  16.5 0.6 concatenate.12.grids
  17.1 6.6 %far_maps.1 = (bf16[208,512]{1,0:T(8,128)(2,1)}, bf16[208,512]{1,0:T(8,128)(2,1)}, bf16[208,512]{1,0:T(8,128)(2,1)}, bf16[208,512]{1,0:T(8,128)(2,1)}, bf16[4,80,512]{2,1,0:T(8,128)(2,1)}) custom-call(s32[2]{0:T(128)} %pad_add_fusion.who, f32[8,19]{1,0:T(8,128)} %concatenate.12.grids, bf16[8,5,64,256]{3,2,1,0:T(8,128)(2,1)} %bitcast.8, ...), custom_call_target="tpu_custom_call" | custom-call | tf_op jit(solution)/shard_map/far_maps/pallas_call | solution.py:376
  23.6 1.2 %collective-permute-start.6 = (bf16[208,512]{1,0:T(8,128)(2,1)}, bf16[208,512]{1,0:T(8,128)(2,1)S(1)}, u32[]{:S(2)}, u32[]{:S(2)}) collective-permute-start(bf16[208,512]{1,0:T(8,128)(2,1)} %get-tuple-element.26), channel_id=1, source_target_pairs={{0,2},{2,0},{4,6},{6,4},{8,10},{10,8},{12,14},{14,12},{1,3},{3,1},... | collective-permute-start | bytes 638984 | tf_op jit(solution)/shard_map/ppermute | solution.py:320
  24.9 0.0 copy-start.8
  24.9 0.0 copy-start.7
  24.9 0.0 copy-start.6
  24.9 4.6 %near_maps.1 = (f32[208,512]{1,0:T(8,128)}, f32[208,512]{1,0:T(8,128)}, f32[208,512]{1,0:T(8,128)}, f32[208,512]{1,0:T(8,128)}) custom-call(s32[2]{0:T(128)} %pad_add_fusion.who, f32[8,19]{1,0:T(8,128)} %concatenate.12.grids, bf16[4,80,512]{2,1,0:T(8,128)(2,1)} %get-tuple-element.22.ms, bf16[8,5,256,128]{3,2,1,0:T(8,128)(2,1)} %bitcast.6, ...), custom_call_target="tpu_custom_call" | custom-call | tf_op jit(solution)/shard_map/near_maps/pallas_call | solution.py:396
  29.5 0.0 copy-done.8
  29.5 0.2 collective-permute-start.8
  29.8 0.0 copy-done.7
  29.8 1.2 %collective-permute-start.10 = (bf16[208,512]{1,0:T(8,128)(2,1)S(1)}, bf16[208,512]{1,0:T(8,128)(2,1)S(1)}, u32[]{:S(2)}, u32[]{:S(2)}) collective-permute-start(bf16[208,512]{1,0:T(8,128)(2,1)S(1)} %copy-done.7), channel_id=1, source_target_pairs={{0,2},{2,0},{4,6},{6,4},{8,10},{10,8},{12,14},{14,12},{1,3},{3,1},... | collective-permute-start | bytes 638984 | tf_op jit(solution)/shard_map/ppermute | solution.py:320
  31.0 0.0 copy-done.6
  31.0 0.2 collective-permute-start.5
  31.2 0.0 collective-permute-done.6
  31.2 1.1 %add_convert_fusion.2 = bf16[208,512]{1,0:T(8,128)(2,1)S(1)} fusion(f32[208,512]{1,0:T(8,128)} %get-tuple-element.25, bf16[208,512]{1,0:T(8,128)(2,1)S(1)} %collective-permute-done.6), kind=kLoop, calls=%fused_computation.2 | loop fusion | flops 319488 | bytes 851968 | tf_op jit(solution)/shard_map/convert_element_type | solution.py:432
  32.3 3.3 %collective-permute-start.7 = (bf16[208,512]{1,0:T(8,128)(2,1)S(1)}, bf16[208,512]{1,0:T(8,128)(2,1)S(1)}, u32[]{:S(2)}, u32[]{:S(2)}) collective-permute-start(bf16[208,512]{1,0:T(8,128)(2,1)S(1)} %add_convert_fusion.2), channel_id=1, source_target_pairs={{0,12},{2,14},{4,8},{6,10},{8,4},{10,6},{12,0},{14,2},{1,13},{3,15... | collective-permute-start | bytes 638984 | tf_op jit(solution)/shard_map/ppermute | solution.py:320
  35.6 0.0 collective-permute-done.8
  35.6 1.1 %add_convert_fusion.1 = bf16[208,512]{1,0:T(8,128)(2,1)S(1)} fusion(f32[208,512]{1,0:T(8,128)} %get-tuple-element.27, bf16[208,512]{1,0:T(8,128)(2,1)S(1)} %collective-permute-done.8), kind=kLoop, calls=%fused_computation.1 | loop fusion | flops 319488 | bytes 851968 | tf_op jit(solution)/shard_map/convert_element_type | solution.py:432
  36.7 0.1 collective-permute-start.9
  36.8 1.6 %collective-permute-done.10 = bf16[208,512]{1,0:T(8,128)(2,1)S(1)} collective-permute-done((bf16[208,512]{1,0:T(8,128)(2,1)S(1)}, bf16[208,512]{1,0:T(8,128)(2,1)S(1)}, u32[]{:S(2)}, u32[]{:S(2)}) %collective-permute-start.10) | collective-permute-done | bytes 213024 | tf_op jit(solution)/shard_map/ppermute | solution.py:320
  38.3 1.1 %add_convert_fusion = bf16[208,512]{1,0:T(8,128)(2,1)S(1)} fusion(f32[208,512]{1,0:T(8,128)} %get-tuple-element.29, bf16[208,512]{1,0:T(8,128)(2,1)S(1)} %collective-permute-done.10), kind=kLoop, calls=%fused_computation | loop fusion | flops 319488 | bytes 851968 | tf_op jit(solution)/shard_map/convert_element_type | solution.py:432
  39.4 0.6 %collective-permute-start.11 = (bf16[208,512]{1,0:T(8,128)(2,1)S(1)}, bf16[208,512]{1,0:T(8,128)(2,1)S(1)}, u32[]{:S(2)}, u32[]{:S(2)}) collective-permute-start(bf16[208,512]{1,0:T(8,128)(2,1)S(1)} %add_convert_fusion), channel_id=1, source_target_pairs={{0,4},{2,6},{4,0},{6,2},{8,12},{10,14},{12,8},{14,10},{1,5},{3,7},... | collective-permute-start | bytes 638984 | tf_op jit(solution)/shard_map/ppermute | solution.py:320
  40.0 2.9 %collective-permute-done.5.refs_1_ = bf16[208,512]{1,0:T(8,128)(2,1)S(1)} collective-permute-done((bf16[208,512]{1,0:T(8,128)(2,1)S(1)}, bf16[208,512]{1,0:T(8,128)(2,1)S(1)}, u32[]{:S(2)}, u32[]{:S(2)}) %collective-permute-start.5) | collective-permute-done | bytes 213024 | tf_op jit(solution)/shard_map/ppermute | solution.py:320
  42.9 0.0 copy-start
  42.9 0.0 collective-permute-done.7.refs_2_
  42.9 0.0 copy-start.1
  42.9 8.5 %collective-permute-done.9.refs_3_ = bf16[208,512]{1,0:T(8,128)(2,1)S(1)} collective-permute-done((bf16[208,512]{1,0:T(8,128)(2,1)S(1)}, bf16[208,512]{1,0:T(8,128)(2,1)S(1)}, u32[]{:S(2)}, u32[]{:S(2)}) %collective-permute-start.9) | collective-permute-done | bytes 213024 | tf_op jit(solution)/shard_map/ppermute | solution.py:320
  51.4 0.0 copy-start.2
  51.4 0.0 collective-permute-done.11.refs_4_
  51.5 0.0 copy-start.3
  51.5 1.1 %add_convert_fusion.3.ms_ref = bf16[80,512]{1,0:T(8,128)(2,1)S(1)} fusion(f32[208,512]{1,0:T(8,128)} %get-tuple-element.23.refs_0_, bf16[208,512]{1,0:T(8,128)(2,1)S(1)} %collective-permute-done.11.refs_4_, bf16[208,512]{1,0:T(8,128)(2,1)S(1)} %collective-permute-done.9.refs_3_, bf16[208,512]{1,0:T(8,128)(2,1)S(1)} %collective-permute-done.7.refs_2_, ...), kind=kLoop, calls=%fused_computation.3 | loop fusion | flops 368640 | bytes 573440 | tf_op jit(solution)/shard_map/convert_element_type | solution.py:433
  52.6 0.0 copy-start.4
  52.6 3.0 %collective-permute-start.12 = (bf16[80,512]{1,0:T(8,128)(2,1)S(1)}, bf16[80,512]{1,0:T(8,128)(2,1)S(1)}, u32[]{:S(2)}, u32[]{:S(2)}) collective-permute-start(bf16[80,512]{1,0:T(8,128)(2,1)S(1)} %add_convert_fusion.3.ms_ref), channel_id=1, source_target_pairs={{0,1},{1,0},{2,3},{3,2},{4,5},{5,4},{6,7},{7,6},{8,9},{9,8},{10,11... | collective-permute-start | bytes 245768 | tf_op jit(solution)/shard_map/ppermute | solution.py:434
  55.6 2.3 %tables.1 = (bf16[8,128,384]{2,1,0:T(8,128)(2,1)}, bf16[256,512]{1,0:T(8,128)(2,1)}) custom-call(s32[2]{0:T(128)} %pad_add_fusion.who, f32[8,8]{1,0:T(8,128)} %mix.1, f32[8]{0:T(128)} %gain.3, f32[8]{0:T(128)} %synth.1), custom_call_target="tpu_custom_call" | custom-call | tf_op jit(solution)/shard_map/tables/pallas_call | solution.py:418
  57.8 0.0 collective-permute-done.12.other_ref
  57.9 0.0 copy-start.5
  57.9 0.0 copy-done
  57.9 0.0 copy-done.1
  57.9 0.0 copy-done.2
  57.9 0.0 copy-done.3
  57.9 0.0 copy-done.4
  57.9 0.6 copy-done.5
  58.5 4.7 %finish.1 = bf16[8,128,512]{2,1,0:T(8,128)(2,1)} custom-call(f32[8]{0:T(128)} %gain.3, bf16[8,128,384]{2,1,0:T(8,128)(2,1)} %get-tuple-element.18.up_ref, bf16[256,512]{1,0:T(8,128)(2,1)} %get-tuple-element.19.cols_ref, bf16[80,512]{1,0:T(8,128)(2,1)} %copy-done.4, bf16[80,512]{1,0:T(8,128)(2,1)} %copy-done.5, f32[208,512]{1,0:T(8,128)} %get-tuple-element.23.refs_0_, ...), custom_call_target="tpu_custom_call" | custom-call | tf_op jit(solution)/shard_map/finish/pallas_call | solution.py:437
Async XLA Ops:
  0.0 1.3 %collective-permute-start = (f32[1,8]{1,0:T(1,128)}, f32[1,8]{1,0:T(1,128)S(1)}, u32[]{:S(2)}, u32[]{:S(2)}) collective-permute-start(f32[1,8]{1,0:T(1,128)} %param.13), channel_id=1, source_target_pairs={{0,1},{1,0},{2,3},{3,2},{4,5},{5,4},{6,7},{7,6},{8,9},{9,8},{10,11... | collective-permute-start | bytes 104 | tf_op jit(solution)/shard_map/ppermute | solution.py:342
  2.0 3.4 %collective-permute-start.1 = (f32[1,19]{1,0:T(1,128)S(1)}, f32[1,19]{1,0:T(1,128)S(1)}, u32[]{:S(2)}, u32[]{:S(2)}) collective-permute-start(f32[1,19]{1,0:T(1,128)S(1)} %pad_maximum_fusion.1), channel_id=1, source_target_pairs={{0,2},{2,0},{4,6},{6,4},{8,10},{10,8},{12,14},{14,12},{1,3},{3,1},... | collective-permute-start | bytes 236 | tf_op jit(solution)/shard_map/ppermute | solution.py:320
  6.1 10.3 %collective-permute-start.2 = (f32[2,19]{1,0:T(2,128)S(1)}, f32[2,19]{1,0:T(2,128)S(1)}, u32[]{:S(2)}, u32[]{:S(2)}) collective-permute-start(f32[2,19]{1,0:T(2,128)S(1)} %pad_maximum_fusion), channel_id=1, source_target_pairs={{0,4},{2,6},{4,0},{6,2},{8,12},{10,14},{12,8},{14,10},{1,5},{3,7},... | collective-permute-start | bytes 464 | tf_op jit(solution)/shard_map/ppermute | solution.py:320
  7.6 8.8 %collective-permute-start.3 = (f32[2,19]{1,0:T(2,128)S(1)}, f32[2,19]{1,0:T(2,128)S(1)}, u32[]{:S(2)}, u32[]{:S(2)}) collective-permute-start(f32[2,19]{1,0:T(2,128)S(1)} %pad_maximum_fusion), channel_id=1, source_target_pairs={{0,8},{2,10},{4,12},{6,14},{8,0},{10,2},{12,4},{14,6},{1,9},{3,11}... | collective-permute-start | bytes 464 | tf_op jit(solution)/shard_map/ppermute | solution.py:320
  10.0 6.5 %collective-permute-start.4 = (f32[2,19]{1,0:T(2,128)S(1)}, f32[2,19]{1,0:T(2,128)S(1)}, u32[]{:S(2)}, u32[]{:S(2)}) collective-permute-start(f32[2,19]{1,0:T(2,128)S(1)} %pad_maximum_fusion), channel_id=1, source_target_pairs={{0,12},{2,14},{4,8},{6,10},{8,4},{10,6},{12,0},{14,2},{1,13},{3,15... | collective-permute-start | bytes 464 | tf_op jit(solution)/shard_map/ppermute | solution.py:320
  23.6 7.6 %collective-permute-start.6 = (bf16[208,512]{1,0:T(8,128)(2,1)}, bf16[208,512]{1,0:T(8,128)(2,1)S(1)}, u32[]{:S(2)}, u32[]{:S(2)}) collective-permute-start(bf16[208,512]{1,0:T(8,128)(2,1)} %get-tuple-element.26), channel_id=1, source_target_pairs={{0,2},{2,0},{4,6},{6,4},{8,10},{10,8},{12,14},{14,12},{1,3},{3,1},... | collective-permute-start | bytes 638984 | tf_op jit(solution)/shard_map/ppermute | solution.py:320
  24.9 4.6 %copy-start.8 = (bf16[208,512]{1,0:T(8,128)(2,1)S(1)}, bf16[208,512]{1,0:T(8,128)(2,1)}, u32[]{:S(2)}) copy-start(bf16[208,512]{1,0:T(8,128)(2,1)} %get-tuple-element.28) | copy-start | bytes 638980
  24.9 4.9 %copy-start.7 = (bf16[208,512]{1,0:T(8,128)(2,1)S(1)}, bf16[208,512]{1,0:T(8,128)(2,1)}, u32[]{:S(2)}) copy-start(bf16[208,512]{1,0:T(8,128)(2,1)} %get-tuple-element.30) | copy-start | bytes 638980
  24.9 6.1 %copy-start.6 = (bf16[208,512]{1,0:T(8,128)(2,1)S(1)}, bf16[208,512]{1,0:T(8,128)(2,1)}, u32[]{:S(2)}) copy-start(bf16[208,512]{1,0:T(8,128)(2,1)} %get-tuple-element.24) | copy-start | bytes 638980
  29.5 6.1 %collective-permute-start.8 = (bf16[208,512]{1,0:T(8,128)(2,1)S(1)}, bf16[208,512]{1,0:T(8,128)(2,1)S(1)}, u32[]{:S(2)}, u32[]{:S(2)}) collective-permute-start(bf16[208,512]{1,0:T(8,128)(2,1)S(1)} %copy-done.8), channel_id=1, source_target_pairs={{0,2},{2,0},{4,6},{6,4},{8,10},{10,8},{12,14},{14,12},{1,3},{3,1},... | collective-permute-start | bytes 638984 | tf_op jit(solution)/shard_map/ppermute | solution.py:320
  29.8 8.6 %collective-permute-start.10 = (bf16[208,512]{1,0:T(8,128)(2,1)S(1)}, bf16[208,512]{1,0:T(8,128)(2,1)S(1)}, u32[]{:S(2)}, u32[]{:S(2)}) collective-permute-start(bf16[208,512]{1,0:T(8,128)(2,1)S(1)} %copy-done.7), channel_id=1, source_target_pairs={{0,2},{2,0},{4,6},{6,4},{8,10},{10,8},{12,14},{14,12},{1,3},{3,1},... | collective-permute-start | bytes 638984 | tf_op jit(solution)/shard_map/ppermute | solution.py:320
  31.0 11.9 %collective-permute-start.5 = (bf16[208,512]{1,0:T(8,128)(2,1)S(1)}, bf16[208,512]{1,0:T(8,128)(2,1)S(1)}, u32[]{:S(2)}, u32[]{:S(2)}) collective-permute-start(bf16[208,512]{1,0:T(8,128)(2,1)S(1)} %copy-done.6), channel_id=1, source_target_pairs={{0,2},{2,0},{4,6},{6,4},{8,10},{10,8},{12,14},{14,12},{1,3},{3,1},... | collective-permute-start | bytes 638984 | tf_op jit(solution)/shard_map/ppermute | solution.py:320
  32.3 10.6 %collective-permute-start.7 = (bf16[208,512]{1,0:T(8,128)(2,1)S(1)}, bf16[208,512]{1,0:T(8,128)(2,1)S(1)}, u32[]{:S(2)}, u32[]{:S(2)}) collective-permute-start(bf16[208,512]{1,0:T(8,128)(2,1)S(1)} %add_convert_fusion.2), channel_id=1, source_target_pairs={{0,12},{2,14},{4,8},{6,10},{8,4},{10,6},{12,0},{14,2},{1,13},{3,15... | collective-permute-start | bytes 638984 | tf_op jit(solution)/shard_map/ppermute | solution.py:320
  36.7 14.8 %collective-permute-start.9 = (bf16[208,512]{1,0:T(8,128)(2,1)S(1)}, bf16[208,512]{1,0:T(8,128)(2,1)S(1)}, u32[]{:S(2)}, u32[]{:S(2)}) collective-permute-start(bf16[208,512]{1,0:T(8,128)(2,1)S(1)} %add_convert_fusion.1), channel_id=1, source_target_pairs={{0,8},{2,10},{4,12},{6,14},{8,0},{10,2},{12,4},{14,6},{1,9},{3,11}... | collective-permute-start | bytes 638984 | tf_op jit(solution)/shard_map/ppermute | solution.py:320
  39.4 12.1 %collective-permute-start.11 = (bf16[208,512]{1,0:T(8,128)(2,1)S(1)}, bf16[208,512]{1,0:T(8,128)(2,1)S(1)}, u32[]{:S(2)}, u32[]{:S(2)}) collective-permute-start(bf16[208,512]{1,0:T(8,128)(2,1)S(1)} %add_convert_fusion), channel_id=1, source_target_pairs={{0,4},{2,6},{4,0},{6,2},{8,12},{10,14},{12,8},{14,10},{1,5},{3,7},... | collective-permute-start | bytes 638984 | tf_op jit(solution)/shard_map/ppermute | solution.py:320
  42.9 15.0 %copy-start = (bf16[208,512]{1,0:T(8,128)(2,1)}, bf16[208,512]{1,0:T(8,128)(2,1)S(1)}, u32[]{:S(2)}) copy-start(bf16[208,512]{1,0:T(8,128)(2,1)S(1)} %collective-permute-done.5.refs_1_) | copy-start | bytes 638980
  42.9 15.0 %copy-start.1 = (bf16[208,512]{1,0:T(8,128)(2,1)}, bf16[208,512]{1,0:T(8,128)(2,1)S(1)}, u32[]{:S(2)}) copy-start(bf16[208,512]{1,0:T(8,128)(2,1)S(1)} %collective-permute-done.7.refs_2_) | copy-start | bytes 638980
  51.4 6.4 %copy-start.2 = (bf16[208,512]{1,0:T(8,128)(2,1)}, bf16[208,512]{1,0:T(8,128)(2,1)S(1)}, u32[]{:S(2)}) copy-start(bf16[208,512]{1,0:T(8,128)(2,1)S(1)} %collective-permute-done.9.refs_3_) | copy-start | bytes 638980
  51.5 6.4 %copy-start.3 = (bf16[208,512]{1,0:T(8,128)(2,1)}, bf16[208,512]{1,0:T(8,128)(2,1)S(1)}, u32[]{:S(2)}) copy-start(bf16[208,512]{1,0:T(8,128)(2,1)S(1)} %collective-permute-done.11.refs_4_) | copy-start | bytes 638980
  52.6 5.3 %copy-start.4 = (bf16[80,512]{1,0:T(8,128)(2,1)}, bf16[80,512]{1,0:T(8,128)(2,1)S(1)}, u32[]{:S(2)}) copy-start(bf16[80,512]{1,0:T(8,128)(2,1)S(1)} %add_convert_fusion.3.ms_ref) | copy-start | bytes 245764
  52.6 5.3 %collective-permute-start.12 = (bf16[80,512]{1,0:T(8,128)(2,1)S(1)}, bf16[80,512]{1,0:T(8,128)(2,1)S(1)}, u32[]{:S(2)}, u32[]{:S(2)}) collective-permute-start(bf16[80,512]{1,0:T(8,128)(2,1)S(1)} %add_convert_fusion.3.ms_ref), channel_id=1, source_target_pairs={{0,1},{1,0},{2,3},{3,2},{4,5},{5,4},{6,7},{7,6},{8,9},{9,8},{10,11... | collective-permute-start | bytes 245768 | tf_op jit(solution)/shard_map/ppermute | solution.py:434
  57.9 0.6 copy-start.5

commit v3 on v2

--- a/solution.py
+++ b/solution.py
@@ -15,11 +15,11 @@
 
 F32 = jnp.float32
 BF16 = jnp.bfloat16
-VMEM_LIMIT = 56 * 1024 * 1024
-
-
-def params():
-    return pltpu.CompilerParams(vmem_limit_bytes=VMEM_LIMIT)
+MIB = 1024 * 1024
+
+
+def params(mib):
+    return pltpu.CompilerParams(vmem_limit_bytes=mib * MIB)
 
 
 def whole(memory_space=pltpu.VMEM):
@@ -53,31 +53,6 @@
     return left + (right - left) * within
 
 
-def cell_sums(group, capacity, who, list_ref, pan_ref, ms_ref, pan_out, ms_out, pan_acc, ms_acc):
-    first = pl.program_id(0) * group
-    block, coarse = pan_ref.shape[1], ms_ref.shape[1]
-    pan_acc[...] = jnp.zeros_like(pan_acc)
-    ms_acc[...] = jnp.zeros_like(ms_acc)
-
-    def add(j, carry):
-        place = ((list_ref[0, j] // capacity) ^ who[0]) - first
-        row, col = list_ref[1, j], list_ref[2, j]
-        cell = place * KC + lax.rem(col, KC)
-
-        @pl.when((place >= 0) & (place < group))
-        def _():
-            rows = pl.ds(pl.multiple_of(row * block, block), block)
-            pan_acc[cell, rows, :] += pan_ref[j].astype(F32)
-            rows = pl.ds(pl.multiple_of(row * coarse, coarse), coarse)
-            ms_acc[cell, rows, :] += ms_ref[j].astype(F32)
-
-        return carry
-
-    lax.fori_loop(0, pan_ref.shape[0], add, 0)
-    pan_out[...] = pan_acc[...].astype(BF16)
-    ms_out[...] = ms_acc[...].astype(BF16)
-
-
 def repeat_rows(x):
     return jnp.concatenate([x, x], axis=0)
 
@@ -123,7 +98,7 @@
 
 
 def ms_piece(bands, c, g, grids, cells, spread):
-    coarse = cells.shape[1] // KR
+    coarse = cells[0].shape[0] // KR
     half = 128 // coarse
     halves = bands // half
     crows, ccols = TR // 4, TC // 4
@@ -169,7 +144,7 @@
 
 
 def pan_piece(c, g, grids, cells, table):
-    block = cells.shape[1] // KR
+    block = cells[0].shape[0] // KR
     position = iota((TR, 128), 0)
     y = along(row_nodes(grids, g), position // GRID, position, 0.0, 0, TR // GRID, TR // GRID - 1)
     lane = iota((TR, 128), 1)
@@ -194,72 +169,96 @@
     return jnp.dot(held, table[...], preferred_element_type=F32)
 
 
-def far_maps(n, bands, who, grids, ms_cells, pan_cells, *refs):
-    pairs = n // 2
-    outs, near = refs[:pairs], refs[pairs]
-    spread, (table, edge) = refs[pairs + 1 : pairs + 3], refs[pairs + 3 :]
-    step = pl.program_id(0)
-    me, c = who[0], who[1]
+def cell_sums(capacity, who, list_ref, pan_hbm, ms_hbm, pan_out, ms_out, *rest):
+    pan_acc, ms_acc, pan_ref, ms_ref, sems = rest
+    block, coarse = pan_ref.shape[1], ms_ref.shape[1]
+    parts = sems.shape[0]
+    each = pan_ref.shape[0] // parts
+    copies = []
+    for i in range(parts):
+        at = pl.ds(i * each, each)
+        copies.append(pltpu.make_async_copy(pan_hbm.at[at], pan_ref.at[at], sems.at[i, 0]))
+        copies.append(pltpu.make_async_copy(ms_hbm.at[at], ms_ref.at[at], sems.at[i, 1]))
+    for copy in copies:
+        copy.start()
+    pan_acc[...] = jnp.zeros_like(pan_acc)
+    ms_acc[...] = jnp.zeros_like(ms_acc)
+
+    def add(j, carry):
+        place = (list_ref[0, j] // capacity) ^ who[0]
+        row, col = list_ref[1, j], list_ref[2, j]
+        cell = place * KC + lax.rem(col, KC)
+        rows = pl.ds(pl.multiple_of(row * block, block), block)
+        pan_acc[cell, rows, :] += pan_ref[j].astype(F32)
+        rows = pl.ds(pl.multiple_of(row * coarse, coarse), coarse)
+        ms_acc[cell, rows, :] += ms_ref[j].astype(F32)
+        return carry
+
+    for i in range(parts):
+        copies[2 * i].wait()
+        copies[2 * i + 1].wait()
+        lax.fori_loop(i * each, (i + 1) * each, add, 0)
+    pan_out[...] = pan_acc[...].astype(BF16)
+    ms_out[...] = ms_acc[...].astype(BF16)
+
+
+def halo_rows(above, below):
+    mine = (iota(above.shape, 0) & 2) == 0
+    value = jnp.where(mine, above, below)
+    return jnp.concatenate([value, jnp.zeros_like(value)], axis=0).astype(BF16)
+
+
+def ms_parts_of(ms_map):
     crows = TR // 4
     tall = crows + 8
-    group = (8, TC)
-    upper = iota(group, 0) < 4
-    base = TR + 2 * crows
-
-    @pl.when(step == 0)
-    def _():
-        for ref in spread:
-            ref[...] = jnp.zeros_like(ref)
-
-    mains = []
-    for u in range(2):
-        g = 2 * step + u
-        ms_map = ms_piece(bands, c, g, grids, ms_cells[u], spread[u])
-        main = jnp.concatenate([ms_map[0:crows], ms_map[tall : tall + crows]], axis=0)
-        mains.append(main.astype(BF16))
-        edge[(me ^ g) + 1] = jnp.where(upper, ms_map[crows:tall], ms_map[tall + crows : 2 * tall])
-    pan_map = pan_piece(c, n - 1 - 2 * step, grids, pan_cells[0], table).astype(BF16)
-    near[pairs - 1 - step, 0 : 2 * crows, :] = mains[0]
-    for k in range(pairs):
-
-        @pl.when(step == k)
-        def _(k=k):
-            outs[k][0:TR, :] = pan_map
-            outs[pairs - 1 - k][TR:base, :] = mains[1]
-
-    @pl.when(step == pairs - 1)
-    def _():
-        edge[0] = jnp.zeros(group, F32)
-        edge[n + 1] = jnp.zeros(group, F32)
-        mine = (iota(group, 0) & 2) == 0
-
-        def halo(g):
-            dest = me ^ g
-            value = jnp.where(mine, edge[dest], edge[dest + 2])
-            return jnp.concatenate([value, jnp.zeros_like(value)], axis=0).astype(BF16)
-
-        for k in range(pairs):
-            outs[k][base:, :] = halo(n - 1 - 2 * k)
-            near[k, 2 * crows :, :] = halo(n - 2 - 2 * k)
-
-
-def near_maps(n, fold, who, grids, ms, *refs):
-    pairs = n // 2
-    cells, outs, table = refs[:fold], refs[fold : fold + pairs], refs[fold + pairs :]
-    step = pl.program_id(0)
-    for u in range(fold):
-        g = n - 2 - 2 * (fold * step + u)
-        pan_map = pan_piece(who[1], g, grids, cells[u][0], table[u])
-        ms_map = ms[u].astype(F32)
-        for k in range(u, pairs, fold):
-
-            @pl.when(fold * step + u == k)
-            def _(k=k):
-                outs[k][0:TR, :] = pan_map
-                outs[k][TR:, :] = ms_map
-
-
-def tables(bands, who, mix, gain, synth, up_out, cols_out):
+    main = jnp.concatenate([ms_map[0:crows], ms_map[tall : tall + crows]], axis=0).astype(BF16)
+    upper = iota((8, ms_map.shape[1]), 0) < 4
+    return main, jnp.where(upper, ms_map[crows:tall], ms_map[tall + crows : 2 * tall])
+
+
+def group_maps(n, bands, first, count, who, grids, cells_hbm, ms_hbm, *refs):
+    scratch = refs[-7:]
+    outs = refs[-7 - count : -7]
+    spread, table, main, edge, cells, ms, sems = scratch
+    me, c = who[0], who[1]
+    low = (me ^ first) & -count
+    around = [low + i for i in range(count)]
+    around += [jnp.maximum(low - 1, 0), jnp.minimum(low + count, n - 1)]
+    copies = [
+        pltpu.make_async_copy(ms_hbm.at[pl.ds((t ^ me) * KC, KC)], ms.at[i], sems.at[i])
+        for i, t in enumerate(around)
+    ]
+    copies.append(
+        pltpu.make_async_copy(cells_hbm.at[pl.ds(first * KC, count * KC)], cells, sems.at[count + 2])
+    )
+    for copy in copies:
+        copy.start()
+    for ref in spread:
+        ref[...] = jnp.zeros_like(ref)
+    for copy in copies:
+        copy.wait()
+    for i, t in enumerate(around):
+        held = [ms[i, j] for j in range(KC)]
+        own, ends = ms_parts_of(ms_piece(bands, c, t ^ me, grids, held, spread[i % len(spread)]))
+        if i < count:
+            main[i] = own
+            edge[i + 1] = ends
+        elif i == count:
+            edge[0] = jnp.where(low > 0, ends, jnp.zeros_like(ends))
+        else:
+            edge[count + 1] = jnp.where(low + count < n, ends, jnp.zeros_like(ends))
+    base = TR + main.shape[1]
+    for u in range(count):
+        g = first + count - 1 - u
+        held = [cells[(g - first) * KC + j] for j in range(KC)]
+        out = outs[u]
+        at = (me ^ g) - low
+        out[0:TR, :] = pan_piece(c, g, grids, held, table[u]).astype(out.dtype)
+        out[TR:base, :] = main[at].astype(out.dtype)
+        out[base:, :] = halo_rows(edge[at], edge[at + 2]).astype(out.dtype)
+
+
+def tables(bands, who, mix, gain, synth, after, up_out, cols_out):
     c = who[1]
     crows, ccols = TR // 4, TC // 4
     half = bands // 2
@@ -311,9 +310,11 @@
         pan[...] = total
 
     count = up_ref.shape[0]
+    table = jnp.concatenate([up_ref[u] for u in range(count)], axis=0)
+    value = jnp.dot(table, across[...], preferred_element_type=F32)
     for u in range(count):
-        value = jnp.dot(up_ref[u], across[...], preferred_element_type=F32)
-        out[u] = (value + gain[count * step + u] * pan[...]).astype(BF16)
+        band = value[u * TR : (u + 1) * TR]
+        out[u] = (band + gain[count * step + u] * pan[...]).astype(BF16)
 
 
 def exchange(x, step, count):
@@ -344,93 +345,101 @@
     pair = jnp.concatenate([mine, exchange(mine, 1, n)], axis=0)
     grids = jnp.concatenate([pair] + [exchange(pair, k, n) for k in range(2, n, 2)], axis=0)
 
-    group = min(n, 8)
-    pan_cells, ms_cells = pl.pallas_call(
-        functools.partial(cell_sums, group, capacity),
-        grid=(n // group,),
-        in_specs=[whole(pltpu.SMEM), whole(pltpu.SMEM), whole(), whole()],
-        out_specs=[
-            pl.BlockSpec((group * KC, KR * block, block), lambda i: (i, 0, 0)),
-            pl.BlockSpec((group * KC, KR * coarse, bands * coarse), lambda i: (i, 0, 0)),
-        ],
+    tall = 2 * (TR // 4) + 16
+    height = TR + tall
+    parts = 4
+    hbm = pl.BlockSpec(memory_space=pltpu.HBM)
+    cells, ms_cells = pl.pallas_call(
+        functools.partial(cell_sums, capacity),
+        in_specs=[whole(pltpu.SMEM)] * 2 + [hbm, hbm],
+        out_specs=[whole()] * 2,
         out_shape=[
             jax.ShapeDtypeStruct((n * KC, KR * block, block), BF16),
             jax.ShapeDtypeStruct((n * KC, KR * coarse, bands * coarse), BF16),
         ],
         scratch_shapes=[
-            pltpu.VMEM((group * KC, KR * block, block), F32),
-            pltpu.VMEM((group * KC, KR * coarse, bands * coarse), F32),
+            pltpu.VMEM((n * KC, KR * block, block), F32),
+            pltpu.VMEM((n * KC, KR * coarse, bands * coarse), F32),
+            pltpu.VMEM(pan_blocks.shape, BF16),
+            pltpu.VMEM(ms_blocks.shape, BF16),
+            pltpu.SemaphoreType.DMA((parts, 2)),
         ],
-        compiler_params=params(),
+        compiler_params=params(60),
+        cost_estimate=pl.CostEstimate(flops=10**9, bytes_accessed=16 * MIB, transcendentals=0),
         name="cell_sums",
     )(who, send_list, pan_blocks, ms_blocks)
-
-    start = TR
-    tall = 2 * (TR // 4) + 16
-    height = TR + tall
-    pan_cells = pan_cells.reshape(n, KC, KR * block, block)
-    ms_cells = ms_cells.reshape(n, KC, KR * coarse, bands * coarse)
-
-    pairs = n // 2
-    result = pl.BlockSpec((height, TC), lambda i: (0, 0))
-    *far, near_ms = pl.pallas_call(
-        functools.partial(far_maps, n, bands),
-        grid=(pairs,),
-        in_specs=[
-            whole(pltpu.SMEM),
-            whole(pltpu.SMEM),
-            pl.BlockSpec((2,) + ms_cells.shape[1:], lambda i: (i, 0, 0, 0)),
-            pl.BlockSpec((1,) + pan_cells.shape[1:], lambda i: (n - 1 - 2 * i, 0, 0, 0)),
-        ],
-        out_specs=[result] * pairs + [pl.BlockSpec((pairs, tall, TC), lambda i: (0, 0, 0))],
-        scratch_shapes=[pltpu.VMEM((KC * 128, TC), BF16)] * 2
-        + [pltpu.VMEM((KC * block, TC), BF16), pltpu.VMEM((n + 2, 8, TC), F32)],
-        out_shape=[jax.ShapeDtypeStruct((height, TC), BF16)] * pairs
-        + [jax.ShapeDtypeStruct((pairs, tall, TC), BF16)],
-        compiler_params=params(),
-        name="far_maps",
-    )(who, grids, ms_cells, pan_cells)
-    steps = [n - 2 - 2 * i for i in range(pairs)]
-    theirs = [exchange(piece, 1, n) for piece in far]
-    fold = 2
-    near = pl.pallas_call(
-        functools.partial(near_maps, n, fold),
-        grid=(pairs // fold,),
-        in_specs=[
-            whole(pltpu.SMEM),
-            whole(pltpu.SMEM),
-            pl.BlockSpec((fold, tall, TC), lambda i: (i, 0, 0)),
-        ]
-        + [
-            pl.BlockSpec(
-                (1,) + pan_cells.shape[1:], lambda i, u=u: (n - 2 - 2 * (fold * i + u), 0, 0, 0)
-            )
-            for u in range(fold)
-        ],
-        out_specs=[result] * pairs,
-        scratch_shapes=[pltpu.VMEM((KC * block, TC), BF16)] * fold,
-        out_shape=[jax.ShapeDtypeStruct((height, TC), F32)] * pairs,
-        compiler_params=params(),
-        name="near_maps",
-    )(who, grids, near_ms, *([pan_cells] * fold))
+    top = n // 2
+
+    held = {}
+
+    def make(first, count, *after):
+        order = range(first + count - 1, first - 1, -1)
+        kept = [k == 0 or (k >= top and k % 2 == 0) for k in order]
+        made = pl.pallas_call(
+            functools.partial(group_maps, n, bands, first, count),
+            in_specs=[whole(pltpu.SMEM)] * 2
+            + [hbm] * 2
+            + [pl.BlockSpec(memory_space=pl.ANY)] * len(after),
+            out_specs=[whole()] * count,
+            out_shape=[jax.ShapeDtypeStruct((height, TC), F32 if keep else BF16) for keep in kept],
+            scratch_shapes=[
+                [pltpu.VMEM((KC * 128, TC), BF16)] * 2,
+                [pltpu.VMEM((KC * block, TC), BF16)] * count,
+                pltpu.VMEM((count, tall - 16, TC), BF16),
+                pltpu.VMEM((count + 2, 8, TC), F32),
+                pltpu.VMEM((count * KC, KR * block, block), BF16),
+                pltpu.VMEM((count + 2, KC, KR * coarse, bands * coarse), BF16),
+                pltpu.SemaphoreType.DMA((count + 3,)),
+            ],
+            compiler_params=params(60),
+            name="group_maps",
+        )(who, grids, cells, ms_cells, *after)
+        held.update((k, [piece]) for k, piece in zip(order, made))
+
+
+    def pass_on(k, bit):
+        got = held.pop(k)
+        if len(got) > 1:
+            got = [sum(part.astype(F32) for part in got).astype(BF16)]
+        held[k ^ bit].append(exchange(got[0], bit, n))
+        return got[0]
+
+    after = ()
+    for k in range(n - 2, top - 1, -2):
+        make(k, 2, *after)
+        after = (held[k + 1][0],)
+    for k in range(n - 1, top - 1, -2):
+        pass_on(k, 1)
+    quad = min(4, top)
+    bit = 2
+    while bit < top:
+        for k in range(n - bit, top - 1, -2 * bit):
+            sent = pass_on(k, bit)
+            if k == n - 2:
+                for first in range(top - quad, -1, -quad):
+                    make(first, quad, sent)
+        bit *= 2
+    filler = pass_on(top, top)
+    for k in sorted(range(1, top), key=lambda k: -k):
+        pass_on(k, k)
+    mine, last, *others, early = held[0]
+    got = [mine + early.astype(F32), *others, last]
 
     lanes = 3 * 128
     up, cols = pl.pallas_call(
         functools.partial(tables, bands),
-        in_specs=[whole(pltpu.SMEM)] * 4,
+        in_specs=[whole(pltpu.SMEM)] * 4 + [pl.BlockSpec(memory_space=pl.ANY)],
         out_specs=[whole(), whole()],
         out_shape=[
             jax.ShapeDtypeStruct((bands, TR, lanes), BF16),
             jax.ShapeDtypeStruct((TC // 2, TC), BF16),
         ],
-        compiler_params=params(),
+        compiler_params=params(8),
         name="tables",
-    )(who, band_mix, band_gain, synth_weight)
-
-    got = [near[-1], theirs[-1]]
-    for k, a, b in zip(steps[:-1], near, theirs):
-        got.append(exchange((a + b.astype(F32)).astype(BF16), k, n))
-    ms_map = sum(part[start:].astype(F32) for part in got).astype(BF16)
+    )(who, band_mix, band_gain, synth_weight, filler)
+
+    got, up, cols = lax.optimization_barrier((got, up, cols))
+    ms_map = sum(part[TR:].astype(F32) for part in got).astype(BF16)
     other = lax.ppermute(ms_map, "mcol", [(0, 1), (1, 0)])
     each = 2
     once = lambda x: pl.BlockSpec(x.shape, lambda i: (0, 0))
@@ -448,7 +457,7 @@
         out_specs=pl.BlockSpec((each, TR, TC), lambda i: (i, 0, 0)),
         out_shape=jax.ShapeDtypeStruct((bands, TR, TC), BF16),
         scratch_shapes=[pltpu.VMEM((lanes, TC), BF16), pltpu.VMEM((TR, TC), F32)],
-        compiler_params=params(),
+        compiler_params=params(16),
         name="finish",
     )(band_gain, up, cols, ms_map, other, *got)
 

time: 63.7 us -> 57.7 us (0.906)
  the two profiles are of different devices: /device:TPU:1 before, /device:TPU:11 now
where the time goes in v3:
time: 57.7 us; the launch traced here: 57.4 us
  Pallas kernels  25.4 us (44%)
  starting transfers between devices  17.4 us (30%)
  waiting for transfers between devices  10.4 us (18%)
  other arithmetic  3.33 us (6%)
  local copies, waits for them, and re-layouts  0.65 us (1%)
    pallas_call x3, Pallas kernels, make(): pl.pallas_call(functools.partial(group_maps, n, bands, first, count), in_...  15.5 us
    ppermute x11, starting transfers between devices, exchange(): return lax.ppermute(x, 'mrow', [(i, i ^ step) for i in range(count)])  12.1 us
    ppermute x11, waiting for transfers between devices, exchange(): return lax.ppermute(x, 'mrow', [(i, i ^ step) for i in range(count)])  8.5 us
    pallas_call x1, Pallas kernels, local(): pl.pallas_call(functools.partial(cell_sums, capacity), in_specs=[whole(pl...  5.5 us
    ppermute x1, starting transfers between devices, local(): other = lax.ppermute(ms_map, 'mcol', [(0, 1), (1, 0)])  4.66 us
    pallas_call x1, Pallas kernels, local(): pl.pallas_call(functools.partial(finish, bands), grid=(bands // each,), i...  3.15 us
    pallas_call x1, Pallas kernels, local(): pl.pallas_call(functools.partial(tables, bands), in_specs=[whole(pltpu.SM...  1.23 us
  transfers between devices with their start and end apart: 13, of which 6 were waited for; matrix products, arithmetic and copies ran while one was open for 3% of the time, Pallas kernels for 31%

profile of v3, /device:TPU:11, one launch (start us, length us, event | category | flops | bytes accessed | tf_op | source)
XLA Modules:
  0.0 57.4 jit_solution(16542555264621885113)
XLA Ops:
  0.0 0.7 %collective-permute-start = (f32[1,8]{1,0:T(1,128)}, f32[1,8]{1,0:T(1,128)S(1)}, u32[]{:S(2)}, u32[]{:S(2)}) collective-permute-start(f32[1,8]{1,0:T(1,128)} %param.13), channel_id=1, source_target_pairs={{0,1},{1,0},{2,3},{3,2},{4,5},{5,4},{6,7},{7,6},{8,9},{9,8},{10,11... | collective-permute-start | bytes 104 | tf_op jit(solution)/shard_map/ppermute | solution.py:343
  0.7 1.0 %collective-permute-done = f32[1,8]{1,0:T(1,128)S(1)} collective-permute-done((f32[1,8]{1,0:T(1,128)}, f32[1,8]{1,0:T(1,128)S(1)}, u32[]{:S(2)}, u32[]{:S(2)}) %collective-permute-start) | collective-permute-done | bytes 64 | tf_op jit(solution)/shard_map/ppermute | solution.py:343
  1.6 0.7 %pad_maximum_fusion.1 = f32[1,19]{1,0:T(1,128)S(1)} fusion(f32[1,8]{1,0:T(1,128)S(1)} %collective-permute-done, f32[1,8]{1,0:T(1,128)} %param.13, f32[1,3]{1,0:T(1,128)} %bitcast.3), kind=kLoop, calls=%fused_computation.6 | loop fusion | flops 38 | bytes 152 | tf_op jit(solution)/shard_map/concatenate | solution.py:344
  2.4 1.2 %collective-permute-start.1 = (f32[1,19]{1,0:T(1,128)S(1)}, f32[1,19]{1,0:T(1,128)S(1)}, u32[]{:S(2)}, u32[]{:S(2)}) collective-permute-start(f32[1,19]{1,0:T(1,128)S(1)} %pad_maximum_fusion.1), channel_id=1, source_target_pairs={{0,2},{2,0},{4,6},{6,4},{8,10},{10,8},{12,14},{14,12},{1,3},{3,1},... | collective-permute-start | bytes 236 | tf_op jit(solution)/shard_map/ppermute | solution.py:321
  3.6 0.6 %pad_add_fusion.who = s32[2]{0:T(128)} fusion(s32[1]{0:T(128)} %bitcast.1, s32[1]{0:T(128)} %bitcast), kind=kLoop, calls=%fused_computation.5 | loop fusion | flops 2 | bytes 16 | tf_op jit(solution)/shard_map/stack | solution.py:341
  4.2 0.5 collective-permute-done.1
  4.8 0.7 %pad_maximum_fusion = f32[2,19]{1,0:T(2,128)S(1)} fusion(f32[1,19]{1,0:T(1,128)S(1)} %collective-permute-done.1, f32[1,8]{1,0:T(1,128)S(1)} %collective-permute-done, f32[1,8]{1,0:T(1,128)} %param.13, f32[1,3]{1,0:T(1,128)} %bitcast.4), kind=kLoop, calls=%fused_computation.4 | loop fusion | flops 114 | bytes 304 | tf_op jit(solution)/shard_map/concatenate | solution.py:345
  5.5 0.2 collective-permute-start.2
  5.7 2.3 %collective-permute-start.3 = (f32[2,19]{1,0:T(2,128)S(1)}, f32[2,19]{1,0:T(2,128)S(1)}, u32[]{:S(2)}, u32[]{:S(2)}) collective-permute-start(f32[2,19]{1,0:T(2,128)S(1)} %pad_maximum_fusion), channel_id=1, source_target_pairs={{0,8},{2,10},{4,12},{6,14},{8,0},{10,2},{12,4},{14,6},{1,9},{3,11}... | collective-permute-start | bytes 464 | tf_op jit(solution)/shard_map/ppermute | solution.py:321
  8.0 0.2 collective-permute-start.4
  8.2 5.5 %cell_sums.1 = (bf16[40,256,128]{2,1,0:T(8,128)(2,1)}, bf16[40,64,256]{2,1,0:T(8,128)(2,1)}) custom-call(s32[2]{0:T(128)} %pad_add_fusion.who, s32[3,64]{1,0:T(4,128)} %list_ref.1, bf16[64,128,128]{2,1,0:T(8,128)(2,1)} %pan_hbm.1, bf16[64,32,256]{2,1,0:T(8,128)(2,1)} %ms_hbm.1), custom_call_target="tpu_custom_call" | custom-call | flops 1000000000 | bytes 16777216 | tf_op jit(solution)/shard_map/cell_sums/pallas_call | solution.py:352
  13.7 0.0 collective-permute-done.2
  13.7 0.0 collective-permute-done.3
  13.7 0.0 collective-permute-done.4
  13.7 0.6 %concatenate.12.grids = f32[8,19]{1,0:T(8,128)} concatenate(f32[1,19]{1,0:T(1,128)S(1)} %pad_maximum_fusion.1, f32[1,19]{1,0:T(1,128)S(1)} %collective-permute-done.1, f32[2,19]{1,0:T(2,128)S(1)} %collective-permute-done.2, f32[2,19]{1,0:T(2,128)S(1)} %collective-permute-done.3, f32[2,19]{1,0:T(2,128)S(1)} %collective-permute-done.4), dimensions={0} | concatenate | bytes 1216 | tf_op jit(solution)/shard_map/concatenate | solution.py:346
  14.3 4.7 %group_maps.3 = (bf16[208,512]{1,0:T(8,128)(2,1)}, f32[208,512]{1,0:T(8,128)}) custom-call(s32[2]{0:T(128)} %pad_add_fusion.who, f32[8,19]{1,0:T(8,128)} %concatenate.12.grids, bf16[40,256,128]{2,1,0:T(8,128)(2,1)} %get-tuple-element.23.cells_hbm, bf16[40,64,256]{2,1,0:T(8,128)(2,1)} %get-tuple-element.24.ms_hbm), custom_call_target="tpu_custom_call" | custom-call | tf_op jit(solution)/shard_map/group_maps/pallas_call | solution.py:378
  19.0 0.0 copy-start.6
  19.0 1.3 %collective-permute-start.5 = (bf16[208,512]{1,0:T(8,128)(2,1)}, bf16[208,512]{1,0:T(8,128)(2,1)S(1)}, u32[]{:S(2)}, u32[]{:S(2)}) collective-permute-start(bf16[208,512]{1,0:T(8,128)(2,1)} %get-tuple-element.26.refs_0_), channel_id=1, source_target_pairs={{0,2},{2,0},{4,6},{6,4},{8,10},{10,8},{12,14},{14,12},{1,3},{3,1},... | collective-permute-start | bytes 638984 | tf_op jit(solution)/shard_map/ppermute | solution.py:321
  20.3 4.7 %group_maps.5 = (bf16[208,512]{1,0:T(8,128)(2,1)}, f32[208,512]{1,0:T(8,128)}) custom-call(s32[2]{0:T(128)} %pad_add_fusion.who, f32[8,19]{1,0:T(8,128)} %concatenate.12.grids, bf16[40,256,128]{2,1,0:T(8,128)(2,1)} %get-tuple-element.23.cells_hbm, bf16[40,64,256]{2,1,0:T(8,128)(2,1)} %get-tuple-element.24.ms_hbm, bf16[208,512]{1,0:T(8,128)(2,1)} %get-tuple-element.26.refs_0_), custom_call_target="tpu_custom_call" | custom-call | tf_op jit(solution)/shard_map/group_maps/pallas_call | solution.py:378
  25.0 0.3 collective-permute-start.9
  25.3 0.0 collective-permute-done.5
  25.3 0.0 copy-done.6
  25.4 0.0 copy-start.4
  25.4 0.0 copy-start.5
  25.4 0.0 copy-start
  25.4 0.0 copy-start.1
  25.4 0.0 copy-start.2
  25.4 0.0 copy-start.3
  25.4 1.2 %collective-permute-start.10 = (bf16[208,512]{1,0:T(8,128)(2,1)S(1)}, bf16[208,512]{1,0:T(8,128)(2,1)S(1)}, u32[]{:S(2)}, u32[]{:S(2)}) collective-permute-start(bf16[208,512]{1,0:T(8,128)(2,1)S(1)} %add_convert_fusion.1.refs_0_), channel_id=1, source_target_pairs={{0,4},{2,6},{4,0},{6,2},{8,12},{10,14},{12,8},{14,10},{1,5},{3,7},... | collective-permute-start | bytes 638984 | tf_op jit(solution)/shard_map/ppermute | solution.py:321
  26.6 0.0 copy-done.4
  26.6 6.1 %group_maps.4 = (bf16[208,512]{1,0:T(8,128)(2,1)}, bf16[208,512]{1,0:T(8,128)(2,1)}, bf16[208,512]{1,0:T(8,128)(2,1)}, f32[208,512]{1,0:T(8,128)}) custom-call(s32[2]{0:T(128)} %pad_add_fusion.who, f32[8,19]{1,0:T(8,128)} %concatenate.12.grids, bf16[40,256,128]{2,1,0:T(8,128)(2,1)} %get-tuple-element.23.cells_hbm, ...), custom_call_target="tpu_custom_call" | custom-call | tf_op jit(solution)/shard_map/group_maps/pallas_call | solution.py:378
  32.8 1.3 %collective-permute-start.6 = (bf16[208,512]{1,0:T(8,128)(2,1)}, bf16[208,512]{1,0:T(8,128)(2,1)S(1)}, u32[]{:S(2)}, u32[]{:S(2)}) collective-permute-start(bf16[208,512]{1,0:T(8,128)(2,1)} %get-tuple-element.28), channel_id=1, source_target_pairs={{0,2},{2,0},{4,6},{6,4},{8,10},{10,8},{12,14},{14,12},{1,3},{3,1},... | collective-permute-start | bytes 638984 | tf_op jit(solution)/shard_map/ppermute | solution.py:321
  34.1 0.5 collective-permute-start.7
  34.6 0.9 %collective-permute-start.8 = (bf16[208,512]{1,0:T(8,128)(2,1)}, bf16[208,512]{1,0:T(8,128)(2,1)S(1)}, u32[]{:S(2)}, u32[]{:S(2)}) collective-permute-start(bf16[208,512]{1,0:T(8,128)(2,1)} %get-tuple-element.30), channel_id=1, source_target_pairs={{0,4},{2,6},{4,0},{6,2},{8,12},{10,14},{12,8},{14,10},{1,5},{3,7},... | collective-permute-start | bytes 638984 | tf_op jit(solution)/shard_map/ppermute | solution.py:321
  35.5 0.0 collective-permute-done.9
  35.5 0.0 collective-permute-done.10
  35.5 0.0 copy-done.5
  35.5 0.1 add_convert_fusion.after
  35.6 2.7 %collective-permute-start.11 = (bf16[208,512]{1,0:T(8,128)(2,1)S(1)}, bf16[208,512]{1,0:T(8,128)(2,1)S(1)}, u32[]{:S(2)}, u32[]{:S(2)}) collective-permute-start(bf16[208,512]{1,0:T(8,128)(2,1)S(1)} %add_convert_fusion.after), channel_id=1, source_target_pairs={{0,8},{2,10},{4,12},{6,14},{8,0},{10,2},{12,4},{14,6},{1,9},{3,11}... | collective-permute-start | bytes 638984 | tf_op jit(solution)/shard_map/ppermute | solution.py:321
  38.3 0.0 copy-done
  38.3 0.0 copy-done.1
  38.3 0.0 copy-done.2
  38.3 0.0 copy-done.3
  38.3 1.2 %tables.1 = (bf16[8,128,384]{2,1,0:T(8,128)(2,1)S(1)}, bf16[256,512]{1,0:T(8,128)(2,1)S(1)}) custom-call(s32[2]{0:T(128)S(1)} %copy-done, f32[8,8]{1,0:T(8,128)S(1)} %copy-done.1, f32[8]{0:T(128)S(1)} %copy-done.2, f32[8]{0:T(128)S(1)} %copy-done.3, bf16[208,512]{1,0:T(8,128)(2,1)S(1)} %add_convert_fusion.after), custom_call_target="tpu_custom_call" | custom-call | tf_op jit(solution)/shard_map/tables/pallas_call | solution.py:429
  39.6 0.9 %collective-permute-done.6 = bf16[208,512]{1,0:T(8,128)(2,1)S(1)} collective-permute-done((bf16[208,512]{1,0:T(8,128)(2,1)}, bf16[208,512]{1,0:T(8,128)(2,1)S(1)}, u32[]{:S(2)}, u32[]{:S(2)}) %collective-permute-start.6) | collective-permute-done | bytes 213024 | tf_op jit(solution)/shard_map/ppermute | solution.py:321
  40.5 1.1 %convert_add_fusion.refs_0_ = f32[208,512]{1,0:T(8,128)S(1)} fusion(f32[208,512]{1,0:T(8,128)} %get-tuple-element.27, bf16[208,512]{1,0:T(8,128)(2,1)S(1)} %collective-permute-done.6), kind=kLoop, calls=%fused_computation.1 | loop fusion | flops 212992 | bytes 1064960 | tf_op jit(solution)/shard_map/add | solution.py:426
  41.5 0.0 collective-permute-done.7.refs_1_
  41.6 3.9 %collective-permute-done.8.refs_2_ = bf16[208,512]{1,0:T(8,128)(2,1)S(1)} collective-permute-done((bf16[208,512]{1,0:T(8,128)(2,1)}, bf16[208,512]{1,0:T(8,128)(2,1)S(1)}, u32[]{:S(2)}, u32[]{:S(2)}) %collective-permute-start.8) | collective-permute-done | bytes 213024 | tf_op jit(solution)/shard_map/ppermute | solution.py:321
  45.4 3.1 %collective-permute-done.11.refs_3_ = bf16[208,512]{1,0:T(8,128)(2,1)S(1)} collective-permute-done((bf16[208,512]{1,0:T(8,128)(2,1)S(1)}, bf16[208,512]{1,0:T(8,128)(2,1)S(1)}, u32[]{:S(2)}, u32[]{:S(2)}) %collective-permute-start.11) | collective-permute-done | bytes 213024 | tf_op jit(solution)/shard_map/ppermute | solution.py:321
  48.6 4.7 %collective-permute-start.12 = (bf16[80,512]{1,0:T(8,128)(2,1)S(1)}, bf16[80,512]{1,0:T(8,128)(2,1)S(1)}, u32[]{:S(2)}, u32[]{:S(2)}) collective-permute-start(bf16[80,512]{1,0:T(8,128)(2,1)S(1)} %add_convert_fusion.2.ms_ref), channel_id=1, source_target_pairs={{0,1},{1,0},{2,3},{3,2},{4,5},{5,4},{6,7},{7,6},{8,9},{9,8},{10,11... | collective-permute-start | bytes 245768 | tf_op jit(solution)/shard_map/ppermute | solution.py:443
  53.3 0.9 %collective-permute-done.12.other_ref = bf16[80,512]{1,0:T(8,128)(2,1)S(1)} collective-permute-done((bf16[80,512]{1,0:T(8,128)(2,1)S(1)}, bf16[80,512]{1,0:T(8,128)(2,1)S(1)}, u32[]{:S(2)}, u32[]{:S(2)}) %collective-permute-start.12) | collective-permute-done | bytes 81952 | tf_op jit(solution)/shard_map/ppermute | solution.py:443
  54.2 3.2 %finish.1 = bf16[8,128,512]{2,1,0:T(8,128)(2,1)} custom-call(f32[8]{0:T(128)S(1)} %copy-done.2, bf16[8,128,384]{2,1,0:T(8,128)(2,1)S(1)} %get-tuple-element.35.up_ref, bf16[256,512]{1,0:T(8,128)(2,1)S(1)} %get-tuple-element.36.cols_ref, bf16[80,512]{1,0:T(8,128)(2,1)S(1)} %add_convert_fusion.2.ms_ref, bf16[80,512]{1,0:T(8,128)(2,1)S(1)} %collective-permute-done.12.other_ref, ...), custom_call_target="tpu_custom_call" | custom-call | tf_op jit(solution)/shard_map/finish/pallas_call | solution.py:446
  (2 shorter events, 0.1 us)
Async XLA Ops:
  0.0 1.6 %collective-permute-start = (f32[1,8]{1,0:T(1,128)}, f32[1,8]{1,0:T(1,128)S(1)}, u32[]{:S(2)}, u32[]{:S(2)}) collective-permute-start(f32[1,8]{1,0:T(1,128)} %param.13), channel_id=1, source_target_pairs={{0,1},{1,0},{2,3},{3,2},{4,5},{5,4},{6,7},{7,6},{8,9},{9,8},{10,11... | collective-permute-start | bytes 104 | tf_op jit(solution)/shard_map/ppermute | solution.py:343
  2.4 2.4 %collective-permute-start.1 = (f32[1,19]{1,0:T(1,128)S(1)}, f32[1,19]{1,0:T(1,128)S(1)}, u32[]{:S(2)}, u32[]{:S(2)}) collective-permute-start(f32[1,19]{1,0:T(1,128)S(1)} %pad_maximum_fusion.1), channel_id=1, source_target_pairs={{0,2},{2,0},{4,6},{6,4},{8,10},{10,8},{12,14},{14,12},{1,3},{3,1},... | collective-permute-start | bytes 236 | tf_op jit(solution)/shard_map/ppermute | solution.py:321
  5.5 8.2 %collective-permute-start.2 = (f32[2,19]{1,0:T(2,128)S(1)}, f32[2,19]{1,0:T(2,128)S(1)}, u32[]{:S(2)}, u32[]{:S(2)}) collective-permute-start(f32[2,19]{1,0:T(2,128)S(1)} %pad_maximum_fusion), channel_id=1, source_target_pairs={{0,4},{2,6},{4,0},{6,2},{8,12},{10,14},{12,8},{14,10},{1,5},{3,7},... | collective-permute-start | bytes 464 | tf_op jit(solution)/shard_map/ppermute | solution.py:321
  5.7 8.0 %collective-permute-start.3 = (f32[2,19]{1,0:T(2,128)S(1)}, f32[2,19]{1,0:T(2,128)S(1)}, u32[]{:S(2)}, u32[]{:S(2)}) collective-permute-start(f32[2,19]{1,0:T(2,128)S(1)} %pad_maximum_fusion), channel_id=1, source_target_pairs={{0,8},{2,10},{4,12},{6,14},{8,0},{10,2},{12,4},{14,6},{1,9},{3,11}... | collective-permute-start | bytes 464 | tf_op jit(solution)/shard_map/ppermute | solution.py:321
  8.0 5.7 %collective-permute-start.4 = (f32[2,19]{1,0:T(2,128)S(1)}, f32[2,19]{1,0:T(2,128)S(1)}, u32[]{:S(2)}, u32[]{:S(2)}) collective-permute-start(f32[2,19]{1,0:T(2,128)S(1)} %pad_maximum_fusion), channel_id=1, source_target_pairs={{0,12},{2,14},{4,8},{6,10},{8,4},{10,6},{12,0},{14,2},{1,13},{3,15... | collective-permute-start | bytes 464 | tf_op jit(solution)/shard_map/ppermute | solution.py:321
  19.0 6.3 %copy-start.6 = (f32[208,512]{1,0:T(8,128)S(1)}, f32[208,512]{1,0:T(8,128)}, u32[]{:S(2)}) copy-start(f32[208,512]{1,0:T(8,128)} %get-tuple-element.25) | copy-start | bytes 1277956
  19.0 6.3 %collective-permute-start.5 = (bf16[208,512]{1,0:T(8,128)(2,1)}, bf16[208,512]{1,0:T(8,128)(2,1)S(1)}, u32[]{:S(2)}, u32[]{:S(2)}) collective-permute-start(bf16[208,512]{1,0:T(8,128)(2,1)} %get-tuple-element.26.refs_0_), channel_id=1, source_target_pairs={{0,2},{2,0},{4,6},{6,4},{8,10},{10,8},{12,14},{14,12},{1,3},{3,1},... | collective-permute-start | bytes 638984 | tf_op jit(solution)/shard_map/ppermute | solution.py:321
  25.0 10.5 %collective-permute-start.9 = (bf16[208,512]{1,0:T(8,128)(2,1)}, bf16[208,512]{1,0:T(8,128)(2,1)S(1)}, u32[]{:S(2)}, u32[]{:S(2)}) collective-permute-start(bf16[208,512]{1,0:T(8,128)(2,1)} %get-tuple-element.32), channel_id=1, source_target_pairs={{0,2},{2,0},{4,6},{6,4},{8,10},{10,8},{12,14},{14,12},{1,3},{3,1},... | collective-permute-start | bytes 638984 | tf_op jit(solution)/shard_map/ppermute | solution.py:321
  25.4 1.3 %copy-start.4 = (bf16[208,512]{1,0:T(8,128)(2,1)}, bf16[208,512]{1,0:T(8,128)(2,1)S(1)}, u32[]{:S(2)}) copy-start(bf16[208,512]{1,0:T(8,128)(2,1)S(1)} %add_convert_fusion.1.refs_0_) | copy-start | bytes 638980
  25.4 10.1 %copy-start.5 = (f32[208,512]{1,0:T(8,128)S(1)}, f32[208,512]{1,0:T(8,128)}, u32[]{:S(2)}) copy-start(f32[208,512]{1,0:T(8,128)} %get-tuple-element.31) | copy-start | bytes 1277956
  25.4 12.9 %copy-start = (s32[2]{0:T(128)S(1)}, s32[2]{0:T(128)}, u32[]{:S(2)}) copy-start(s32[2]{0:T(128)} %pad_add_fusion.who) | copy-start | bytes 28
  25.4 12.9 %copy-start.1 = (f32[8,8]{1,0:T(8,128)S(1)}, f32[8,8]{1,0:T(8,128)}, u32[]{:S(2)}) copy-start(f32[8,8]{1,0:T(8,128)} %mix.1) | copy-start | bytes 772
  25.4 12.9 %copy-start.2 = (f32[8]{0:T(128)S(1)}, f32[8]{0:T(128)}, u32[]{:S(2)}) copy-start(f32[8]{0:T(128)} %gain.3) | copy-start | bytes 100
  25.4 12.9 %copy-start.3 = (f32[8]{0:T(128)S(1)}, f32[8]{0:T(128)}, u32[]{:S(2)}) copy-start(f32[8]{0:T(128)} %synth.1) | copy-start | bytes 100
  25.4 10.1 %collective-permute-start.10 = (bf16[208,512]{1,0:T(8,128)(2,1)S(1)}, bf16[208,512]{1,0:T(8,128)(2,1)S(1)}, u32[]{:S(2)}, u32[]{:S(2)}) collective-permute-start(bf16[208,512]{1,0:T(8,128)(2,1)S(1)} %add_convert_fusion.1.refs_0_), channel_id=1, source_target_pairs={{0,4},{2,6},{4,0},{6,2},{8,12},{10,14},{12,8},{14,10},{1,5},{3,7},... | collective-permute-start | bytes 638984 | tf_op jit(solution)/shard_map/ppermute | solution.py:321
  32.8 7.7 %collective-permute-start.6 = (bf16[208,512]{1,0:T(8,128)(2,1)}, bf16[208,512]{1,0:T(8,128)(2,1)S(1)}, u32[]{:S(2)}, u32[]{:S(2)}) collective-permute-start(bf16[208,512]{1,0:T(8,128)(2,1)} %get-tuple-element.28), channel_id=1, source_target_pairs={{0,2},{2,0},{4,6},{6,4},{8,10},{10,8},{12,14},{14,12},{1,3},{3,1},... | collective-permute-start | bytes 638984 | tf_op jit(solution)/shard_map/ppermute | solution.py:321
  34.1 7.4 %collective-permute-start.7 = (bf16[208,512]{1,0:T(8,128)(2,1)}, bf16[208,512]{1,0:T(8,128)(2,1)S(1)}, u32[]{:S(2)}, u32[]{:S(2)}) collective-permute-start(bf16[208,512]{1,0:T(8,128)(2,1)} %get-tuple-element.29), channel_id=1, source_target_pairs={{0,6},{2,4},{4,2},{6,0},{8,14},{10,12},{12,10},{14,8},{1,7},{3,5},... | collective-permute-start | bytes 638984 | tf_op jit(solution)/shard_map/ppermute | solution.py:321
  34.6 10.8 %collective-permute-start.8 = (bf16[208,512]{1,0:T(8,128)(2,1)}, bf16[208,512]{1,0:T(8,128)(2,1)S(1)}, u32[]{:S(2)}, u32[]{:S(2)}) collective-permute-start(bf16[208,512]{1,0:T(8,128)(2,1)} %get-tuple-element.30), channel_id=1, source_target_pairs={{0,4},{2,6},{4,0},{6,2},{8,12},{10,14},{12,8},{14,10},{1,5},{3,7},... | collective-permute-start | bytes 638984 | tf_op jit(solution)/shard_map/ppermute | solution.py:321
  35.6 13.0 %collective-permute-start.11 = (bf16[208,512]{1,0:T(8,128)(2,1)S(1)}, bf16[208,512]{1,0:T(8,128)(2,1)S(1)}, u32[]{:S(2)}, u32[]{:S(2)}) collective-permute-start(bf16[208,512]{1,0:T(8,128)(2,1)S(1)} %add_convert_fusion.after), channel_id=1, source_target_pairs={{0,8},{2,10},{4,12},{6,14},{8,0},{10,2},{12,4},{14,6},{1,9},{3,11}... | collective-permute-start | bytes 638984 | tf_op jit(solution)/shard_map/ppermute | solution.py:321
  48.6 5.6 %collective-permute-start.12 = (bf16[80,512]{1,0:T(8,128)(2,1)S(1)}, bf16[80,512]{1,0:T(8,128)(2,1)S(1)}, u32[]{:S(2)}, u32[]{:S(2)}) collective-permute-start(bf16[80,512]{1,0:T(8,128)(2,1)S(1)} %add_convert_fusion.2.ms_ref), channel_id=1, source_target_pairs={{0,1},{1,0},{2,3},{3,2},{4,5},{5,4},{6,7},{7,6},{8,9},{9,8},{10,11... | collective-permute-start | bytes 245768 | tf_op jit(solution)/shard_map/ppermute | solution.py:443

commit v4 on v3

--- a/solution.py
+++ b/solution.py
@@ -441,7 +441,7 @@
     got, up, cols = lax.optimization_barrier((got, up, cols))
     ms_map = sum(part[TR:].astype(F32) for part in got).astype(BF16)
     other = lax.ppermute(ms_map, "mcol", [(0, 1), (1, 0)])
-    each = 2
+    each = 4
     once = lambda x: pl.BlockSpec(x.shape, lambda i: (0, 0))
     return pl.pallas_call(
         functools.partial(finish, bands),

time: 57.7 us -> 57.1 us (0.990)
  Pallas kernels: 25.4 us -> 24.8 us
    pallas_call x1, Pallas kernels: 3.15 us -> 2.51 us  [local(): pl.pallas_call(functools.partial(finish, bands), grid=(bands // each,), i...]
where the time goes in v4:
time: 57.1 us; the launch traced here: 56.7 us
  Pallas kernels  24.8 us (43%)
  starting transfers between devices  17.4 us (30%)
  waiting for transfers between devices  10.4 us (18%)
  other arithmetic  3.33 us (6%)
  local copies, waits for them, and re-layouts  0.65 us (1%)
    pallas_call x3, Pallas kernels, make(): pl.pallas_call(functools.partial(group_maps, n, bands, first, count), in_...  15.5 us
    ppermute x11, starting transfers between devices, exchange(): return lax.ppermute(x, 'mrow', [(i, i ^ step) for i in range(count)])  12.1 us
    ppermute x11, waiting for transfers between devices, exchange(): return lax.ppermute(x, 'mrow', [(i, i ^ step) for i in range(count)])  8.5 us
    pallas_call x1, Pallas kernels, local(): pl.pallas_call(functools.partial(cell_sums, capacity), in_specs=[whole(pl...  5.5 us
    ppermute x1, starting transfers between devices, local(): other = lax.ppermute(ms_map, 'mcol', [(0, 1), (1, 0)])  4.66 us
    pallas_call x1, Pallas kernels, local(): pl.pallas_call(functools.partial(finish, bands), grid=(bands // each,), i...  2.51 us
    pallas_call x1, Pallas kernels, local(): pl.pallas_call(functools.partial(tables, bands), in_specs=[whole(pltpu.SM...  1.23 us
  transfers between devices with their start and end apart: 13, of which 6 were waited for; matrix products, arithmetic and copies ran while one was open for 3% of the time, Pallas kernels for 31%

profile of v4, /device:TPU:11, one launch (start us, length us, event | category | flops | bytes accessed | tf_op | source)
XLA Modules:
  0.0 56.7 jit_solution(5213964808110927896)
XLA Ops:
  0.0 0.7 %collective-permute-start = (f32[1,8]{1,0:T(1,128)}, f32[1,8]{1,0:T(1,128)S(1)}, u32[]{:S(2)}, u32[]{:S(2)}) collective-permute-start(f32[1,8]{1,0:T(1,128)} %param.13), channel_id=1, source_target_pairs={{0,1},{1,0},{2,3},{3,2},{4,5},{5,4},{6,7},{7,6},{8,9},{9,8},{10,11... | collective-permute-start | bytes 104 | tf_op jit(solution)/shard_map/ppermute | solution.py:343
  0.7 1.0 %collective-permute-done = f32[1,8]{1,0:T(1,128)S(1)} collective-permute-done((f32[1,8]{1,0:T(1,128)}, f32[1,8]{1,0:T(1,128)S(1)}, u32[]{:S(2)}, u32[]{:S(2)}) %collective-permute-start) | collective-permute-done | bytes 64 | tf_op jit(solution)/shard_map/ppermute | solution.py:343
  1.6 0.7 %pad_maximum_fusion.1 = f32[1,19]{1,0:T(1,128)S(1)} fusion(f32[1,8]{1,0:T(1,128)S(1)} %collective-permute-done, f32[1,8]{1,0:T(1,128)} %param.13, f32[1,3]{1,0:T(1,128)} %bitcast.3), kind=kLoop, calls=%fused_computation.6 | loop fusion | flops 38 | bytes 152 | tf_op jit(solution)/shard_map/concatenate | solution.py:344
  2.4 1.2 %collective-permute-start.1 = (f32[1,19]{1,0:T(1,128)S(1)}, f32[1,19]{1,0:T(1,128)S(1)}, u32[]{:S(2)}, u32[]{:S(2)}) collective-permute-start(f32[1,19]{1,0:T(1,128)S(1)} %pad_maximum_fusion.1), channel_id=1, source_target_pairs={{0,2},{2,0},{4,6},{6,4},{8,10},{10,8},{12,14},{14,12},{1,3},{3,1},... | collective-permute-start | bytes 236 | tf_op jit(solution)/shard_map/ppermute | solution.py:321
  3.6 0.6 %pad_add_fusion.who = s32[2]{0:T(128)} fusion(s32[1]{0:T(128)} %bitcast.1, s32[1]{0:T(128)} %bitcast), kind=kLoop, calls=%fused_computation.5 | loop fusion | flops 2 | bytes 16 | tf_op jit(solution)/shard_map/stack | solution.py:341
  4.2 0.5 collective-permute-done.1
  4.8 0.7 %pad_maximum_fusion = f32[2,19]{1,0:T(2,128)S(1)} fusion(f32[1,19]{1,0:T(1,128)S(1)} %collective-permute-done.1, f32[1,8]{1,0:T(1,128)S(1)} %collective-permute-done, f32[1,8]{1,0:T(1,128)} %param.13, f32[1,3]{1,0:T(1,128)} %bitcast.4), kind=kLoop, calls=%fused_computation.4 | loop fusion | flops 114 | bytes 304 | tf_op jit(solution)/shard_map/concatenate | solution.py:345
  5.5 0.2 collective-permute-start.2
  5.7 2.3 %collective-permute-start.3 = (f32[2,19]{1,0:T(2,128)S(1)}, f32[2,19]{1,0:T(2,128)S(1)}, u32[]{:S(2)}, u32[]{:S(2)}) collective-permute-start(f32[2,19]{1,0:T(2,128)S(1)} %pad_maximum_fusion), channel_id=1, source_target_pairs={{0,8},{2,10},{4,12},{6,14},{8,0},{10,2},{12,4},{14,6},{1,9},{3,11}... | collective-permute-start | bytes 464 | tf_op jit(solution)/shard_map/ppermute | solution.py:321
  8.0 0.2 collective-permute-start.4
  8.2 5.5 %cell_sums.1 = (bf16[40,256,128]{2,1,0:T(8,128)(2,1)}, bf16[40,64,256]{2,1,0:T(8,128)(2,1)}) custom-call(s32[2]{0:T(128)} %pad_add_fusion.who, s32[3,64]{1,0:T(4,128)} %list_ref.1, bf16[64,128,128]{2,1,0:T(8,128)(2,1)} %pan_hbm.1, bf16[64,32,256]{2,1,0:T(8,128)(2,1)} %ms_hbm.1), custom_call_target="tpu_custom_call" | custom-call | flops 1000000000 | bytes 16777216 | tf_op jit(solution)/shard_map/cell_sums/pallas_call | solution.py:352
  13.7 0.0 collective-permute-done.2
  13.7 0.0 collective-permute-done.3
  13.7 0.0 collective-permute-done.4
  13.7 0.6 %concatenate.12.grids = f32[8,19]{1,0:T(8,128)} concatenate(f32[1,19]{1,0:T(1,128)S(1)} %pad_maximum_fusion.1, f32[1,19]{1,0:T(1,128)S(1)} %collective-permute-done.1, f32[2,19]{1,0:T(2,128)S(1)} %collective-permute-done.2, f32[2,19]{1,0:T(2,128)S(1)} %collective-permute-done.3, f32[2,19]{1,0:T(2,128)S(1)} %collective-permute-done.4), dimensions={0} | concatenate | bytes 1216 | tf_op jit(solution)/shard_map/concatenate | solution.py:346
  14.3 4.7 %group_maps.3 = (bf16[208,512]{1,0:T(8,128)(2,1)}, f32[208,512]{1,0:T(8,128)}) custom-call(s32[2]{0:T(128)} %pad_add_fusion.who, f32[8,19]{1,0:T(8,128)} %concatenate.12.grids, bf16[40,256,128]{2,1,0:T(8,128)(2,1)} %get-tuple-element.23.cells_hbm, bf16[40,64,256]{2,1,0:T(8,128)(2,1)} %get-tuple-element.24.ms_hbm), custom_call_target="tpu_custom_call" | custom-call | tf_op jit(solution)/shard_map/group_maps/pallas_call | solution.py:378
  19.0 0.0 copy-start.6
  19.0 1.3 %collective-permute-start.5 = (bf16[208,512]{1,0:T(8,128)(2,1)}, bf16[208,512]{1,0:T(8,128)(2,1)S(1)}, u32[]{:S(2)}, u32[]{:S(2)}) collective-permute-start(bf16[208,512]{1,0:T(8,128)(2,1)} %get-tuple-element.26.refs_0_), channel_id=1, source_target_pairs={{0,2},{2,0},{4,6},{6,4},{8,10},{10,8},{12,14},{14,12},{1,3},{3,1},... | collective-permute-start | bytes 638984 | tf_op jit(solution)/shard_map/ppermute | solution.py:321
  20.3 4.7 %group_maps.5 = (bf16[208,512]{1,0:T(8,128)(2,1)}, f32[208,512]{1,0:T(8,128)}) custom-call(s32[2]{0:T(128)} %pad_add_fusion.who, f32[8,19]{1,0:T(8,128)} %concatenate.12.grids, bf16[40,256,128]{2,1,0:T(8,128)(2,1)} %get-tuple-element.23.cells_hbm, bf16[40,64,256]{2,1,0:T(8,128)(2,1)} %get-tuple-element.24.ms_hbm, bf16[208,512]{1,0:T(8,128)(2,1)} %get-tuple-element.26.refs_0_), custom_call_target="tpu_custom_call" | custom-call | tf_op jit(solution)/shard_map/group_maps/pallas_call | solution.py:378
  25.0 0.3 collective-permute-start.9
  25.3 0.0 collective-permute-done.5
  25.3 0.0 copy-done.6
  25.4 0.0 copy-start.4
  25.4 0.0 copy-start.5
  25.4 0.0 copy-start
  25.4 0.0 copy-start.1
  25.4 0.0 copy-start.2
  25.4 0.0 copy-start.3
  25.4 1.2 %collective-permute-start.10 = (bf16[208,512]{1,0:T(8,128)(2,1)S(1)}, bf16[208,512]{1,0:T(8,128)(2,1)S(1)}, u32[]{:S(2)}, u32[]{:S(2)}) collective-permute-start(bf16[208,512]{1,0:T(8,128)(2,1)S(1)} %add_convert_fusion.1.refs_0_), channel_id=1, source_target_pairs={{0,4},{2,6},{4,0},{6,2},{8,12},{10,14},{12,8},{14,10},{1,5},{3,7},... | collective-permute-start | bytes 638984 | tf_op jit(solution)/shard_map/ppermute | solution.py:321
  26.6 0.0 copy-done.4
  26.6 6.1 %group_maps.4 = (bf16[208,512]{1,0:T(8,128)(2,1)}, bf16[208,512]{1,0:T(8,128)(2,1)}, bf16[208,512]{1,0:T(8,128)(2,1)}, f32[208,512]{1,0:T(8,128)}) custom-call(s32[2]{0:T(128)} %pad_add_fusion.who, f32[8,19]{1,0:T(8,128)} %concatenate.12.grids, bf16[40,256,128]{2,1,0:T(8,128)(2,1)} %get-tuple-element.23.cells_hbm, ...), custom_call_target="tpu_custom_call" | custom-call | tf_op jit(solution)/shard_map/group_maps/pallas_call | solution.py:378
  32.8 1.3 %collective-permute-start.6 = (bf16[208,512]{1,0:T(8,128)(2,1)}, bf16[208,512]{1,0:T(8,128)(2,1)S(1)}, u32[]{:S(2)}, u32[]{:S(2)}) collective-permute-start(bf16[208,512]{1,0:T(8,128)(2,1)} %get-tuple-element.28), channel_id=1, source_target_pairs={{0,2},{2,0},{4,6},{6,4},{8,10},{10,8},{12,14},{14,12},{1,3},{3,1},... | collective-permute-start | bytes 638984 | tf_op jit(solution)/shard_map/ppermute | solution.py:321
  34.1 0.5 collective-permute-start.7
  34.6 0.9 %collective-permute-start.8 = (bf16[208,512]{1,0:T(8,128)(2,1)}, bf16[208,512]{1,0:T(8,128)(2,1)S(1)}, u32[]{:S(2)}, u32[]{:S(2)}) collective-permute-start(bf16[208,512]{1,0:T(8,128)(2,1)} %get-tuple-element.30), channel_id=1, source_target_pairs={{0,4},{2,6},{4,0},{6,2},{8,12},{10,14},{12,8},{14,10},{1,5},{3,7},... | collective-permute-start | bytes 638984 | tf_op jit(solution)/shard_map/ppermute | solution.py:321
  35.5 0.0 collective-permute-done.9
  35.5 0.0 collective-permute-done.10
  35.5 0.0 copy-done.5
  35.5 0.1 add_convert_fusion.after
  35.6 2.7 %collective-permute-start.11 = (bf16[208,512]{1,0:T(8,128)(2,1)S(1)}, bf16[208,512]{1,0:T(8,128)(2,1)S(1)}, u32[]{:S(2)}, u32[]{:S(2)}) collective-permute-start(bf16[208,512]{1,0:T(8,128)(2,1)S(1)} %add_convert_fusion.after), channel_id=1, source_target_pairs={{0,8},{2,10},{4,12},{6,14},{8,0},{10,2},{12,4},{14,6},{1,9},{3,11}... | collective-permute-start | bytes 638984 | tf_op jit(solution)/shard_map/ppermute | solution.py:321
  38.3 0.0 copy-done
  38.3 0.0 copy-done.1
  38.3 0.0 copy-done.2
  38.3 0.0 copy-done.3
  38.3 1.2 %tables.1 = (bf16[8,128,384]{2,1,0:T(8,128)(2,1)S(1)}, bf16[256,512]{1,0:T(8,128)(2,1)S(1)}) custom-call(s32[2]{0:T(128)S(1)} %copy-done, f32[8,8]{1,0:T(8,128)S(1)} %copy-done.1, f32[8]{0:T(128)S(1)} %copy-done.2, f32[8]{0:T(128)S(1)} %copy-done.3, bf16[208,512]{1,0:T(8,128)(2,1)S(1)} %add_convert_fusion.after), custom_call_target="tpu_custom_call" | custom-call | tf_op jit(solution)/shard_map/tables/pallas_call | solution.py:429
  39.6 0.9 %collective-permute-done.6 = bf16[208,512]{1,0:T(8,128)(2,1)S(1)} collective-permute-done((bf16[208,512]{1,0:T(8,128)(2,1)}, bf16[208,512]{1,0:T(8,128)(2,1)S(1)}, u32[]{:S(2)}, u32[]{:S(2)}) %collective-permute-start.6) | collective-permute-done | bytes 213024 | tf_op jit(solution)/shard_map/ppermute | solution.py:321
  40.5 1.1 %convert_add_fusion.refs_0_ = f32[208,512]{1,0:T(8,128)S(1)} fusion(f32[208,512]{1,0:T(8,128)} %get-tuple-element.27, bf16[208,512]{1,0:T(8,128)(2,1)S(1)} %collective-permute-done.6), kind=kLoop, calls=%fused_computation.1 | loop fusion | flops 212992 | bytes 1064960 | tf_op jit(solution)/shard_map/add | solution.py:426
  41.5 0.0 collective-permute-done.7.refs_1_
  41.6 3.9 %collective-permute-done.8.refs_2_ = bf16[208,512]{1,0:T(8,128)(2,1)S(1)} collective-permute-done((bf16[208,512]{1,0:T(8,128)(2,1)}, bf16[208,512]{1,0:T(8,128)(2,1)S(1)}, u32[]{:S(2)}, u32[]{:S(2)}) %collective-permute-start.8) | collective-permute-done | bytes 213024 | tf_op jit(solution)/shard_map/ppermute | solution.py:321
  45.4 3.1 %collective-permute-done.11.refs_3_ = bf16[208,512]{1,0:T(8,128)(2,1)S(1)} collective-permute-done((bf16[208,512]{1,0:T(8,128)(2,1)S(1)}, bf16[208,512]{1,0:T(8,128)(2,1)S(1)}, u32[]{:S(2)}, u32[]{:S(2)}) %collective-permute-start.11) | collective-permute-done | bytes 213024 | tf_op jit(solution)/shard_map/ppermute | solution.py:321
  48.6 4.7 %collective-permute-start.12 = (bf16[80,512]{1,0:T(8,128)(2,1)S(1)}, bf16[80,512]{1,0:T(8,128)(2,1)S(1)}, u32[]{:S(2)}, u32[]{:S(2)}) collective-permute-start(bf16[80,512]{1,0:T(8,128)(2,1)S(1)} %add_convert_fusion.2.ms_ref), channel_id=1, source_target_pairs={{0,1},{1,0},{2,3},{3,2},{4,5},{5,4},{6,7},{7,6},{8,9},{9,8},{10,11... | collective-permute-start | bytes 245768 | tf_op jit(solution)/shard_map/ppermute | solution.py:443
  53.3 0.9 %collective-permute-done.12.other_ref = bf16[80,512]{1,0:T(8,128)(2,1)S(1)} collective-permute-done((bf16[80,512]{1,0:T(8,128)(2,1)S(1)}, bf16[80,512]{1,0:T(8,128)(2,1)S(1)}, u32[]{:S(2)}, u32[]{:S(2)}) %collective-permute-start.12) | collective-permute-done | bytes 81952 | tf_op jit(solution)/shard_map/ppermute | solution.py:443
  54.2 2.5 %finish.1 = bf16[8,128,512]{2,1,0:T(8,128)(2,1)} custom-call(f32[8]{0:T(128)S(1)} %copy-done.2, bf16[8,128,384]{2,1,0:T(8,128)(2,1)S(1)} %get-tuple-element.35.up_ref, bf16[256,512]{1,0:T(8,128)(2,1)S(1)} %get-tuple-element.36.cols_ref, bf16[80,512]{1,0:T(8,128)(2,1)S(1)} %add_convert_fusion.2.ms_ref, bf16[80,512]{1,0:T(8,128)(2,1)S(1)} %collective-permute-done.12.other_ref, ...), custom_call_target="tpu_custom_call" | custom-call | tf_op jit(solution)/shard_map/finish/pallas_call | solution.py:446
  (2 shorter events, 0.1 us)
Async XLA Ops:
  0.0 1.6 %collective-permute-start = (f32[1,8]{1,0:T(1,128)}, f32[1,8]{1,0:T(1,128)S(1)}, u32[]{:S(2)}, u32[]{:S(2)}) collective-permute-start(f32[1,8]{1,0:T(1,128)} %param.13), channel_id=1, source_target_pairs={{0,1},{1,0},{2,3},{3,2},{4,5},{5,4},{6,7},{7,6},{8,9},{9,8},{10,11... | collective-permute-start | bytes 104 | tf_op jit(solution)/shard_map/ppermute | solution.py:343
  2.4 2.4 %collective-permute-start.1 = (f32[1,19]{1,0:T(1,128)S(1)}, f32[1,19]{1,0:T(1,128)S(1)}, u32[]{:S(2)}, u32[]{:S(2)}) collective-permute-start(f32[1,19]{1,0:T(1,128)S(1)} %pad_maximum_fusion.1), channel_id=1, source_target_pairs={{0,2},{2,0},{4,6},{6,4},{8,10},{10,8},{12,14},{14,12},{1,3},{3,1},... | collective-permute-start | bytes 236 | tf_op jit(solution)/shard_map/ppermute | solution.py:321
  5.5 8.2 %collective-permute-start.2 = (f32[2,19]{1,0:T(2,128)S(1)}, f32[2,19]{1,0:T(2,128)S(1)}, u32[]{:S(2)}, u32[]{:S(2)}) collective-permute-start(f32[2,19]{1,0:T(2,128)S(1)} %pad_maximum_fusion), channel_id=1, source_target_pairs={{0,4},{2,6},{4,0},{6,2},{8,12},{10,14},{12,8},{14,10},{1,5},{3,7},... | collective-permute-start | bytes 464 | tf_op jit(solution)/shard_map/ppermute | solution.py:321
  5.7 8.0 %collective-permute-start.3 = (f32[2,19]{1,0:T(2,128)S(1)}, f32[2,19]{1,0:T(2,128)S(1)}, u32[]{:S(2)}, u32[]{:S(2)}) collective-permute-start(f32[2,19]{1,0:T(2,128)S(1)} %pad_maximum_fusion), channel_id=1, source_target_pairs={{0,8},{2,10},{4,12},{6,14},{8,0},{10,2},{12,4},{14,6},{1,9},{3,11}... | collective-permute-start | bytes 464 | tf_op jit(solution)/shard_map/ppermute | solution.py:321
  8.0 5.7 %collective-permute-start.4 = (f32[2,19]{1,0:T(2,128)S(1)}, f32[2,19]{1,0:T(2,128)S(1)}, u32[]{:S(2)}, u32[]{:S(2)}) collective-permute-start(f32[2,19]{1,0:T(2,128)S(1)} %pad_maximum_fusion), channel_id=1, source_target_pairs={{0,12},{2,14},{4,8},{6,10},{8,4},{10,6},{12,0},{14,2},{1,13},{3,15... | collective-permute-start | bytes 464 | tf_op jit(solution)/shard_map/ppermute | solution.py:321
  19.0 6.3 %copy-start.6 = (f32[208,512]{1,0:T(8,128)S(1)}, f32[208,512]{1,0:T(8,128)}, u32[]{:S(2)}) copy-start(f32[208,512]{1,0:T(8,128)} %get-tuple-element.25) | copy-start | bytes 1277956
  19.0 6.3 %collective-permute-start.5 = (bf16[208,512]{1,0:T(8,128)(2,1)}, bf16[208,512]{1,0:T(8,128)(2,1)S(1)}, u32[]{:S(2)}, u32[]{:S(2)}) collective-permute-start(bf16[208,512]{1,0:T(8,128)(2,1)} %get-tuple-element.26.refs_0_), channel_id=1, source_target_pairs={{0,2},{2,0},{4,6},{6,4},{8,10},{10,8},{12,14},{14,12},{1,3},{3,1},... | collective-permute-start | bytes 638984 | tf_op jit(solution)/shard_map/ppermute | solution.py:321
  25.0 10.5 %collective-permute-start.9 = (bf16[208,512]{1,0:T(8,128)(2,1)}, bf16[208,512]{1,0:T(8,128)(2,1)S(1)}, u32[]{:S(2)}, u32[]{:S(2)}) collective-permute-start(bf16[208,512]{1,0:T(8,128)(2,1)} %get-tuple-element.32), channel_id=1, source_target_pairs={{0,2},{2,0},{4,6},{6,4},{8,10},{10,8},{12,14},{14,12},{1,3},{3,1},... | collective-permute-start | bytes 638984 | tf_op jit(solution)/shard_map/ppermute | solution.py:321
  25.4 1.3 %copy-start.4 = (bf16[208,512]{1,0:T(8,128)(2,1)}, bf16[208,512]{1,0:T(8,128)(2,1)S(1)}, u32[]{:S(2)}) copy-start(bf16[208,512]{1,0:T(8,128)(2,1)S(1)} %add_convert_fusion.1.refs_0_) | copy-start | bytes 638980
  25.4 10.1 %copy-start.5 = (f32[208,512]{1,0:T(8,128)S(1)}, f32[208,512]{1,0:T(8,128)}, u32[]{:S(2)}) copy-start(f32[208,512]{1,0:T(8,128)} %get-tuple-element.31) | copy-start | bytes 1277956
  25.4 12.9 %copy-start = (s32[2]{0:T(128)S(1)}, s32[2]{0:T(128)}, u32[]{:S(2)}) copy-start(s32[2]{0:T(128)} %pad_add_fusion.who) | copy-start | bytes 28
  25.4 12.9 %copy-start.1 = (f32[8,8]{1,0:T(8,128)S(1)}, f32[8,8]{1,0:T(8,128)}, u32[]{:S(2)}) copy-start(f32[8,8]{1,0:T(8,128)} %mix.1) | copy-start | bytes 772
  25.4 12.9 %copy-start.2 = (f32[8]{0:T(128)S(1)}, f32[8]{0:T(128)}, u32[]{:S(2)}) copy-start(f32[8]{0:T(128)} %gain.3) | copy-start | bytes 100
  25.4 12.9 %copy-start.3 = (f32[8]{0:T(128)S(1)}, f32[8]{0:T(128)}, u32[]{:S(2)}) copy-start(f32[8]{0:T(128)} %synth.1) | copy-start | bytes 100
  25.4 10.1 %collective-permute-start.10 = (bf16[208,512]{1,0:T(8,128)(2,1)S(1)}, bf16[208,512]{1,0:T(8,128)(2,1)S(1)}, u32[]{:S(2)}, u32[]{:S(2)}) collective-permute-start(bf16[208,512]{1,0:T(8,128)(2,1)S(1)} %add_convert_fusion.1.refs_0_), channel_id=1, source_target_pairs={{0,4},{2,6},{4,0},{6,2},{8,12},{10,14},{12,8},{14,10},{1,5},{3,7},... | collective-permute-start | bytes 638984 | tf_op jit(solution)/shard_map/ppermute | solution.py:321
  32.8 7.7 %collective-permute-start.6 = (bf16[208,512]{1,0:T(8,128)(2,1)}, bf16[208,512]{1,0:T(8,128)(2,1)S(1)}, u32[]{:S(2)}, u32[]{:S(2)}) collective-permute-start(bf16[208,512]{1,0:T(8,128)(2,1)} %get-tuple-element.28), channel_id=1, source_target_pairs={{0,2},{2,0},{4,6},{6,4},{8,10},{10,8},{12,14},{14,12},{1,3},{3,1},... | collective-permute-start | bytes 638984 | tf_op jit(solution)/shard_map/ppermute | solution.py:321
  34.1 7.4 %collective-permute-start.7 = (bf16[208,512]{1,0:T(8,128)(2,1)}, bf16[208,512]{1,0:T(8,128)(2,1)S(1)}, u32[]{:S(2)}, u32[]{:S(2)}) collective-permute-start(bf16[208,512]{1,0:T(8,128)(2,1)} %get-tuple-element.29), channel_id=1, source_target_pairs={{0,6},{2,4},{4,2},{6,0},{8,14},{10,12},{12,10},{14,8},{1,7},{3,5},... | collective-permute-start | bytes 638984 | tf_op jit(solution)/shard_map/ppermute | solution.py:321
  34.6 10.8 %collective-permute-start.8 = (bf16[208,512]{1,0:T(8,128)(2,1)}, bf16[208,512]{1,0:T(8,128)(2,1)S(1)}, u32[]{:S(2)}, u32[]{:S(2)}) collective-permute-start(bf16[208,512]{1,0:T(8,128)(2,1)} %get-tuple-element.30), channel_id=1, source_target_pairs={{0,4},{2,6},{4,0},{6,2},{8,12},{10,14},{12,8},{14,10},{1,5},{3,7},... | collective-permute-start | bytes 638984 | tf_op jit(solution)/shard_map/ppermute | solution.py:321
  35.6 13.0 %collective-permute-start.11 = (bf16[208,512]{1,0:T(8,128)(2,1)S(1)}, bf16[208,512]{1,0:T(8,128)(2,1)S(1)}, u32[]{:S(2)}, u32[]{:S(2)}) collective-permute-start(bf16[208,512]{1,0:T(8,128)(2,1)S(1)} %add_convert_fusion.after), channel_id=1, source_target_pairs={{0,8},{2,10},{4,12},{6,14},{8,0},{10,2},{12,4},{14,6},{1,9},{3,11}... | collective-permute-start | bytes 638984 | tf_op jit(solution)/shard_map/ppermute | solution.py:321
  48.6 5.6 %collective-permute-start.12 = (bf16[80,512]{1,0:T(8,128)(2,1)S(1)}, bf16[80,512]{1,0:T(8,128)(2,1)S(1)}, u32[]{:S(2)}, u32[]{:S(2)}) collective-permute-start(bf16[80,512]{1,0:T(8,128)(2,1)S(1)} %add_convert_fusion.2.ms_ref), channel_id=1, source_target_pairs={{0,1},{1,0},{2,3},{3,2},{4,5},{5,4},{6,7},{7,6},{8,9},{9,8},{10,11... | collective-permute-start | bytes 245768 | tf_op jit(solution)/shard_map/ppermute | solution.py:443

commit v5 on v4

--- a/solution.py
+++ b/solution.py
@@ -391,7 +391,7 @@
                 pltpu.VMEM((count + 2, KC, KR * coarse, bands * coarse), BF16),
                 pltpu.SemaphoreType.DMA((count + 3,)),
             ],
-            compiler_params=params(60),
+            compiler_params=params(44),
             name="group_maps",
         )(who, grids, cells, ms_cells, *after)
         held.update((k, [piece]) for k, piece in zip(order, made))

time: 57.1 us -> 55.6 us (0.974)
  Pallas kernels: 24.8 us -> 21.2 us
  local copies, waits for them, and re-layouts: 0.65 us -> 3.1 us
  other arithmetic: 3.33 us -> 2.34 us
    pallas_call x3, Pallas kernels: 15.5 us -> 12 us  [make(): pl.pallas_call(functools.partial(group_maps, n, bands, first, count), in_...]
    unnamed x14 -> x12, local copies, waits for them, and re-layouts: 0.04 us -> 3.07 us
    add x1, other arithmetic: 1.06 us -> 0.06 us  [local(): got = [mine + early.astype(F32), *others, last]]
    ppermute x1, starting transfers between devices: 4.66 us -> 5.58 us  [local(): other = lax.ppermute(ms_map, 'mcol', [(0, 1), (1, 0)])]
    concatenate x1, local copies, waits for them, and re-layouts: 0.61 us -> 0.02 us  [local(): jnp.concatenate([pair] + [exchange(pair, k, n) for k in range(2, n, 2)],...]
  transfers between devices with their start and end apart: 13 -> 13, of which waited for: 6 -> 6; matrix products, arithmetic and copies ran while one was open for 3% -> 1% of each run, Pallas kernels for 31% -> 27%
where the time goes in v5:
time: 55.6 us; the launch traced here: 55.4 us
  Pallas kernels  21.2 us (38%)
  starting transfers between devices  17.8 us (32%)
  waiting for transfers between devices  10.7 us (19%)
  local copies, waits for them, and re-layouts  3.1 us (6%)
  other arithmetic  2.34 us (4%)
    pallas_call x3, Pallas kernels, make(): pl.pallas_call(functools.partial(group_maps, n, bands, first, count), in_...  12 us
    ppermute x11, starting transfers between devices, exchange(): return lax.ppermute(x, 'mrow', [(i, i ^ step) for i in range(count)])  11.6 us
    ppermute x11, waiting for transfers between devices, exchange(): return lax.ppermute(x, 'mrow', [(i, i ^ step) for i in range(count)])  8.87 us
    ppermute x1, starting transfers between devices, local(): other = lax.ppermute(ms_map, 'mcol', [(0, 1), (1, 0)])  5.58 us
    pallas_call x1, Pallas kernels, local(): pl.pallas_call(functools.partial(cell_sums, capacity), in_specs=[whole(pl...  5.51 us
    unnamed x12, local copies, waits for them, and re-layouts  3.07 us
    pallas_call x1, Pallas kernels, local(): pl.pallas_call(functools.partial(finish, bands), grid=(bands // each,), i...  2.49 us
    pallas_call x1, Pallas kernels, local(): pl.pallas_call(functools.partial(tables, bands), in_specs=[whole(pltpu.SM...  1.23 us
  transfers between devices with their start and end apart: 13, of which 6 were waited for; matrix products, arithmetic and copies ran while one was open for 1% of the time, Pallas kernels for 27%

profile of v5, /device:TPU:11, one launch (start us, length us, event | category | flops | bytes accessed | tf_op | source)
XLA Modules:
  0.0 55.4 jit_solution(7051009358655916156)
XLA Ops:
  0.0 0.7 %collective-permute-start = (f32[1,8]{1,0:T(1,128)}, f32[1,8]{1,0:T(1,128)S(1)}, u32[]{:S(2)}, u32[]{:S(2)}) collective-permute-start(f32[1,8]{1,0:T(1,128)} %param.13), channel_id=1, source_target_pairs={{0,1},{1,0},{2,3},{3,2},{4,5},{5,4},{6,7},{7,6},{8,9},{9,8},{10,11... | collective-permute-start | bytes 104 | tf_op jit(solution)/shard_map/ppermute | solution.py:343
  0.7 1.0 %collective-permute-done = f32[1,8]{1,0:T(1,128)S(1)} collective-permute-done((f32[1,8]{1,0:T(1,128)}, f32[1,8]{1,0:T(1,128)S(1)}, u32[]{:S(2)}, u32[]{:S(2)}) %collective-permute-start) | collective-permute-done | bytes 64 | tf_op jit(solution)/shard_map/ppermute | solution.py:343
  1.6 0.7 %pad_maximum_fusion.1 = f32[1,19]{1,0:T(1,128)S(1)} fusion(f32[1,8]{1,0:T(1,128)S(1)} %collective-permute-done, f32[1,8]{1,0:T(1,128)} %param.13, f32[1,3]{1,0:T(1,128)} %bitcast.3), kind=kLoop, calls=%fused_computation.6 | loop fusion | flops 38 | bytes 152 | tf_op jit(solution)/shard_map/concatenate | solution.py:344
  2.4 1.2 %collective-permute-start.1 = (f32[1,19]{1,0:T(1,128)S(1)}, f32[1,19]{1,0:T(1,128)S(1)}, u32[]{:S(2)}, u32[]{:S(2)}) collective-permute-start(f32[1,19]{1,0:T(1,128)S(1)} %pad_maximum_fusion.1), channel_id=1, source_target_pairs={{0,2},{2,0},{4,6},{6,4},{8,10},{10,8},{12,14},{14,12},{1,3},{3,1},... | collective-permute-start | bytes 236 | tf_op jit(solution)/shard_map/ppermute | solution.py:321
  3.6 0.6 %pad_add_fusion.who = s32[2]{0:T(128)} fusion(s32[1]{0:T(128)} %bitcast.1, s32[1]{0:T(128)} %bitcast), kind=kLoop, calls=%fused_computation.5 | loop fusion | flops 2 | bytes 16 | tf_op jit(solution)/shard_map/stack | solution.py:341
  4.2 0.0 copy-start.2
  4.2 0.5 collective-permute-done.1
  4.8 0.7 %pad_maximum_fusion = f32[2,19]{1,0:T(2,128)S(1)} fusion(f32[1,19]{1,0:T(1,128)S(1)} %collective-permute-done.1, f32[1,8]{1,0:T(1,128)S(1)} %collective-permute-done, f32[1,8]{1,0:T(1,128)} %param.13, f32[1,3]{1,0:T(1,128)} %bitcast.4), kind=kLoop, calls=%fused_computation.4 | loop fusion | flops 114 | bytes 304 | tf_op jit(solution)/shard_map/concatenate | solution.py:345
  5.5 0.2 collective-permute-start.2
  5.7 2.3 %collective-permute-start.3 = (f32[2,19]{1,0:T(2,128)S(1)}, f32[2,19]{1,0:T(2,128)S(1)}, u32[]{:S(2)}, u32[]{:S(2)}) collective-permute-start(f32[2,19]{1,0:T(2,128)S(1)} %pad_maximum_fusion), channel_id=1, source_target_pairs={{0,8},{2,10},{4,12},{6,14},{8,0},{10,2},{12,4},{14,6},{1,9},{3,11}... | collective-permute-start | bytes 464 | tf_op jit(solution)/shard_map/ppermute | solution.py:321
  8.0 0.2 collective-permute-start.4
  8.2 5.5 %cell_sums.1 = (bf16[40,256,128]{2,1,0:T(8,128)(2,1)}, bf16[40,64,256]{2,1,0:T(8,128)(2,1)}) custom-call(s32[2]{0:T(128)} %pad_add_fusion.who, s32[3,64]{1,0:T(4,128)} %list_ref.1, bf16[64,128,128]{2,1,0:T(8,128)(2,1)} %pan_hbm.1, bf16[64,32,256]{2,1,0:T(8,128)(2,1)} %ms_hbm.1), custom_call_target="tpu_custom_call" | custom-call | flops 1000000000 | bytes 16777216 | tf_op jit(solution)/shard_map/cell_sums/pallas_call | solution.py:352
  13.7 0.0 collective-permute-done.2
  13.7 0.0 collective-permute-done.3
  13.7 0.0 collective-permute-done.4
  13.7 0.0 copy-done.2
  13.7 0.0 copy-start
  13.8 1.7 %copy-done = bf16[40,256,128]{2,1,0:T(8,128)(2,1)S(1)} copy-done((bf16[40,256,128]{2,1,0:T(8,128)(2,1)S(1)}, bf16[40,256,128]{2,1,0:T(8,128)(2,1)}, u32[]{:S(2)}) %copy-start) | copy-done | bytes 2621464
  15.5 0.0 copy-start.1
  15.5 1.3 %copy-done.1 = bf16[40,64,256]{2,1,0:T(8,128)(2,1)S(1)} copy-done((bf16[40,64,256]{2,1,0:T(8,128)(2,1)S(1)}, bf16[40,64,256]{2,1,0:T(8,128)(2,1)}, u32[]{:S(2)}) %copy-start.1) | copy-done | bytes 1310744
  16.8 3.6 %group_maps.3 = (bf16[208,512]{1,0:T(8,128)(2,1)S(1)}, f32[208,512]{1,0:T(8,128)S(1)}) custom-call(s32[2]{0:T(128)S(1)} %copy-done.2, f32[8,19]{1,0:T(8,128)S(1)} %concatenate.12.grids, bf16[40,256,128]{2,1,0:T(8,128)(2,1)S(1)} %copy-done, bf16[40,64,256]{2,1,0:T(8,128)(2,1)S(1)} %copy-done.1), custom_call_target="tpu_custom_call" | custom-call | tf_op jit(solution)/shard_map/group_maps/pallas_call | solution.py:378
  20.4 1.3 %collective-permute-start.5 = (bf16[208,512]{1,0:T(8,128)(2,1)S(1)}, bf16[208,512]{1,0:T(8,128)(2,1)S(1)}, u32[]{:S(2)}, u32[]{:S(2)}) collective-permute-start(bf16[208,512]{1,0:T(8,128)(2,1)S(1)} %get-tuple-element.26.refs_0_), channel_id=1, source_target_pairs={{0,2},{2,0},{4,6},{6,4},{8,10},{10,8},{12,14},{14,12},{1,3},{3,1},... | collective-permute-start | bytes 638984 | tf_op jit(solution)/shard_map/ppermute | solution.py:321
  21.7 3.6 %group_maps.5 = (bf16[208,512]{1,0:T(8,128)(2,1)S(1)}, f32[208,512]{1,0:T(8,128)S(1)}) custom-call(s32[2]{0:T(128)S(1)} %copy-done.2, f32[8,19]{1,0:T(8,128)S(1)} %concatenate.12.grids, bf16[40,256,128]{2,1,0:T(8,128)(2,1)S(1)} %copy-done, bf16[40,64,256]{2,1,0:T(8,128)(2,1)S(1)} %copy-done.1, bf16[208,512]{1,0:T(8,128)(2,1)S(1)} %get-tuple-element.26.refs_0_), custom_call_target="tpu_custom_call" | custom-call | tf_op jit(solution)/shard_map/group_maps/pallas_call | solution.py:378
  25.2 0.3 collective-permute-start.9
  25.5 0.0 collective-permute-done.5
  25.6 0.0 copy-start.3
  25.6 0.0 copy-start.4
  25.6 0.0 copy-start.5
  25.6 1.2 %collective-permute-start.10 = (bf16[208,512]{1,0:T(8,128)(2,1)S(1)}, bf16[208,512]{1,0:T(8,128)(2,1)S(1)}, u32[]{:S(2)}, u32[]{:S(2)}) collective-permute-start(bf16[208,512]{1,0:T(8,128)(2,1)S(1)} %add_convert_fusion.1.refs_0_), channel_id=1, source_target_pairs={{0,4},{2,6},{4,0},{6,2},{8,12},{10,14},{12,8},{14,10},{1,5},{3,7},... | collective-permute-start | bytes 638984 | tf_op jit(solution)/shard_map/ppermute | solution.py:321
  26.8 4.9 %group_maps.4 = (bf16[208,512]{1,0:T(8,128)(2,1)S(1)}, bf16[208,512]{1,0:T(8,128)(2,1)S(1)}, bf16[208,512]{1,0:T(8,128)(2,1)S(1)}, f32[208,512]{1,0:T(8,128)S(1)}) custom-call(s32[2]{0:T(128)S(1)} %copy-done.2, f32[8,19]{1,0:T(8,128)S(1)} %concatenate.12.grids, bf16[40,256,128]{2,1,0:T(8,128)(2,1)S(1)} %copy-done, bf16[40,64,256]{2,1,0:T(8,128)(2,1)S(1)} %copy-done.1, ...), custom_call_target="tpu_custom_call" | custom-call | tf_op jit(solution)/shard_map/group_maps/pallas_call | solution.py:378
  31.7 1.3 %collective-permute-start.6 = (bf16[208,512]{1,0:T(8,128)(2,1)S(1)}, bf16[208,512]{1,0:T(8,128)(2,1)S(1)}, u32[]{:S(2)}, u32[]{:S(2)}) collective-permute-start(bf16[208,512]{1,0:T(8,128)(2,1)S(1)} %get-tuple-element.28), channel_id=1, source_target_pairs={{0,2},{2,0},{4,6},{6,4},{8,10},{10,8},{12,14},{14,12},{1,3},{3,1},... | collective-permute-start | bytes 638984 | tf_op jit(solution)/shard_map/ppermute | solution.py:321
  33.0 0.3 collective-permute-start.7
  33.3 1.1 %collective-permute-start.8 = (bf16[208,512]{1,0:T(8,128)(2,1)S(1)}, bf16[208,512]{1,0:T(8,128)(2,1)S(1)}, u32[]{:S(2)}, u32[]{:S(2)}) collective-permute-start(bf16[208,512]{1,0:T(8,128)(2,1)S(1)} %get-tuple-element.30), channel_id=1, source_target_pairs={{0,4},{2,6},{4,0},{6,2},{8,12},{10,14},{12,8},{14,10},{1,5},{3,7},... | collective-permute-start | bytes 638984 | tf_op jit(solution)/shard_map/ppermute | solution.py:321
  34.4 0.0 collective-permute-done.9
  34.4 0.0 collective-permute-done.10
  34.4 0.1 add_convert_fusion.after
  34.5 2.2 %collective-permute-start.11 = (bf16[208,512]{1,0:T(8,128)(2,1)S(1)}, bf16[208,512]{1,0:T(8,128)(2,1)S(1)}, u32[]{:S(2)}, u32[]{:S(2)}) collective-permute-start(bf16[208,512]{1,0:T(8,128)(2,1)S(1)} %add_convert_fusion.after), channel_id=1, source_target_pairs={{0,8},{2,10},{4,12},{6,14},{8,0},{10,2},{12,4},{14,6},{1,9},{3,11}... | collective-permute-start | bytes 638984 | tf_op jit(solution)/shard_map/ppermute | solution.py:321
  36.7 0.0 copy-done.3
  36.7 0.0 copy-done.4
  36.7 0.0 copy-done.5
  36.7 1.2 %tables.1 = (bf16[8,128,384]{2,1,0:T(8,128)(2,1)S(1)}, bf16[256,512]{1,0:T(8,128)(2,1)S(1)}) custom-call(s32[2]{0:T(128)S(1)} %copy-done.2, f32[8,8]{1,0:T(8,128)S(1)} %copy-done.3, f32[8]{0:T(128)S(1)} %copy-done.4, f32[8]{0:T(128)S(1)} %copy-done.5, bf16[208,512]{1,0:T(8,128)(2,1)S(1)} %add_convert_fusion.after), custom_call_target="tpu_custom_call" | custom-call | tf_op jit(solution)/shard_map/tables/pallas_call | solution.py:429
  38.0 0.8 %collective-permute-done.6 = bf16[208,512]{1,0:T(8,128)(2,1)S(1)} collective-permute-done((bf16[208,512]{1,0:T(8,128)(2,1)S(1)}, bf16[208,512]{1,0:T(8,128)(2,1)S(1)}, u32[]{:S(2)}, u32[]{:S(2)}) %collective-permute-start.6) | collective-permute-done | bytes 213024 | tf_op jit(solution)/shard_map/ppermute | solution.py:321
  38.8 0.1 convert_add_fusion.refs_0_
  38.8 0.0 collective-permute-done.7.refs_1_
  38.8 3.0 %collective-permute-done.8.refs_2_ = bf16[208,512]{1,0:T(8,128)(2,1)S(1)} collective-permute-done((bf16[208,512]{1,0:T(8,128)(2,1)S(1)}, bf16[208,512]{1,0:T(8,128)(2,1)S(1)}, u32[]{:S(2)}, u32[]{:S(2)}) %collective-permute-start.8) | collective-permute-done | bytes 213024 | tf_op jit(solution)/shard_map/ppermute | solution.py:321
  41.8 4.6 %collective-permute-done.11.refs_3_ = bf16[208,512]{1,0:T(8,128)(2,1)S(1)} collective-permute-done((bf16[208,512]{1,0:T(8,128)(2,1)S(1)}, bf16[208,512]{1,0:T(8,128)(2,1)S(1)}, u32[]{:S(2)}, u32[]{:S(2)}) %collective-permute-start.11) | collective-permute-done | bytes 213024 | tf_op jit(solution)/shard_map/ppermute | solution.py:321
  46.4 5.6 %collective-permute-start.12 = (bf16[80,512]{1,0:T(8,128)(2,1)S(1)}, bf16[80,512]{1,0:T(8,128)(2,1)S(1)}, u32[]{:S(2)}, u32[]{:S(2)}) collective-permute-start(bf16[80,512]{1,0:T(8,128)(2,1)S(1)} %add_convert_fusion.2.ms_ref), channel_id=1, source_target_pairs={{0,1},{1,0},{2,3},{3,2},{4,5},{5,4},{6,7},{7,6},{8,9},{9,8},{10,11... | collective-permute-start | bytes 245768 | tf_op jit(solution)/shard_map/ppermute | solution.py:443
  52.0 0.9 %collective-permute-done.12.other_ref = bf16[80,512]{1,0:T(8,128)(2,1)S(1)} collective-permute-done((bf16[80,512]{1,0:T(8,128)(2,1)S(1)}, bf16[80,512]{1,0:T(8,128)(2,1)S(1)}, u32[]{:S(2)}, u32[]{:S(2)}) %collective-permute-start.12) | collective-permute-done | bytes 81952 | tf_op jit(solution)/shard_map/ppermute | solution.py:443
  52.9 2.5 %finish.1 = bf16[8,128,512]{2,1,0:T(8,128)(2,1)} custom-call(f32[8]{0:T(128)S(1)} %copy-done.4, bf16[8,128,384]{2,1,0:T(8,128)(2,1)S(1)} %get-tuple-element.35.up_ref, bf16[256,512]{1,0:T(8,128)(2,1)S(1)} %get-tuple-element.36.cols_ref, bf16[80,512]{1,0:T(8,128)(2,1)S(1)} %add_convert_fusion.2.ms_ref, bf16[80,512]{1,0:T(8,128)(2,1)S(1)} %collective-permute-done.12.other_ref, ...), custom_call_target="tpu_custom_call" | custom-call | tf_op jit(solution)/shard_map/finish/pallas_call | solution.py:446
  (3 shorter events, 0.1 us)
Async XLA Ops:
  0.0 1.6 %collective-permute-start = (f32[1,8]{1,0:T(1,128)}, f32[1,8]{1,0:T(1,128)S(1)}, u32[]{:S(2)}, u32[]{:S(2)}) collective-permute-start(f32[1,8]{1,0:T(1,128)} %param.13), channel_id=1, source_target_pairs={{0,1},{1,0},{2,3},{3,2},{4,5},{5,4},{6,7},{7,6},{8,9},{9,8},{10,11... | collective-permute-start | bytes 104 | tf_op jit(solution)/shard_map/ppermute | solution.py:343
  2.4 2.4 %collective-permute-start.1 = (f32[1,19]{1,0:T(1,128)S(1)}, f32[1,19]{1,0:T(1,128)S(1)}, u32[]{:S(2)}, u32[]{:S(2)}) collective-permute-start(f32[1,19]{1,0:T(1,128)S(1)} %pad_maximum_fusion.1), channel_id=1, source_target_pairs={{0,2},{2,0},{4,6},{6,4},{8,10},{10,8},{12,14},{14,12},{1,3},{3,1},... | collective-permute-start | bytes 236 | tf_op jit(solution)/shard_map/ppermute | solution.py:321
  4.2 9.5 %copy-start.2 = (s32[2]{0:T(128)S(1)}, s32[2]{0:T(128)}, u32[]{:S(2)}) copy-start(s32[2]{0:T(128)} %pad_add_fusion.who) | copy-start | bytes 28
  5.5 8.2 %collective-permute-start.2 = (f32[2,19]{1,0:T(2,128)S(1)}, f32[2,19]{1,0:T(2,128)S(1)}, u32[]{:S(2)}, u32[]{:S(2)}) collective-permute-start(f32[2,19]{1,0:T(2,128)S(1)} %pad_maximum_fusion), channel_id=1, source_target_pairs={{0,4},{2,6},{4,0},{6,2},{8,12},{10,14},{12,8},{14,10},{1,5},{3,7},... | collective-permute-start | bytes 464 | tf_op jit(solution)/shard_map/ppermute | solution.py:321
  5.7 8.0 %collective-permute-start.3 = (f32[2,19]{1,0:T(2,128)S(1)}, f32[2,19]{1,0:T(2,128)S(1)}, u32[]{:S(2)}, u32[]{:S(2)}) collective-permute-start(f32[2,19]{1,0:T(2,128)S(1)} %pad_maximum_fusion), channel_id=1, source_target_pairs={{0,8},{2,10},{4,12},{6,14},{8,0},{10,2},{12,4},{14,6},{1,9},{3,11}... | collective-permute-start | bytes 464 | tf_op jit(solution)/shard_map/ppermute | solution.py:321
  8.0 5.7 %collective-permute-start.4 = (f32[2,19]{1,0:T(2,128)S(1)}, f32[2,19]{1,0:T(2,128)S(1)}, u32[]{:S(2)}, u32[]{:S(2)}) collective-permute-start(f32[2,19]{1,0:T(2,128)S(1)} %pad_maximum_fusion), channel_id=1, source_target_pairs={{0,12},{2,14},{4,8},{6,10},{8,4},{10,6},{12,0},{14,2},{1,13},{3,15... | collective-permute-start | bytes 464 | tf_op jit(solution)/shard_map/ppermute | solution.py:321
  13.7 1.7 %copy-start = (bf16[40,256,128]{2,1,0:T(8,128)(2,1)S(1)}, bf16[40,256,128]{2,1,0:T(8,128)(2,1)}, u32[]{:S(2)}) copy-start(bf16[40,256,128]{2,1,0:T(8,128)(2,1)} %get-tuple-element.23.cells_hbm) | copy-start | bytes 7864324
  15.5 1.3 %copy-start.1 = (bf16[40,64,256]{2,1,0:T(8,128)(2,1)S(1)}, bf16[40,64,256]{2,1,0:T(8,128)(2,1)}, u32[]{:S(2)}) copy-start(bf16[40,64,256]{2,1,0:T(8,128)(2,1)} %get-tuple-element.24.ms_hbm) | copy-start | bytes 3932164
  20.4 5.2 %collective-permute-start.5 = (bf16[208,512]{1,0:T(8,128)(2,1)S(1)}, bf16[208,512]{1,0:T(8,128)(2,1)S(1)}, u32[]{:S(2)}, u32[]{:S(2)}) collective-permute-start(bf16[208,512]{1,0:T(8,128)(2,1)S(1)} %get-tuple-element.26.refs_0_), channel_id=1, source_target_pairs={{0,2},{2,0},{4,6},{6,4},{8,10},{10,8},{12,14},{14,12},{1,3},{3,1},... | collective-permute-start | bytes 638984 | tf_op jit(solution)/shard_map/ppermute | solution.py:321
  25.2 9.2 %collective-permute-start.9 = (bf16[208,512]{1,0:T(8,128)(2,1)S(1)}, bf16[208,512]{1,0:T(8,128)(2,1)S(1)}, u32[]{:S(2)}, u32[]{:S(2)}) collective-permute-start(bf16[208,512]{1,0:T(8,128)(2,1)S(1)} %get-tuple-element.32), channel_id=1, source_target_pairs={{0,2},{2,0},{4,6},{6,4},{8,10},{10,8},{12,14},{14,12},{1,3},{3,1},... | collective-permute-start | bytes 638984 | tf_op jit(solution)/shard_map/ppermute | solution.py:321
  25.6 11.1 %copy-start.3 = (f32[8,8]{1,0:T(8,128)S(1)}, f32[8,8]{1,0:T(8,128)}, u32[]{:S(2)}) copy-start(f32[8,8]{1,0:T(8,128)} %mix.1) | copy-start | bytes 772
  25.6 11.1 %copy-start.4 = (f32[8]{0:T(128)S(1)}, f32[8]{0:T(128)}, u32[]{:S(2)}) copy-start(f32[8]{0:T(128)} %gain.3) | copy-start | bytes 100
  25.6 11.1 %copy-start.5 = (f32[8]{0:T(128)S(1)}, f32[8]{0:T(128)}, u32[]{:S(2)}) copy-start(f32[8]{0:T(128)} %synth.1) | copy-start | bytes 100
  25.6 8.8 %collective-permute-start.10 = (bf16[208,512]{1,0:T(8,128)(2,1)S(1)}, bf16[208,512]{1,0:T(8,128)(2,1)S(1)}, u32[]{:S(2)}, u32[]{:S(2)}) collective-permute-start(bf16[208,512]{1,0:T(8,128)(2,1)S(1)} %add_convert_fusion.1.refs_0_), channel_id=1, source_target_pairs={{0,4},{2,6},{4,0},{6,2},{8,12},{10,14},{12,8},{14,10},{1,5},{3,7},... | collective-permute-start | bytes 638984 | tf_op jit(solution)/shard_map/ppermute | solution.py:321
  31.7 7.0 %collective-permute-start.6 = (bf16[208,512]{1,0:T(8,128)(2,1)S(1)}, bf16[208,512]{1,0:T(8,128)(2,1)S(1)}, u32[]{:S(2)}, u32[]{:S(2)}) collective-permute-start(bf16[208,512]{1,0:T(8,128)(2,1)S(1)} %get-tuple-element.28), channel_id=1, source_target_pairs={{0,2},{2,0},{4,6},{6,4},{8,10},{10,8},{12,14},{14,12},{1,3},{3,1},... | collective-permute-start | bytes 638984 | tf_op jit(solution)/shard_map/ppermute | solution.py:321
  33.0 5.8 %collective-permute-start.7 = (bf16[208,512]{1,0:T(8,128)(2,1)S(1)}, bf16[208,512]{1,0:T(8,128)(2,1)S(1)}, u32[]{:S(2)}, u32[]{:S(2)}) collective-permute-start(bf16[208,512]{1,0:T(8,128)(2,1)S(1)} %get-tuple-element.29), channel_id=1, source_target_pairs={{0,6},{2,4},{4,2},{6,0},{8,14},{10,12},{12,10},{14,8},{1,7},{3,5},... | collective-permute-start | bytes 638984 | tf_op jit(solution)/shard_map/ppermute | solution.py:321
  33.3 8.5 %collective-permute-start.8 = (bf16[208,512]{1,0:T(8,128)(2,1)S(1)}, bf16[208,512]{1,0:T(8,128)(2,1)S(1)}, u32[]{:S(2)}, u32[]{:S(2)}) collective-permute-start(bf16[208,512]{1,0:T(8,128)(2,1)S(1)} %get-tuple-element.30), channel_id=1, source_target_pairs={{0,4},{2,6},{4,0},{6,2},{8,12},{10,14},{12,8},{14,10},{1,5},{3,7},... | collective-permute-start | bytes 638984 | tf_op jit(solution)/shard_map/ppermute | solution.py:321
  34.5 11.8 %collective-permute-start.11 = (bf16[208,512]{1,0:T(8,128)(2,1)S(1)}, bf16[208,512]{1,0:T(8,128)(2,1)S(1)}, u32[]{:S(2)}, u32[]{:S(2)}) collective-permute-start(bf16[208,512]{1,0:T(8,128)(2,1)S(1)} %add_convert_fusion.after), channel_id=1, source_target_pairs={{0,8},{2,10},{4,12},{6,14},{8,0},{10,2},{12,4},{14,6},{1,9},{3,11}... | collective-permute-start | bytes 638984 | tf_op jit(solution)/shard_map/ppermute | solution.py:321
  46.4 6.5 %collective-permute-start.12 = (bf16[80,512]{1,0:T(8,128)(2,1)S(1)}, bf16[80,512]{1,0:T(8,128)(2,1)S(1)}, u32[]{:S(2)}, u32[]{:S(2)}) collective-permute-start(bf16[80,512]{1,0:T(8,128)(2,1)S(1)} %add_convert_fusion.2.ms_ref), channel_id=1, source_target_pairs={{0,1},{1,0},{2,3},{3,2},{4,5},{5,4},{6,7},{7,6},{8,9},{9,8},{10,11... | collective-permute-start | bytes 245768 | tf_op jit(solution)/shard_map/ppermute | solution.py:443
